TPU v7x, 256 devices: a whole 4x4x8 slice. The times are simulated.
256 devices in a mesh: img: 128 (over y, z, x_lo, core), band: 2 (over x_hi).
Axes of the slice: x: 4 (x_hi: 2, x_lo: 2; x = x_hi * 2 + x_lo), y: 4, z: 8, core: 2. Of those that a mesh axis runs over, the one named last changes fastest.
Arguments:
- latents: bfloat16 [512, 256, 384], P('img', 'band'), may hold values from -6 to 6
- pos_row: int32 [512, 256], P('img', 'band'), may hold values from 0 to 15, as said below
- pos_col: int32 [512, 256], P('img', 'band'), may hold values from 0 to 15, as said below
- timesteps: int32 [512], P('img'), may hold values from 0 to 999
- labels: int32 [512], P('img'), may hold values from 0 to 1000
- t_w1: bfloat16 [256, 384], replicated, may hold values from -0.375 to 0.375
- t_w2: bfloat16 [384, 384], replicated, may hold values from -0.3125 to 0.3125
- label_table: bfloat16 [1001, 384], replicated, may hold values from -6 to 6
- mod_w: bfloat16 [384, 2304], replicated, may hold values from -0.3125 to 0.3125
- qkv_w: bfloat16 [384, 1152], replicated, may hold values from -0.3125 to 0.3125
- q_gain: float32 [64], replicated, may hold values from 0.5 to 1.5
- k_gain: float32 [64], replicated, may hold values from 0.5 to 1.5
- proj_w: bfloat16 [384, 384], replicated, may hold values from -1.25 to 1.25
- gate_up_w: bfloat16 [384, 2048], replicated, may hold values from -0.3125 to 0.3125
- down_w: bfloat16 [1024, 384], replicated, may hold values from -0.1875 to 0.1875
- out_grad: bfloat16 [512, 256, 384], P('img', 'band'), may hold values from -6 to 6
Outputs:
- block_out: bfloat16 [512, 256, 384], P('img', 'band')
- latents_grad: float32 [512, 256, 384], P('img', 'band')
- t_w1_grad: float32 [256, 384], replicated
- t_w2_grad: float32 [384, 384], replicated
- label_table_grad: float32 [1001, 384], replicated
- mod_w_grad: float32 [384, 2304], replicated
- qkv_w_grad: float32 [384, 1152], replicated
- q_gain_grad: float32 [64], replicated
- k_gain_grad: float32 [64], replicated
- proj_w_grad: float32 [384, 384], replicated
- gate_up_w_grad: float32 [384, 2048], replicated
- down_w_grad: float32 [1024, 384], replicated
Inputs may be any that keep to these rules, and one draw needn't show every extreme that they name: The 256 patches of each image hold the cells of its 16 x 16 grid once each, in an order drawn for each image; pos_row is a cell's row. pos_col is the column of the same cell.
All inputs are finite; a program needn't handle non-finite values.
Results may differ from a plain program's by a relative error of at most 0.014.
Values may be sent and summed in bfloat16 or wider, within the bound.
No kernel may reach another device: no remote copies, remote signals or barrier semaphores. Data moves between devices by JAX's collectives and lax.ppermute only.
A program may use at most 128 MiB of HBM per device.

v0:
```python
import itertools
import math

import jax
import jax.numpy as jnp
from jax import lax
from jax.experimental import pallas as pl
from jax.experimental.pallas import tpu as pltpu
from jax.sharding import PartitionSpec as P

AXES = ("img", "band")
SIZES = {"y": 4, "z": 8, "x": 4, "c": 2}
f32 = jnp.float32
bf16 = jnp.bfloat16
EPS = 1e-06
MIB = 1024 * 1024


def dot(a, b):
    return jnp.dot(a, b, preferred_element_type=f32)


def dot_nt(a, b):
    return lax.dot_general(a, b, (((1,), (1,)), ((), ())), preferred_element_type=f32)


def dot_tn(a, b):
    return lax.dot_general(a, b, (((0,), (0,)), ((), ())), preferred_element_type=f32)


def inv_rms(v):
    return lax.rsqrt(jnp.mean(v * v, axis=-1, keepdims=True) + EPS)


def lane_iota(shape):
    return lax.broadcasted_iota(jnp.int32, shape, len(shape) - 1)


def head_mean(v):
    r = lax.broadcasted_iota(jnp.int32, (128, 128), 0) < 64
    c = lax.broadcasted_iota(jnp.int32, (128, 128), 1) < 64
    same = jnp.where(r == c, 1.0 / 64, 0.0).astype(bf16)
    hi = v.astype(bf16)
    lo = (v - hi.astype(f32)).astype(bf16)
    return dot(hi, same) + dot(lo, same)


def partner(v):
    first = (lane_iota((1, 128)) % 32) < 16
    return jnp.where(first, pltpu.roll(v, 112, 1), pltpu.roll(v, 16, 1))


def head_masks():
    low = (lane_iota((1, 128)) < 64).astype(f32)
    return low.astype(bf16), (1.0 - low).astype(bf16)


def both(a_ref, b_ref):
    return jnp.concatenate([a_ref[0], b_ref[0]], axis=0).astype(f32)


def pairs(width=384):
    return [slice(j, j + 128) for j in range(0, width, 128)]


def forward_kernel(
    at_ref, kept_ref, got_ref, mod_ref, w_ref, gain_ref, cos_ref, sin_ref, q_ref, k_ref, v_ref, att_ref
):
    x = both(kept_ref, got_ref)
    h1 = (x * inv_rms(x) * (1.0 + mod_ref[0, 1:2]) + mod_ref[0, 0:1]).astype(bf16)
    z = dot(h1, w_ref[...])
    cosine, sine = cos_ref[0], sin_ref[0]
    masks = head_masks()
    for p in pairs():
        turned = []
        for part in range(2):
            zp = z[:, part * 384 + p.start : part * 384 + p.stop]
            n = zp * lax.rsqrt(head_mean(zp * zp) + EPS) * gain_ref[part : part + 1]
            turned.append(n * cosine + partner(n) * sine)
        q = (turned[0].astype(bf16).astype(f32) * 0.125).astype(bf16)
        k = turned[1].astype(bf16)
        v = z[:, 768 + p.start : 768 + p.stop].astype(bf16)
        q_ref[0, :, p], k_ref[0, :, p], v_ref[0, :, p] = q, k, v
        out = None
        for m in masks:
            e = jnp.exp(dot_nt(q * m, k))
            probs = (e * (1.0 / jnp.sum(e, axis=-1, keepdims=True))).astype(bf16)
            part_out = dot(probs, v * m)
            out = part_out if out is None else out + part_out
        att_ref[0, :, p] = out.astype(bf16)


def mlp_kernel(
    at_ref,
    kept_ref,
    got_ref,
    dkept_ref,
    dgot_ref,
    att_ref,
    mod_ref,
    proj_ref,
    wg_ref,
    wu_ref,
    wd_ref,
    keep_ref,
    send_ref,
    out_ref,
    outsend_ref,
    dmid_ref,
    sums_ref,
    branch_s,
    mid_s,
    h2_s,
    h2t_s,
    dmlp_s,
    mlp_s,
    dh2_s,
    units_s,
):
    j = pl.program_id(0)
    images = range(2)

    def rows(i):
        return slice(i * 256, (i + 1) * 256)

    def dy_of(i):
        return jnp.concatenate([dkept_ref[i], dgot_ref[i]], axis=0).astype(f32)

    @pl.when(j == 0)
    def _():
        branch_s[...] = dot(att_ref[...], proj_ref[...])
        for i in images:
            x = jnp.concatenate([kept_ref[i], got_ref[i]], axis=0).astype(f32)
            mid = x + mod_ref[i, 2:3] * branch_s[rows(i)]
            mid_s[rows(i)] = mid
            h2_s[rows(i)] = (mid * inv_rms(mid) * (1.0 + mod_ref[i, 4:5]) + mod_ref[i, 3:4]).astype(
                bf16
            )
            dmlp_s[rows(i)] = (mod_ref[i, 5:6] * dy_of(i)).astype(bf16)
        h2t_s[...] = h2_s[...].T
        mlp_s[...] = jnp.zeros_like(mlp_s)
        dh2_s[...] = jnp.zeros_like(dh2_s)

    h2 = h2_s[...]
    d_mlp = dmlp_s[...]
    g = dot(h2, wg_ref[...])
    u = dot(h2, wu_ref[...])
    d_hid = dot_nt(d_mlp, wd_ref[...])
    sig = 1.0 / (1.0 + jnp.exp(-g))
    act = g * sig
    hid = (act * u).astype(bf16)
    du = (d_hid * act).astype(bf16)
    dg = (d_hid * u * (sig + act * (1.0 - sig))).astype(bf16)
    mlp_s[...] += dot(hid, wd_ref[...])
    dh2_s[...] += dot_nt(dg, wg_ref[...]) + dot_nt(du, wu_ref[...])
    h2t = h2t_s[...]
    for n, d in ((0, dg), (2, du)):
        grad = dot(h2t, d).astype(bf16)
        for b in range(2):
            units_s[(n + b) // 3, pl.ds((n + b) % 3 * 384, 384)] = grad[:, b * 128 : b * 128 + 128]
    down = dot_tn(hid, d_mlp).astype(bf16)
    for b in range(2):
        for c in range(3):
            units_s[1, pl.ds((b + 1) * 384 + c * 128, 128)] = down[
                b * 128 : b * 128 + 128, c * 128 : c * 128 + 128
            ]
    keep_ref[...] = units_s[at_ref[1]]
    send_ref[...] = units_s[1 - at_ref[1]]

    @pl.when(j == 3)
    def _():
        for i in images:
            mid, mlp, dh2, dy = mid_s[rows(i)], mlp_s[rows(i)], dh2_s[rows(i)], dy_of(i)
            out = (mid + mod_ref[i, 5:6] * mlp).astype(bf16)
            out_ref[i] = out[:128]
            outsend_ref[i] = out[128:]
            s = inv_rms(mid)
            n = mid * s
            e2 = dh2 * (1.0 + mod_ref[i, 4:5])
            d_mid = dy + s * (e2 - n * jnp.mean(e2 * n, axis=-1, keepdims=True))
            dmid_ref[rows(i)] = d_mid
            for k, v in enumerate((d_mid * branch_s[rows(i)], dh2, dh2 * n, dy * mlp)):
                total = jnp.sum(v, axis=0, keepdims=True)
                for b, p in enumerate(pairs()):
                    sums_ref[pl.ds(i * 12 + k * 3 + b, 1)] = total[:, p]


def backward_kernel(
    at_ref,
    kept_ref,
    got_ref,
    mod_ref,
    w_ref,
    gain_ref,
    cos_ref,
    sin_ref,
    q_ref,
    k_ref,
    v_ref,
    att_ref,
    dmid_ref,
    proj_ref,
    keep_ref,
    send_ref,
    grad_ref,
    gradsend_ref,
    sums_ref,
    h1_s,
    dqkv_s,
    dbranch_s,
    att_s,
    gain_s,
    units_s,
):
    i = pl.program_id(0)
    here = pl.ds(pl.multiple_of(i * 256, 256), 256)
    x = both(kept_ref, got_ref)
    s1 = inv_rms(x)
    n1 = x * s1
    h1 = (n1 * (1.0 + mod_ref[0, 1:2]) + mod_ref[0, 0:1]).astype(bf16)
    h1_s[here] = h1
    att_s[here] = att_ref[0]
    d_mid = dmid_ref[...]
    d_branch = (mod_ref[0, 2:3] * d_mid).astype(bf16)
    dbranch_s[here] = d_branch
    d_att = dot_nt(d_branch, proj_ref[...]).astype(bf16)
    z = dot(h1, w_ref[:, :768])
    cosine, sine = cos_ref[0], sin_ref[0]
    masks = head_masks()
    gain_sums = [None, None]
    for p in pairs():
        q, k, v, do = q_ref[0, :, p], k_ref[0, :, p], v_ref[0, :, p], d_att[:, p]
        dq = dk = dv = 0.0
        for m in masks:
            qm, km, vm, dom = q * m, k * m, v * m, do * m
            e = jnp.exp(dot_nt(qm, k))
            soft = e * (1.0 / jnp.sum(e, axis=-1, keepdims=True))
            d_probs = dot_nt(dom, v)
            delta = jnp.sum(soft * d_probs, axis=-1, keepdims=True)
            ds = (soft * (d_probs - delta)).astype(bf16)
            dq = dq + dot(ds, km)
            dk = dk + dot_tn(ds, qm)
            dv = dv + dot_tn(soft.astype(bf16), dom)
        for part, d in enumerate((dq * 0.125, dk)):
            zp = z[:, part * 384 + p.start : part * 384 + p.stop]
            r = lax.rsqrt(head_mean(zp * zp) + EPS)
            n = zp * r
            dn = d * cosine - partner(d) * sine
            total = jnp.sum(dn * n, axis=0, keepdims=True)
            gain_sums[part] = total if gain_sums[part] is None else gain_sums[part] + total
            e = dn * gain_ref[part : part + 1]
            dz = r * (e - n * head_mean(e * n))
            dqkv_s[here, part * 384 + p.start : part * 384 + p.stop] = dz.astype(bf16)
        dqkv_s[here, 768 + p.start : 768 + p.stop] = dv.astype(bf16)
    d_h1 = dot_nt(dqkv_s[here], w_ref[...])
    e1 = d_h1 * (1.0 + mod_ref[0, 1:2])
    grad = d_mid + s1 * (e1 - n1 * jnp.mean(e1 * n1, axis=-1, keepdims=True))
    grad_ref[0] = grad[:128]
    gradsend_ref[0] = grad[128:].astype(bf16)
    gains = [g + pltpu.roll(g, 64, 1) for g in gain_sums]
    gains = jnp.where(lane_iota((1, 128)) < 64, gains[0], gains[1])

    def put_sums(at):
        for k, v in enumerate((d_h1, d_h1 * n1)):
            total = jnp.sum(v, axis=0, keepdims=True)
            for b, p in enumerate(pairs()):
                sums_ref[pl.ds(at * 6 + k * 3 + b, 1)] = total[:, p]

    @pl.when(i == 0)
    def _():
        put_sums(0)
        gain_s[...] = jnp.broadcast_to(gains, (8, 128))

    @pl.when(i == 1)
    def _():
        put_sums(1)
        sums_ref[pl.ds(12, 1)] = gain_s[0:1] + gains
        sums_ref[pl.ds(13, 3)] = jnp.zeros((3, 128), f32)
        h1t = h1_s[...].T
        for part in range(3):
            w = dot(h1t, dqkv_s[:, part * 384 : part * 384 + 384]).astype(bf16)
            for b, p in enumerate(pairs()):
                n = part * 3 + b
                units_s[n // 6, pl.ds(n % 6 * 384, 384)] = w[:, p]
        w = dot_tn(att_s[...], dbranch_s[...]).astype(bf16)
        for b, p in enumerate(pairs()):
            units_s[1, pl.ds((3 + b) * 384, 384)] = w[:, p]
        keep_ref[...] = units_s[at_ref[1]]
        send_ref[...] = units_s[1 - at_ref[1]]


def whole_spec(shape):
    return pl.BlockSpec(shape, lambda *_: (0,) * len(shape))


def params(mib):
    return pltpu.CompilerParams(vmem_limit_bytes=mib * MIB)


def shape_of(shape, dtype):
    return jax.ShapeDtypeStruct(shape, dtype)


def image_spec(shape):
    return pl.BlockSpec((1,) + shape, lambda i, at: (i,) + (0,) * len(shape))


KEPT = pl.BlockSpec((1, 128, 384), lambda i, at: (2 * at[0] + i, 0, 0))
KEPT2 = pl.BlockSpec((2, 128, 384), lambda j, at: (at[0], 0, 0))


def cost(flops, nbytes):
    return pl.CostEstimate(flops=flops, bytes_accessed=nbytes, transcendentals=0)


def forward_call(at, latents, got, mod, qkv_w, gains, cosine, sine):
    act = shape_of((2, 256, 384), bf16)
    return pl.pallas_call(
        forward_kernel,
        grid_spec=pltpu.PrefetchScalarGridSpec(
            num_scalar_prefetch=1,
            grid=(2,),
            in_specs=[
                KEPT,
                image_spec((128, 384)),
                image_spec((6, 384)),
                whole_spec((384, 1152)),
                whole_spec((2, 128)),
                image_spec((256, 128)),
                image_spec((256, 128)),
            ],
            out_specs=[image_spec((256, 384))] * 4,
        ),
        out_shape=[act] * 4,
        compiler_params=params(40),
        cost_estimate=cost(3_000_000_000, 4_000_000),
        name="attention_forward",
    )(at, latents, got, mod, qkv_w, gains, cosine, sine)


def mlp_call(at, latents, got, out_grad, dgot, att, mod, proj_w, gate_up_w, down_w):
    return pl.pallas_call(
        mlp_kernel,
        grid_spec=pltpu.PrefetchScalarGridSpec(
            num_scalar_prefetch=1,
            grid=(4,),
            in_specs=[
                KEPT2,
                whole_spec((2, 128, 384)),
                KEPT2,
                whole_spec((2, 128, 384)),
                whole_spec((512, 384)),
                whole_spec((2, 6, 384)),
                whole_spec((384, 384)),
                pl.BlockSpec((384, 256), lambda j, at: (0, j)),
                pl.BlockSpec((384, 256), lambda j, at: (0, j + 4)),
                pl.BlockSpec((256, 384), lambda j, at: (j, 0)),
            ],
            out_specs=[
                pl.BlockSpec((1152, 128), lambda j, at: (j, 0)),
                pl.BlockSpec((1152, 128), lambda j, at: (j, 0)),
                KEPT2,
                whole_spec((2, 128, 384)),
                whole_spec((512, 384)),
                whole_spec((24, 128)),
            ],
            scratch_shapes=[
                pltpu.VMEM((512, 384), f32),
                pltpu.VMEM((512, 384), f32),
                pltpu.VMEM((512, 384), bf16),
                pltpu.VMEM((384, 512), bf16),
                pltpu.VMEM((512, 384), bf16),
                pltpu.VMEM((512, 384), f32),
                pltpu.VMEM((512, 384), f32),
                pltpu.VMEM((2, 1152, 128), bf16),
            ],
        ),
        out_shape=[
            shape_of((4608, 128), bf16),
            shape_of((4608, 128), bf16),
            shape_of((4, 128, 384), bf16),
            shape_of((2, 128, 384), bf16),
            shape_of((512, 384), f32),
            shape_of((24, 128), f32),
        ],
        compiler_params=params(48),
        cost_estimate=cost(6_000_000_000, 8_000_000),
        name="mlp_both_ways",
    )(at, latents, got, out_grad, dgot, att, mod, proj_w, gate_up_w, gate_up_w, down_w)


def backward_call(at, latents, got, mod, qkv_w, gains, cosine, sine, q, k, v, att, d_mid, proj_w):
    return pl.pallas_call(
        backward_kernel,
        grid_spec=pltpu.PrefetchScalarGridSpec(
            num_scalar_prefetch=1,
            grid=(2,),
            in_specs=[
                KEPT,
                image_spec((128, 384)),
                image_spec((6, 384)),
                whole_spec((384, 1152)),
                whole_spec((2, 128)),
                image_spec((256, 128)),
                image_spec((256, 128)),
            ]
            + [image_spec((256, 384))] * 4
            + [pl.BlockSpec((256, 384), lambda i, at: (i, 0)), whole_spec((384, 384))],
            out_specs=[
                whole_spec((2304, 128)),
                whole_spec((2304, 128)),
                KEPT,
                image_spec((128, 384)),
                whole_spec((16, 128)),
            ],
            scratch_shapes=[
                pltpu.VMEM((512, 384), bf16),
                pltpu.VMEM((512, 1152), bf16),
                pltpu.VMEM((512, 384), bf16),
                pltpu.VMEM((512, 384), bf16),
                pltpu.VMEM((8, 128), f32),
                pltpu.VMEM((2, 2304, 128), bf16),
            ],
        ),
        out_shape=[
            shape_of((2304, 128), bf16),
            shape_of((2304, 128), bf16),
            shape_of((4, 128, 384), f32),
            shape_of((2, 128, 384), bf16),
            shape_of((16, 128), f32),
        ],
        compiler_params=params(48),
        cost_estimate=cost(5_000_000_000, 6_000_000),
        name="attention_backward",
    )(at, latents, got, mod, qkv_w, gains, cosine, sine, q, k, v, att, d_mid, proj_w)


def turn_tables(pos):
    lane = jnp.arange(128)
    rates = 10000.0 ** (-(lane % 16).astype(f32) / 16)
    where_row = (lane % 64) < 32
    pos = pos.astype(f32)
    angle = jnp.where(where_row, pos[..., 0:1], pos[..., 1:2]) * rates
    sign = jnp.where(lane % 32 < 16, -1.0, 1.0)
    return jnp.cos(angle), jnp.sin(angle) * sign


def join_kernel(a_ref, a_got_ref, b_ref, b_got_ref, extra_ref, out_ref):
    out_ref[:, :288] = (a_ref[...].astype(f32) + a_got_ref[...].astype(f32)).astype(bf16)
    out_ref[:, 288:432] = (b_ref[...].astype(f32) + b_got_ref[...].astype(f32)).astype(bf16)
    out_ref[:, 432:] = jnp.broadcast_to(extra_ref[...][None], (16, 48, 128))


def join_call(keep1, got1, keep2, got2, extra):
    big, small = (16, 288, 128), (16, 144, 128)
    return pl.pallas_call(
        join_kernel,
        out_shape=shape_of((16, 480, 128), bf16),
        compiler_params=params(32),
        cost_estimate=cost(2_000_000, 6_000_000),
        name="join_messages",
    )(keep1.reshape(big), got1.reshape(big), keep2.reshape(small), got2.reshape(small), extra)


def sum_kernel(a_ref, out_ref, extra_ref):
    total = a_ref[0, :432].astype(f32)
    for n in range(1, 16):
        total = total + a_ref[n, :432].astype(f32)
    out_ref[:432] = total.astype(bf16)
    out_ref[432:] = jnp.zeros((16, 128), bf16)
    extra_ref[...] = a_ref[:, 432:]


def sum_call(a):
    return pl.pallas_call(
        sum_kernel,
        out_shape=[shape_of((448, 128), bf16), shape_of((16, 48, 128), bf16)],
        compiler_params=params(32),
        cost_estimate=cost(2_000_000, 3_000_000),
        name="sum_xy",
    )(a)


def fetch(at_ref, own_ref, got_ref, slots, sems):
    c = at_ref[1]
    copies = [
        pltpu.make_async_copy(own_ref, slots.at[c], sems.at[0]),
        pltpu.make_async_copy(got_ref, slots.at[1 - c], sems.at[1]),
    ]
    for copy in copies:
        copy.start()
    for copy in copies:
        copy.wait()


def condition_kernel(
    at_ref,
    own_ref,
    got_ref,
    tw1_ref,
    tw2_ref,
    modw_ref,
    tw1g_ref,
    tw2g_ref,
    tableg_ref,
    modwg_ref,
    gains_ref,
    slots,
    rows_s,
    dmod_s,
    cond_s,
    emb_s,
    sems,
):
    fetch(at_ref, own_ref, got_ref, slots, sems)
    for h in range(2):
        for n in range(8):
            part = slots[h, pl.ds(n * 768, 768)]
            rows_s[pl.ds(h * 6144 + n * 768, 768)] = part.astype(f32)

    def line(r):
        return rows_s[pl.ds(r, 256, stride=48), :]

    for i in range(2):
        here = slice(i * 256, i * 256 + 256)
        for k in range(6):
            for b in range(3):
                r = 24 + i * 6 + k * 3 + b if k < 2 else i * 12 + (k - 2) * 3 + b
                at = k * 384 + b * 128
                dmod_s[here, at : at + 128] = line(r).astype(bf16)
        for b in range(2):
            emb_s[here, b * 128 : b * 128 + 128] = line(38 + i * 2 + b).astype(bf16)
        for b in range(3):
            cond_s[here, b * 128 : b * 128 + 128] = line(42 + i * 3 + b)
    gains_ref[...] = jnp.sum(line(36), axis=0, keepdims=True)
    codes = line(37)
    labels = jnp.concatenate([codes[:, i : i + 1] * 32.0 + codes[:, i + 2 : i + 3] for i in range(2)])
    cond = cond_s[...]
    sig = 1.0 / (1.0 + jnp.exp(-cond))
    act_t = (cond * sig).astype(bf16).T
    for k in range(6):
        cols = slice(k * 384, k * 384 + 384)
        modwg_ref[:, cols] = dot(act_t, dmod_s[:, cols])
    d_cond = dot_nt(dmod_s[...], modw_ref[...]) * (sig + cond * sig * (1.0 - sig))
    dc = d_cond.astype(bf16)
    labels = labels.astype(jnp.int32)
    for n in range(4):
        hot = jnp.where(lane_iota((512, 256)) + n * 256 == labels, 1.0, 0.0).astype(bf16)
        rows = dot_tn(hot, dc)
        top = min(256, 1001 - n * 256)
        tableg_ref[n * 256 : n * 256 + top] = rows[:top]
    emb = emb_s[...]
    pre = dot(emb, tw1_ref[...])
    sig = 1.0 / (1.0 + jnp.exp(-pre))
    hid = pre * sig
    tw2g_ref[...] = dot_tn(hid.astype(bf16), dc)
    d_pre = (dot_nt(dc, tw2_ref[...]) * (sig + hid * (1.0 - sig))).astype(bf16)
    tw1g_ref[...] = dot_tn(emb, d_pre)


def condition_call(at, own, got, t_w1, t_w2, mod_w):
    anywhere = pl.BlockSpec(memory_space=pl.ANY)
    shapes = [(256, 384), (384, 384), (1001, 384), (384, 2304), (1, 128)]
    return pl.pallas_call(
        condition_kernel,
        grid_spec=pltpu.PrefetchScalarGridSpec(
            num_scalar_prefetch=1,
            grid=(1,),
            in_specs=[anywhere, anywhere]
            + [whole_spec(s) for s in ((256, 384), (384, 384), (384, 2304))],
            out_specs=[whole_spec(s) for s in shapes],
            scratch_shapes=[
                pltpu.VMEM((2, 6144, 128), bf16),
                pltpu.VMEM((12288, 128), f32),
                pltpu.VMEM((512, 2304), bf16),
                pltpu.VMEM((512, 384), f32),
                pltpu.VMEM((512, 256), bf16),
                pltpu.SemaphoreType.DMA((2,)),
            ],
        ),
        out_shape=[shape_of(s, f32) for s in shapes],
        compiler_params=params(56),
        cost_estimate=cost(4_000_000_000, 12_000_000),
        name="condition_gradients",
    )(at, own, got, t_w1, t_w2, mod_w)


def cuts(start, chunk):
    out, at = [], start
    while at < start + 384:
        n = at // chunk
        stop = min((n + 1) * chunk, start + 384)
        out.append((n, at - n * chunk, stop - n * chunk))
        at = stop
    return out


def unpack_kernel(at_ref, own_ref, got_ref, qkv_ref, proj_ref, gu_ref, down_ref, slots, sems):
    t = pl.program_id(0)

    @pl.when(t == 0)
    def _():
        fetch(at_ref, own_ref, got_ref, slots, sems)

    def unit(half, first, u, chunk, base):
        return jnp.concatenate(
            [slots[half, first + n, base + a : base + b] for n, a, b in cuts(u * 384, chunk)]
        ).astype(f32)

    @pl.when(t < 4)
    def _():
        gu_ref[:, :128] = unit(0, 4 * t, 0, 288, 0)
        gu_ref[:, 128:] = unit(0, 4 * t, 1, 288, 0)
        for b, p in enumerate(pairs()):
            block = unit(t // 2, 8 * (t % 2), b, 144, 288)

            @pl.when(t < 3)
            def _():
                qkv_ref[:, p] = block

            @pl.when(t == 3)
            def _():
                proj_ref[:, p] = block

    @pl.when(t >= 4)
    def _():
        gu_ref[:, :128] = unit(0, 4 * (t - 4), 2, 288, 0)
        gu_ref[:, 128:] = unit(1, 4 * (t - 4), 0, 288, 0)

    for odd in range(2):

        @pl.when(t % 2 == odd)
        def _():
            rows = unit(1, 4 * (t // 2), 1 + odd, 288, 0)
            for b, p in enumerate(pairs()):
                down_ref[:, p] = rows[b * 128 : b * 128 + 128]


def unpack_call(at, own, got):
    anywhere = pl.BlockSpec(memory_space=pl.ANY)
    return pl.pallas_call(
        unpack_kernel,
        grid_spec=pltpu.PrefetchScalarGridSpec(
            num_scalar_prefetch=1,
            grid=(8,),
            in_specs=[anywhere, anywhere],
            out_specs=[
                pl.BlockSpec((384, 384), lambda t, at: (0, jnp.minimum(t, 2))),
                whole_spec((384, 384)),
                pl.BlockSpec((384, 256), lambda t, at: (0, t)),
                pl.BlockSpec((128, 384), lambda t, at: (t, 0)),
            ],
            scratch_shapes=[
                pltpu.VMEM((2, 16, 448, 128), bf16),
                pltpu.SemaphoreType.DMA((2,)),
            ],
        ),
        out_shape=[
            shape_of(s, f32) for s in ((384, 1152), (384, 384), (384, 2048), (1024, 384))
        ],
        compiler_params=params(32),
        cost_estimate=cost(2_000_000, 11_000_000),
        name="unpack_sums",
    )(at, own, got)


def flat(y, z, x, c):
    return ((((y * 8 + z) * 2 + x % 2) * 2 + c) * 2) + x // 2


def groups(axes):
    rest = [a for a in "yzxc" if a not in axes]
    out = []
    for fixed in itertools.product(*[range(SIZES[a]) for a in rest]):
        place = dict(zip(rest, fixed))
        row = []
        for moving in itertools.product(*[range(SIZES[a]) for a in axes]):
            row.append(flat(**{**place, **dict(zip(axes, moving))}))
        out.append(row)
    return out


def exchange(v, axes):
    return lax.all_to_all(v, AXES, 0, 0, tiled=True, axis_index_groups=groups(axes))


def gather(v, axes):
    n = math.prod(SIZES[a] for a in axes)
    return exchange(jnp.broadcast_to(v[None], (n,) + v.shape), axes)


BAND_SWAP = [(n, n ^ 1) for n in range(256)]
CORE_SWAP = [(n, n ^ 2) for n in range(256)]


def swap(v):
    return lax.ppermute(v, AXES, BAND_SWAP)


def core_swap(v):
    return lax.ppermute(v, AXES, CORE_SWAP)


def silu(v):
    return v / (1.0 + jnp.exp(-v))


def condition(t_w1, t_w2, label_table, mod_w, tsteps, labs):
    high = lax.Precision.HIGHEST
    freqs = jnp.exp(-math.log(10000.0) * jnp.arange(128, dtype=f32) / 128)
    angle = tsteps.astype(f32)[:, None] * freqs[None, :]
    emb = jnp.concatenate([jnp.cos(angle), jnp.sin(angle)], axis=-1)
    hidden = jax.nn.silu(jnp.dot(emb, t_w1.astype(f32), precision=high))
    hot = (labs[:, None] == jnp.arange(label_table.shape[0], dtype=jnp.int32)[None, :]).astype(f32)
    cond = jnp.dot(hidden, t_w2.astype(f32), precision=high) + jnp.dot(
        hot, label_table.astype(f32), precision=high
    )
    return emb, cond, jnp.dot(jax.nn.silu(cond), mod_w.astype(f32), precision=high)


def body(
    latents,
    pos_row,
    pos_col,
    timesteps,
    labels,
    t_w1,
    t_w2,
    label_table,
    mod_w,
    qkv_w,
    q_gain,
    k_gain,
    proj_w,
    gate_up_w,
    down_w,
    out_grad,
):
    band = lax.axis_index("band")
    core = lax.axis_index("img") % 2
    at = jnp.stack([band, core]).astype(jnp.int32)
    mine = 2 * band
    other = 2 - mine

    def theirs(v):
        return lax.dynamic_slice_in_dim(v, other, 2, 0)

    def ours(v):
        return lax.dynamic_slice_in_dim(v, mine, 2, 0)

    got = swap(theirs(latents))
    pos = jnp.stack([pos_row, pos_col], axis=-1)
    pos = jnp.concatenate([ours(pos), swap(theirs(pos))], axis=1)
    dgot = swap(theirs(out_grad))
    tsteps, labs = ours(timesteps), ours(labels)
    emb, cond, mod = condition(t_w1, t_w2, label_table, mod_w, tsteps, labs)
    mod = mod.reshape(2, 6, 384)
    gains = jnp.stack([jnp.tile(q_gain, 2), jnp.tile(k_gain, 2)])
    cosine, sine = turn_tables(pos)
    q, k, v, att = forward_call(at, latents, got, mod, qkv_w, gains, cosine, sine)
    keep1, send1, block_out, out_send, d_mid, sums1 = mlp_call(
        at, latents, got, out_grad, dgot, att.reshape(512, 384), mod, proj_w, gate_up_w, down_w
    )
    got1 = core_swap(send1)
    keep2, send2, latents_grad, grad_send, sums2 = backward_call(
        at, latents, got, mod, qkv_w, gains, cosine, sine, q, k, v, att, d_mid, proj_w
    )
    codes = jnp.concatenate([labs // 32, labs % 32]).astype(f32)
    codes = jnp.pad(codes[None], ((0, 0), (0, 124)))
    extra = jnp.concatenate(
        [sums1, sums2[:13], codes, emb.reshape(4, 128), cond.reshape(6, 128)]
    ).astype(bf16)
    chunk, extra = sum_call(
        exchange(join_call(keep1, got1, keep2, core_swap(send2), extra), "xy")
    )
    extra = lax.all_gather(
        extra.reshape(768, 128), AXES, axis=0, tiled=True, axis_index_groups=groups("z")
    )
    chunk = jnp.sum(exchange(chunk.reshape(8, 56, 128), "z").astype(f32), axis=0).astype(bf16)
    chunk = gather(chunk, "z").reshape(448, 128)
    chunk, extra = lax.optimization_barrier((chunk, extra))
    summed = gather(chunk, "xy")
    conditioned = condition_call(at, extra, core_swap(extra), t_w1, t_w2, mod_w)
    out_got, grad_got = swap(out_send), swap(grad_send)
    summed, conditioned, out_got, grad_got = lax.optimization_barrier(
        (summed, conditioned, out_got, grad_got)
    )
    tw1_grad, tw2_grad, table_grad, modw_grad, gain_sums = conditioned
    qkv_sum, proj_sum, gu_sum, down_sum = unpack_call(at, summed, core_swap(summed))
    block_out = lax.dynamic_update_slice_in_dim(block_out, out_got, other, 0)
    latents_grad = lax.dynamic_update_slice_in_dim(
        latents_grad, grad_got.astype(f32), other, 0
    )
    return (
        block_out,
        latents_grad,
        tw1_grad,
        tw2_grad,
        table_grad,
        modw_grad,
        qkv_sum,
        gain_sums[0, :64],
        gain_sums[0, 64:],
        proj_sum,
        gu_sum,
        down_sum,
    )


def solution(mesh):
    split = P("img", "band", None)
    return jax.shard_map(
        body,
        mesh=mesh,
        in_specs=(split, P("img", "band"), P("img", "band"), P("img"), P("img"))
        + (P(),) * 10
        + (split,),
        out_specs=(split, split) + (P(),) * 10,
        check_vma=False,
    )
```

profile of v0, /device:TPU:1, one launch (start us, length us, event | category | flops | bytes accessed | tf_op | source)
XLA Modules:
  0.0 197.9 jit_solution(3607396934428919385)
XLA Ops:
  8.3 3.7 %collective-permute-start = (bf16[2,128,384]{2,1,0:T(8,128)(2,1)S(1)}, bf16[2,128,384]{2,1,0:T(8,128)(2,1)S(1)}, u32[]{:S(2)}, u32[]{:S(2)}) collective-permute-start(bf16[2,128,384]{2,1,0:T(8,128)(2,1)S(1)} %constant_dynamic-slice_fusion.1), channel_id=1, source_target_pairs={{0,1},{1,0},{2,3},{3,2},{4,5},{5,4},{6,7},{7,6},{8,9},{9,8},{10,11... | collective-permute-start | bytes 589832 | tf_op jit(solution)/shard_map/ppermute | solution.py:697
  13.7 3.0 %collective-permute-start.2 = (s32[2,128,2]{1,0,2:T(2,128)S(1)}, s32[2,128,2]{1,0,2:T(2,128)S(1)}, u32[]{:S(2)}, u32[]{:S(2)}) collective-permute-start(s32[2,128,2]{1,0,2:T(2,128)S(1)} %get-tuple-element.91), channel_id=1, source_target_pairs={{0,1},{1,0},{2,3},{3,2},{4,5},{5,4},{6,7},{7,6},{8,9},{9,8},{10,11... | collective-permute-start | bytes 6152 | tf_op jit(solution)/shard_map/ppermute | solution.py:697
  18.3 1.3 fusion.25
  20.3 1.1 fusion.17
  21.4 1.3 fusion.5
  23.6 2.3 %fusion.4 = f32[2,2304]{1,0:T(2,128)S(1)} fusion(bf16[384,2304]{1,0:T(8,128)(2,1)} %modw_ref.1, f32[2,384]{1,0:T(2,128)S(1)} %get-tuple-element.97), kind=kOutput, calls=%fused_computation.15 | convolution fusion | flops 21236736 | bytes 1790976 | tf_op jit(solution)/shard_map/dot_general | solution.py:718
  27.1 5.5 %attention_forward.1 = (bf16[2,256,384]{2,1,0:T(8,128)(2,1)S(1)}, bf16[2,256,384]{2,1,0:T(8,128)(2,1)S(1)}, bf16[2,256,384]{2,1,0:T(8,128)(2,1)S(1)}, bf16[2,256,384]{2,1,0:T(8,128)(2,1)S(1)}) custom-call(s32[2]{0:T(128)S(1)} %pad_add_fusion.at_ref, bf16[4,128,384]{2,1,0:T(8,128)(2,1)S(1)} %copy-done.4, ...), custom_call_target="tpu_custom_call" | custom-call | flops 3000000000 | bytes 4000000 | tf_op jit(solution)/shard_map/attention_forward/pallas_call | solution.py:318
  34.3 9.5 %mlp_both_ways.1 = (bf16[4608,128]{1,0:T(8,128)(2,1)S(1)}, bf16[4608,128]{1,0:T(8,128)(2,1)}, bf16[4,128,384]{2,1,0:T(8,128)(2,1)}, bf16[2,128,384]{2,1,0:T(8,12...) custom-call(s32[2]{0:T(128)S(1)} %pad_add_fusion.at_ref, bf16[4,128,384]{2,1,0:T(8,128)(2,1)S(1)} %copy-done.4, ...), custom_call_target="tpu_custom_call" | custom-call | flops 6000000000 | bytes 8000000 | tf_op jit(solution)/shard_map/mlp_both_ways/pallas_call | solution.py:342
  44.5 1.5 collective-permute-start.3
  47.6 10.2 %attention_backward.1 = (bf16[2304,128]{1,0:T(8,128)(2,1)S(1)}, bf16[2304,128]{1,0:T(8,128)(2,1)}, f32[4,128,384]{2,1,0:T(8,128)}, bf16[2,128,384]{2,1,0:T(8,128)(2,1)S(1)}, f32[16,128]{1,0:T(8,128)S(1)}) custom-call(s32[2]{0:T(128)S(1)} %copy-done.8, bf16[4,128,384]{2,1,0:T(8,128)(2,1)S(1)} %copy-done.4, bf16[2,128,384]{2,1,0:T(8,128)(2,1)S(1)} %copy-done.15, ...), custom_call_target="tpu_custom_call" | custom-call | flops 5000000000 | bytes 6000000 | tf_op jit(solution)/shard_map/attention_backward/pallas_call | solution.py:393
  64.7 1.5 join_messages.1
  66.2 30.1 %all_to_all.20.a_ref = bf16[16,480,128]{2,1,0:T(8,128)(2,1)S(1)} all-to-all(bf16[16,480,128]{2,1,0:T(8,128)(2,1)S(1)} %join_messages.1), channel_id=1, replica_groups={{0,64,128,192,4,68,132,196,1,65,129,193,5,69,133,197},{2,66,130,194,6,7..., dimensions={0} | all-to-all | bytes 3932160 | tf_op jit(solution)/shard_map/all_to_all | solution.py:684
  97.0 15.7 %all_to_all.21 = bf16[8,56,128]{2,1,0:T(8,128)(2,1)S(1)} all-to-all(bf16[8,56,128]{2,1,0:T(8,128)(2,1)S(1)} %bitcast.31), channel_id=1, replica_groups={{0,8,16,24,32,40,48,56},{2,10,18,26,34,42,50,58},{4,12,20,28,36,44,52,6..., dimensions={0} | all-to-all | bytes 229376 | tf_op jit(solution)/shard_map/all_to_all | solution.py:684
  112.8 10.9 %all_to_all.22 = bf16[8,56,128]{2,1,0:T(8,128)(2,1)S(1)} all-to-all(bf16[8,56,128]{2,1,0:T(8,128)(2,1)S(1)} %broadcast_in_dim.58), channel_id=1, replica_groups={{0,8,16,24,32,40,48,56},{2,10,18,26,34,42,50,58},{4,12,20,28,36,44,52,6..., dimensions={0} | all-to-all | bytes 229376 | tf_op jit(solution)/shard_map/all_to_all | solution.py:684
  123.7 12.9 %all-gather.2.cloned.1.call-done.own_ref = bf16[6144,128]{1,0:T(8,128)(2,1)} async-done(((bf16[768,128]{1,0:T(8,128)(2,1)}), bf16[6144,128]{1,0:T(8,128)(2,1)}) %all-gather.2.cloned.1.call-update) | async-done | bytes 1572880 | tf_op jit(solution)/shard_map/all_gather | solution.py:776
  136.7 3.4 %collective-permute-start.5 = (bf16[6144,128]{1,0:T(8,128)(2,1)}, bf16[6144,128]{1,0:T(8,128)(2,1)}, u32[]{:S(2)}, u32[]{:S(2)}) collective-permute-start(bf16[6144,128]{1,0:T(8,128)(2,1)} %all-gather.2.cloned.1.call-done.own_ref), channel_id=1, source_target_pairs={{0,2},{1,3},{2,0},{3,1},{4,6},{5,7},{6,4},{7,5},{8,10},{9,11},{10,... | collective-permute-start | bytes 4718600 | tf_op jit(solution)/shard_map/ppermute | solution.py:701
  140.1 1.6 broadcast_in_dim.59
  141.7 6.4 %all-to-all-start.3 = ((bf16[16,448,128]{2,1,0:T(8,128)(2,1)}), bf16[16,448,128]{2,1,0:T(8,128)(2,1)S(1)}, u32[]{:S(2)}, u32[]{:S(2)}) async-start(bf16[16,448,128]{2,1,0:T(8,128)(2,1)} %broadcast_in_dim.59), calls=%async_computation.3 | async-start | bytes 3670016 | tf_op jit(solution)/shard_map/all_to_all | solution.py:684
  148.2 3.0 %collective-permute-start.6 = (bf16[2,128,384]{2,1,0:T(8,128)(2,1)S(1)}, bf16[2,128,384]{2,1,0:T(8,128)(2,1)S(1)}, u32[]{:S(2)}, u32[]{:S(2)}) collective-permute-start(bf16[2,128,384]{2,1,0:T(8,128)(2,1)S(1)} %copy-done.19), channel_id=1, source_target_pairs={{0,1},{1,0},{2,3},{3,2},{4,5},{5,4},{6,7},{7,6},{8,9},{9,8},{10,11... | collective-permute-start | bytes 589832 | tf_op jit(solution)/shard_map/ppermute | solution.py:697
  151.5 11.1 %condition_gradients.1 = (f32[256,384]{1,0:T(8,128)}, f32[384,384]{1,0:T(8,128)}, f32[1001,384]{1,0:T(8,128)}, f32[384,2304]{1,0:T(8,128)}, f32[1,128]{1,0:T(1,128)}) custom-call(s32[2]{0:T(128)} %copy-done.7, bf16[6144,128]{1,0:T(8,128)(2,1)} %all-gather.2.cloned.1.call-done.own_ref, bf16[6144,128]{1,0:T(8,128)(2,1)} %collective-permute-done.5.got_ref, ...), custom_call_target="tpu_custom_call" | custom-call | flops 4000000000 | bytes 12000000 | tf_op jit(solution)/shard_map/condition_gradients/pallas_call | solution.py:564
  162.6 14.4 %collective-permute-done.6 = bf16[2,128,384]{2,1,0:T(8,128)(2,1)S(1)} collective-permute-done((bf16[2,128,384]{2,1,0:T(8,128)(2,1)S(1)}, bf16[2,128,384]{2,1,0:T(8,128)(2,1)S(1)}, u32[]{:S(2)}, u32[]{:S(2)}) %collective-permute-start.6) | collective-permute-done | bytes 196640 | tf_op jit(solution)/shard_map/ppermute | solution.py:697
  177.0 4.2 %collective-permute-done.7 = bf16[2,128,384]{2,1,0:T(8,128)(2,1)S(1)} collective-permute-done((bf16[2,128,384]{2,1,0:T(8,128)(2,1)S(1)}, bf16[2,128,384]{2,1,0:T(8,128)(2,1)S(1)}, u32[]{:S(2)}, u32[]{:S(2)}) %collective-permute-start.7) | collective-permute-done | bytes 196640 | tf_op jit(solution)/shard_map/ppermute | solution.py:697
  183.0 1.3 slice_bitcast_fusion.2
  185.8 5.3 %unpack_sums.1 = (f32[384,1152]{1,0:T(8,128)}, f32[384,384]{1,0:T(8,128)}, f32[384,2048]{1,0:T(8,128)}, f32[1024,384]{1,0:T(8,128)}) custom-call(s32[2]{0:T(128)S(1)} %copy-done.9, bf16[16,448,128]{2,1,0:T(8,128)(2,1)S(1)} %all-to-all-done.3.own_ref, bf16[16,448,128]{2,1,0:T(8,128)(2,1)S(1)} %collective-permute-done.8.got_ref), custom_call_target="tpu_custom_call" | custom-call | flops 2000000 | bytes 11000000 | tf_op jit(solution)/shard_map/unpack_sums/pallas_call | solution.py:641
  (100 shorter events, 22.1 us)
Async XLA Ops:
  7.2 15.6 %copy-start = (bf16[1001,384]{1,0:T(8,128)(2,1)S(1)}, bf16[1001,384]{1,0:T(8,128)(2,1)}, u32[]{:S(2)}) copy-start(bf16[1001,384]{1,0:T(8,128)(2,1)} %param.23) | copy-start | bytes 2306308
  7.2 129.5 %all-gather.2.cloned.1.call-start = ((), (), s32[]{:S(2)}) async-start(), calls=%async_computation.4 | async-start | bytes 1769472 | tf_op jit(solution)/shard_map/all_gather | solution.py:776
  8.3 18.8 %collective-permute-start = (bf16[2,128,384]{2,1,0:T(8,128)(2,1)S(1)}, bf16[2,128,384]{2,1,0:T(8,128)(2,1)S(1)}, u32[]{:S(2)}, u32[]{:S(2)}) collective-permute-start(bf16[2,128,384]{2,1,0:T(8,128)(2,1)S(1)} %constant_dynamic-slice_fusion.1), channel_id=1, source_target_pairs={{0,1},{1,0},{2,3},{3,2},{4,5},{5,4},{6,7},{7,6},{8,9},{9,8},{10,11... | collective-permute-start | bytes 589832 | tf_op jit(solution)/shard_map/ppermute | solution.py:697
  12.9 19.8 %collective-permute-start.1 = (bf16[2,128,384]{2,1,0:T(8,128)(2,1)S(1)}, bf16[2,128,384]{2,1,0:T(8,128)(2,1)S(1)}, u32[]{:S(2)}, u32[]{:S(2)}) collective-permute-start(bf16[2,128,384]{2,1,0:T(8,128)(2,1)S(1)} %constant_dynamic-slice_fusion), channel_id=1, source_target_pairs={{0,1},{1,0},{2,3},{3,2},{4,5},{5,4},{6,7},{7,6},{8,9},{9,8},{10,11... | collective-permute-start | bytes 589832 | tf_op jit(solution)/shard_map/ppermute | solution.py:697
  13.7 12.2 %collective-permute-start.2 = (s32[2,128,2]{1,0,2:T(2,128)S(1)}, s32[2,128,2]{1,0,2:T(2,128)S(1)}, u32[]{:S(2)}, u32[]{:S(2)}) collective-permute-start(s32[2,128,2]{1,0,2:T(2,128)S(1)} %get-tuple-element.91), channel_id=1, source_target_pairs={{0,1},{1,0},{2,3},{3,2},{4,5},{5,4},{6,7},{7,6},{8,9},{9,8},{10,11... | collective-permute-start | bytes 6152 | tf_op jit(solution)/shard_map/ppermute | solution.py:697
  19.7 7.3 %copy-start.24 = (f32[2,128]{1,0:T(2,128)}, f32[2,128]{1,0:T(2,128)S(1)}, u32[]{:S(2)}) copy-start(f32[2,128]{1,0:T(2,128)S(1)} %get-tuple-element.93) | copy-start | bytes 3076
  26.0 7.4 %copy-start.7 = (s32[2]{0:T(128)}, s32[2]{0:T(128)S(1)}, u32[]{:S(2)}) copy-start(s32[2]{0:T(128)S(1)} %pad_add_fusion.at_ref) | copy-start | bytes 28
  27.1 6.3 %copy-start.14 = (bf16[2,128,384]{2,1,0:T(8,128)(2,1)}, bf16[2,128,384]{2,1,0:T(8,128)(2,1)S(1)}, u32[]{:S(2)}) copy-start(bf16[2,128,384]{2,1,0:T(8,128)(2,1)S(1)} %collective-permute-done.got_ref) | copy-start | bytes 589828
  27.1 6.3 %copy-start.3 = (bf16[4,128,384]{2,1,0:T(8,128)(2,1)S(1)}, bf16[4,128,384]{2,1,0:T(8,128)(2,1)}, u32[]{:S(2)}) copy-start(bf16[4,128,384]{2,1,0:T(8,128)(2,1)} %dkept_ref.1) | copy-start | bytes 1179652
  27.1 6.3 %copy-start.12 = (bf16[1024,384]{1,0:T(8,128)(2,1)S(1)}, bf16[1024,384]{1,0:T(8,128)(2,1)}, u32[]{:S(2)}) copy-start(bf16[1024,384]{1,0:T(8,128)(2,1)} %wd_ref.1) | copy-start | bytes 2359300
  34.3 11.7 %copy-start.11 = (bf16[384,1152]{1,0:T(8,128)(2,1)S(1)}, bf16[384,1152]{1,0:T(8,128)(2,1)}, u32[]{:S(2)}) copy-start(bf16[384,1152]{1,0:T(8,128)(2,1)} %w_ref.3) | copy-start | bytes 2654212
  44.5 13.3 %copy-start.5 = (f32[24,128]{1,0:T(8,128)}, f32[24,128]{1,0:T(8,128)S(1)}, u32[]{:S(2)}) copy-start(f32[24,128]{1,0:T(8,128)S(1)} %get-tuple-element.58) | copy-start | bytes 36868
  44.5 19.1 %collective-permute-start.3 = (bf16[4608,128]{1,0:T(8,128)(2,1)}, bf16[4608,128]{1,0:T(8,128)(2,1)S(1)}, u32[]{:S(2)}, u32[]{:S(2)}) collective-permute-start(bf16[4608,128]{1,0:T(8,128)(2,1)} %get-tuple-element.51), channel_id=1, source_target_pairs={{0,2},{1,3},{2,0},{3,1},{4,6},{5,7},{6,4},{7,5},{8,10},{9,11},{10,... | collective-permute-start | bytes 3538952 | tf_op jit(solution)/shard_map/ppermute | solution.py:701
  47.6 12.3 %copy-start.23 = (f32[2,128]{1,0:T(2,128)S(1)}, f32[2,128]{1,0:T(2,128)}, u32[]{:S(2)}) copy-start(f32[2,128]{1,0:T(2,128)} %copy-done.22) | copy-start | bytes 3076
  47.6 12.3 %copy-start.25 = (f32[2,128]{1,0:T(2,128)S(1)}, f32[2,128]{1,0:T(2,128)}, u32[]{:S(2)}) copy-start(f32[2,128]{1,0:T(2,128)} %copy-done.24) | copy-start | bytes 3076
  59.9 3.7 %collective-permute-start.4 = (bf16[2304,128]{1,0:T(8,128)(2,1)}, bf16[2304,128]{1,0:T(8,128)(2,1)}, u32[]{:S(2)}, u32[]{:S(2)}) collective-permute-start(bf16[2304,128]{1,0:T(8,128)(2,1)} %get-tuple-element.57), channel_id=1, source_target_pairs={{0,2},{1,3},{2,0},{3,1},{4,6},{5,7},{6,4},{7,5},{8,10},{9,11},{10,... | collective-permute-start | bytes 1769480 | tf_op jit(solution)/shard_map/ppermute | solution.py:701
  136.7 14.8 %collective-permute-start.5 = (bf16[6144,128]{1,0:T(8,128)(2,1)}, bf16[6144,128]{1,0:T(8,128)(2,1)}, u32[]{:S(2)}, u32[]{:S(2)}) collective-permute-start(bf16[6144,128]{1,0:T(8,128)(2,1)} %all-gather.2.cloned.1.call-done.own_ref), channel_id=1, source_target_pairs={{0,2},{1,3},{2,0},{3,1},{4,6},{5,7},{6,4},{7,5},{8,10},{9,11},{10,... | collective-permute-start | bytes 4718600 | tf_op jit(solution)/shard_map/ppermute | solution.py:701
  141.7 6.5 %copy-start.19 = (bf16[2,128,384]{2,1,0:T(8,128)(2,1)S(1)}, bf16[2,128,384]{2,1,0:T(8,128)(2,1)}, u32[]{:S(2)}) copy-start(bf16[2,128,384]{2,1,0:T(8,128)(2,1)} %copy-done.18) | copy-start | bytes 589828
  141.7 9.4 %copy-start.21 = (bf16[2,128,384]{2,1,0:T(8,128)(2,1)S(1)}, bf16[2,128,384]{2,1,0:T(8,128)(2,1)}, u32[]{:S(2)}) copy-start(bf16[2,128,384]{2,1,0:T(8,128)(2,1)} %copy-done.20) | copy-start | bytes 589828
  141.7 39.5 %all-to-all-start.3 = ((bf16[16,448,128]{2,1,0:T(8,128)(2,1)}), bf16[16,448,128]{2,1,0:T(8,128)(2,1)S(1)}, u32[]{:S(2)}, u32[]{:S(2)}) async-start(bf16[16,448,128]{2,1,0:T(8,128)(2,1)} %broadcast_in_dim.59), calls=%async_computation.3 | async-start | bytes 3670016 | tf_op jit(solution)/shard_map/all_to_all | solution.py:684
  148.2 28.9 %collective-permute-start.6 = (bf16[2,128,384]{2,1,0:T(8,128)(2,1)S(1)}, bf16[2,128,384]{2,1,0:T(8,128)(2,1)S(1)}, u32[]{:S(2)}, u32[]{:S(2)}) collective-permute-start(bf16[2,128,384]{2,1,0:T(8,128)(2,1)S(1)} %copy-done.19), channel_id=1, source_target_pairs={{0,1},{1,0},{2,3},{3,2},{4,5},{5,4},{6,7},{7,6},{8,9},{9,8},{10,11... | collective-permute-start | bytes 589832 | tf_op jit(solution)/shard_map/ppermute | solution.py:697
  151.1 34.6 %copy-start.9 = (s32[2]{0:T(128)S(1)}, s32[2]{0:T(128)}, u32[]{:S(2)}) copy-start(s32[2]{0:T(128)} %copy-done.7) | copy-start | bytes 28
  151.1 30.1 %collective-permute-start.7 = (bf16[2,128,384]{2,1,0:T(8,128)(2,1)S(1)}, bf16[2,128,384]{2,1,0:T(8,128)(2,1)S(1)}, u32[]{:S(2)}, u32[]{:S(2)}) collective-permute-start(bf16[2,128,384]{2,1,0:T(8,128)(2,1)S(1)} %copy-done.21), channel_id=1, source_target_pairs={{0,1},{1,0},{2,3},{3,2},{4,5},{5,4},{6,7},{7,6},{8,9},{9,8},{10,11... | collective-permute-start | bytes 589832 | tf_op jit(solution)/shard_map/ppermute | solution.py:697
  181.2 4.5 %collective-permute-start.8 = (bf16[16,448,128]{2,1,0:T(8,128)(2,1)S(1)}, bf16[16,448,128]{2,1,0:T(8,128)(2,1)S(1)}, u32[]{:S(2)}, u32[]{:S(2)}) collective-permute-start(bf16[16,448,128]{2,1,0:T(8,128)(2,1)S(1)} %all-to-all-done.3.own_ref), channel_id=1, source_target_pairs={{0,2},{1,3},{2,0},{3,1},{4,6},{5,7},{6,4},{7,5},{8,10},{9,11},{10,... | collective-permute-start | bytes 5505032 | tf_op jit(solution)/shard_map/ppermute | solution.py:701
  (14 other events, 29.2 us)
Sparse Core Ops, SparseCore 0:
  97.2 39.4 all-gather.1
where the time goes:
time: 199 us; the launch traced here: 198 us
  blocking collectives  56.7 us (28%)
  Pallas kernels  43.9 us (22%)
  waiting for transfers between devices  32.3 us (16%)
  starting transfers between devices  22.6 us (11%)
  local copies, waits for them, and re-layouts  16.3 us (8%)
  between operations  14.4 us (7%)
  other arithmetic  6.24 us (3%)
  matrix products  5.55 us (3%)
    all_to_all x3, blocking collectives, exchange(): lax.all_to_all(v, AXES, 0, 0, tiled=True, axis_index_groups=groups(axes))  56.7 us
    ppermute x5, waiting for transfers between devices, swap(): return lax.ppermute(v, AXES, BAND_SWAP)  18.7 us
    all_gather x1, waiting for transfers between devices, body(): lax.all_gather(extra.reshape(768, 128), AXES, axis=0, tiled=True, axis_in...  12.9 us
    pallas_call x1, Pallas kernels, condition_call(): pl.pallas_call(condition_kernel, grid_spec=pltpu.PrefetchScalarGridSpec(n...  11.1 us
    pallas_call x1, Pallas kernels, backward_call(): pl.pallas_call(backward_kernel, grid_spec=pltpu.PrefetchScalarGridSpec(nu...  10.2 us
    ppermute x5, starting transfers between devices, swap(): return lax.ppermute(v, AXES, BAND_SWAP)  10.1 us
    pallas_call x1, Pallas kernels, mlp_call(): pl.pallas_call(mlp_kernel, grid_spec=pltpu.PrefetchScalarGridSpec(num_sca...  9.52 us
    unnamed x54, local copies, waits for them, and re-layouts  7.64 us
  transfers between devices with their start and end apart: 11, of which 4 were waited for; matrix products, arithmetic and copies ran while one was open for 10% of the time, Pallas kernels for 14%

commit v1 on v0

--- a/solution.py
+++ b/solution.py
@@ -7,6 +7,8 @@
 from jax.experimental import pallas as pl
 from jax.experimental.pallas import tpu as pltpu
 from jax.sharding import PartitionSpec as P
+import ml_dtypes
+import numpy as np
 
 AXES = ("img", "band")
 SIZES = {"y": 4, "z": 8, "x": 4, "c": 2}
@@ -56,7 +58,98 @@
 
 
 def both(a_ref, b_ref):
-    return jnp.concatenate([a_ref[0], b_ref[0]], axis=0).astype(f32)
+    return jnp.concatenate([a_ref[0], b_ref[0, :128]], axis=0).astype(f32)
+
+
+def turns(at_ref, image, row_ref, col_ref, got, table_ref):
+    here = pl.ds(2 * at_ref[0] + image, 1)
+    hot = []
+    for n, ref in enumerate((row_ref, col_ref)):
+        kept = ref[here, :].astype(f32)
+        pos = jnp.concatenate([kept, got[0:1, n * 128 : n * 128 + 128].astype(f32)], axis=1)
+        spots = lax.broadcasted_iota(jnp.int32, (16, 256), 0).astype(f32)
+        hot.append(jnp.where(spots == pos, 1.0, 0.0))
+    hot = jnp.concatenate(hot, axis=0).astype(bf16)
+    return [dot_tn(hot, table_ref[n]) + dot_tn(hot, table_ref[n + 1]) for n in (0, 2)]
+
+
+def turn_table():
+    lane = np.arange(128)
+    rates = 10000.0 ** (-(lane % 16) / 16)
+    angle = np.arange(16)[:, None] * rates
+    row_lane = (lane % 64) < 32
+    out = []
+    for v in (np.cos(angle), np.sin(angle) * np.where(lane % 32 < 16, -1.0, 1.0)):
+        v = np.concatenate([np.where(row_lane, v, 0.0), np.where(row_lane, 0.0, v)])
+        high = v.astype(ml_dtypes.bfloat16)
+        out += [high, (v - high.astype(np.float64)).astype(ml_dtypes.bfloat16)]
+    return np.stack(out)
+
+
+def pack_kernel(at_ref, lat_ref, dy_ref, row_ref, col_ref, lat_out, dy_out):
+    other = 2 - 2 * at_ref[0]
+    dy_out[...] = dy_ref[...]
+    for i in range(2):
+        lat_out[i, :128] = lat_ref[i]
+        here = pl.ds(other + i, 1)
+        line = jnp.concatenate(
+            [row_ref[here, :].astype(f32), col_ref[here, :].astype(f32), jnp.zeros((1, 128), f32)],
+            axis=1,
+        )
+        lat_out[i, 128:] = jnp.broadcast_to(line, (16, 384)).astype(bf16)
+
+
+def split(v):
+    hi = v.astype(bf16)
+    return jnp.concatenate([hi, (v - hi.astype(f32)).astype(bf16)], axis=0)
+
+
+def fine_dot(v, w):
+    n = v.shape[0]
+    out = dot(split(v), w)
+    return out[:n] + out[n:]
+
+
+def silu(v):
+    return v / (1.0 + jnp.exp(-v))
+
+
+def modulation_kernel(
+    at_ref, t_ref, l_ref, tw1_ref, tw2_ref, row0_ref, row1_ref, modw_ref, mod_ref, extra_ref
+):
+    first = 2 * at_ref[0]
+    freqs = jnp.exp(lane_iota((1, 128)).astype(f32) * (-math.log(10000.0) / 128))
+    spot = lax.broadcasted_iota(jnp.int32, (16, 1), 0)
+    steps = jnp.where(
+        spot == 0,
+        t_ref[first].astype(f32),
+        jnp.where(spot == 1, t_ref[first + 1].astype(f32), 0.0),
+    )
+    angle = steps * freqs
+    emb = jnp.concatenate([jnp.cos(angle), jnp.sin(angle)], axis=1)
+    hidden = silu(fine_dot(emb, tw1_ref[...]))
+    cond = fine_dot(hidden, tw2_ref[...])
+    for i, ref in enumerate((row0_ref, row1_ref)):
+        label = l_ref[first + i]
+        row = jnp.sum(
+            jnp.where(spot == (label & 15), ref[...].astype(f32), 0.0), axis=0, keepdims=True
+        )
+        cond = cond + jnp.where(spot == i, row, 0.0)
+    mod = fine_dot(silu(cond), modw_ref[...])
+    lane = lane_iota((1, 128))
+    codes = jnp.zeros((1, 128), f32)
+    for i in range(2):
+        label = l_ref[first + i]
+        codes = jnp.where(lane == i, (label >> 5).astype(f32), codes)
+        codes = jnp.where(lane == 2 + i, (label & 31).astype(f32), codes)
+        for k in range(6):
+            mod_ref[i, k : k + 1] = mod[i : i + 1, k * 384 : k * 384 + 384]
+        for b in range(2):
+            extra_ref[1 + i * 2 + b : 2 + i * 2 + b] = emb[i : i + 1, b * 128 : b * 128 + 128]
+        for b, p in enumerate(pairs()):
+            extra_ref[5 + i * 3 + b : 6 + i * 3 + b] = cond[i : i + 1, p]
+    extra_ref[0:1] = codes
+    extra_ref[11:] = jnp.zeros((5, 128), f32)
 
 
 def pairs(width=384):
@@ -64,18 +157,34 @@
 
 
 def forward_kernel(
-    at_ref, kept_ref, got_ref, mod_ref, w_ref, gain_ref, cos_ref, sin_ref, q_ref, k_ref, v_ref, att_ref
+    at_ref,
+    kept_ref,
+    got_ref,
+    mod_ref,
+    w_ref,
+    qgain_ref,
+    kgain_ref,
+    row_ref,
+    col_ref,
+    table_ref,
+    q_ref,
+    k_ref,
+    v_ref,
+    att_ref,
 ):
     x = both(kept_ref, got_ref)
     h1 = (x * inv_rms(x) * (1.0 + mod_ref[0, 1:2]) + mod_ref[0, 0:1]).astype(bf16)
     z = dot(h1, w_ref[...])
-    cosine, sine = cos_ref[0], sin_ref[0]
+    cosine, sine = turns(
+        at_ref, pl.program_id(0), row_ref, col_ref, got_ref[0, 128:144], table_ref
+    )
+    gains = [jnp.concatenate([r[...], r[...]], axis=1) for r in (qgain_ref, kgain_ref)]
     masks = head_masks()
     for p in pairs():
         turned = []
         for part in range(2):
             zp = z[:, part * 384 + p.start : part * 384 + p.stop]
-            n = zp * lax.rsqrt(head_mean(zp * zp) + EPS) * gain_ref[part : part + 1]
+            n = zp * lax.rsqrt(head_mean(zp * zp) + EPS) * gains[part]
             turned.append(n * cosine + partner(n) * sine)
         q = (turned[0].astype(bf16).astype(f32) * 0.125).astype(bf16)
         k = turned[1].astype(bf16)
@@ -130,7 +239,7 @@
     def _():
         branch_s[...] = dot(att_ref[...], proj_ref[...])
         for i in images:
-            x = jnp.concatenate([kept_ref[i], got_ref[i]], axis=0).astype(f32)
+            x = jnp.concatenate([kept_ref[i], got_ref[i, :128]], axis=0).astype(f32)
             mid = x + mod_ref[i, 2:3] * branch_s[rows(i)]
             mid_s[rows(i)] = mid
             h2_s[rows(i)] = (mid * inv_rms(mid) * (1.0 + mod_ref[i, 4:5]) + mod_ref[i, 3:4]).astype(
@@ -191,9 +300,11 @@
     got_ref,
     mod_ref,
     w_ref,
-    gain_ref,
-    cos_ref,
-    sin_ref,
+    qgain_ref,
+    kgain_ref,
+    row_ref,
+    col_ref,
+    table_ref,
     q_ref,
     k_ref,
     v_ref,
@@ -225,7 +336,10 @@
     dbranch_s[here] = d_branch
     d_att = dot_nt(d_branch, proj_ref[...]).astype(bf16)
     z = dot(h1, w_ref[:, :768])
-    cosine, sine = cos_ref[0], sin_ref[0]
+    cosine, sine = turns(
+        at_ref, pl.program_id(0), row_ref, col_ref, got_ref[0, 128:144], table_ref
+    )
+    gains = [jnp.concatenate([r[...], r[...]], axis=1) for r in (qgain_ref, kgain_ref)]
     masks = head_masks()
     gain_sums = [None, None]
     for p in pairs():
@@ -248,7 +362,7 @@
             dn = d * cosine - partner(d) * sine
             total = jnp.sum(dn * n, axis=0, keepdims=True)
             gain_sums[part] = total if gain_sums[part] is None else gain_sums[part] + total
-            e = dn * gain_ref[part : part + 1]
+            e = dn * gains[part]
             dz = r * (e - n * head_mean(e * n))
             dqkv_s[here, part * 384 + p.start : part * 384 + p.stop] = dz.astype(bf16)
         dqkv_s[here, 768 + p.start : 768 + p.stop] = dv.astype(bf16)
@@ -257,8 +371,8 @@
     grad = d_mid + s1 * (e1 - n1 * jnp.mean(e1 * n1, axis=-1, keepdims=True))
     grad_ref[0] = grad[:128]
     gradsend_ref[0] = grad[128:].astype(bf16)
-    gains = [g + pltpu.roll(g, 64, 1) for g in gain_sums]
-    gains = jnp.where(lane_iota((1, 128)) < 64, gains[0], gains[1])
+    gain_sums = [g + pltpu.roll(g, 64, 1) for g in gain_sums]
+    gain_sums = jnp.where(lane_iota((1, 128)) < 64, gain_sums[0], gain_sums[1])
 
     def put_sums(at):
         for k, v in enumerate((d_h1, d_h1 * n1)):
@@ -269,12 +383,12 @@
     @pl.when(i == 0)
     def _():
         put_sums(0)
-        gain_s[...] = jnp.broadcast_to(gains, (8, 128))
+        gain_s[...] = jnp.broadcast_to(gain_sums, (8, 128))
 
     @pl.when(i == 1)
     def _():
         put_sums(1)
-        sums_ref[pl.ds(12, 1)] = gain_s[0:1] + gains
+        sums_ref[pl.ds(12, 1)] = gain_s[0:1] + gain_sums
         sums_ref[pl.ds(13, 3)] = jnp.zeros((3, 128), f32)
         h1t = h1_s[...].T
         for part in range(3):
@@ -313,7 +427,51 @@
     return pl.CostEstimate(flops=flops, bytes_accessed=nbytes, transcendentals=0)
 
 
-def forward_call(at, latents, got, mod, qkv_w, gains, cosine, sine):
+def pack_call(at, latents, out_grad, pos_row, pos_col):
+    theirs = pl.BlockSpec((2, 128, 384), lambda j, at: (1 - at[0], 0, 0))
+    shapes = [(2, 144, 384), (2, 128, 384)]
+    return pl.pallas_call(
+        pack_kernel,
+        grid_spec=pltpu.PrefetchScalarGridSpec(
+            num_scalar_prefetch=1,
+            grid=(1,),
+            in_specs=[theirs, theirs, whole_spec((4, 128)), whole_spec((4, 128))],
+            out_specs=[whole_spec(s) for s in shapes],
+        ),
+        out_shape=[shape_of(s, bf16) for s in shapes],
+        compiler_params=params(8),
+        cost_estimate=cost(200_000, 800_000),
+        name="pack_swaps",
+    )(at, latents, out_grad, pos_row, pos_col)
+
+
+def modulation_call(at, timesteps, labels, t_w1, t_w2, label_table, mod_w):
+    def row_spec(i):
+        return pl.BlockSpec((16, 384), lambda j, at, t, l: (l[2 * at[0] + i] >> 4, 0))
+
+    shapes = [(2, 6, 384), (16, 128)]
+    return pl.pallas_call(
+        modulation_kernel,
+        grid_spec=pltpu.PrefetchScalarGridSpec(
+            num_scalar_prefetch=3,
+            grid=(1,),
+            in_specs=[
+                whole_spec((256, 384)),
+                whole_spec((384, 384)),
+                row_spec(0),
+                row_spec(1),
+                whole_spec((384, 2304)),
+            ],
+            out_specs=[whole_spec(s) for s in shapes],
+        ),
+        out_shape=[shape_of(s, f32) for s in shapes],
+        compiler_params=params(16),
+        cost_estimate=cost(1_000_000_000, 3_000_000),
+        name="modulation",
+    )(at, timesteps, labels, t_w1, t_w2, label_table, label_table, mod_w)
+
+
+def forward_call(at, latents, got, mod, qkv_w, *rest):
     act = shape_of((2, 256, 384), bf16)
     return pl.pallas_call(
         forward_kernel,
@@ -322,20 +480,22 @@
             grid=(2,),
             in_specs=[
                 KEPT,
-                image_spec((128, 384)),
+                image_spec((144, 384)),
                 image_spec((6, 384)),
                 whole_spec((384, 1152)),
-                whole_spec((2, 128)),
-                image_spec((256, 128)),
-                image_spec((256, 128)),
+                whole_spec((1, 64)),
+                whole_spec((1, 64)),
+                whole_spec((4, 128)),
+                whole_spec((4, 128)),
+                whole_spec((4, 32, 128)),
             ],
             out_specs=[image_spec((256, 384))] * 4,
         ),
         out_shape=[act] * 4,
-        compiler_params=params(40),
+        compiler_params=params(12),
         cost_estimate=cost(3_000_000_000, 4_000_000),
         name="attention_forward",
-    )(at, latents, got, mod, qkv_w, gains, cosine, sine)
+    )(at, latents, got, mod, qkv_w, *rest)
 
 
 def mlp_call(at, latents, got, out_grad, dgot, att, mod, proj_w, gate_up_w, down_w):
@@ -346,7 +506,7 @@
             grid=(4,),
             in_specs=[
                 KEPT2,
-                whole_spec((2, 128, 384)),
+                whole_spec((2, 144, 384)),
                 KEPT2,
                 whole_spec((2, 128, 384)),
                 whole_spec((512, 384)),
@@ -383,13 +543,13 @@
             shape_of((512, 384), f32),
             shape_of((24, 128), f32),
         ],
-        compiler_params=params(48),
+        compiler_params=params(16),
         cost_estimate=cost(6_000_000_000, 8_000_000),
         name="mlp_both_ways",
     )(at, latents, got, out_grad, dgot, att, mod, proj_w, gate_up_w, gate_up_w, down_w)
 
 
-def backward_call(at, latents, got, mod, qkv_w, gains, cosine, sine, q, k, v, att, d_mid, proj_w):
+def backward_call(at, latents, got, mod, qkv_w, *rest):
     return pl.pallas_call(
         backward_kernel,
         grid_spec=pltpu.PrefetchScalarGridSpec(
@@ -397,12 +557,14 @@
             grid=(2,),
             in_specs=[
                 KEPT,
-                image_spec((128, 384)),
+                image_spec((144, 384)),
                 image_spec((6, 384)),
                 whole_spec((384, 1152)),
-                whole_spec((2, 128)),
-                image_spec((256, 128)),
-                image_spec((256, 128)),
+                whole_spec((1, 64)),
+                whole_spec((1, 64)),
+                whole_spec((4, 128)),
+                whole_spec((4, 128)),
+                whole_spec((4, 32, 128)),
             ]
             + [image_spec((256, 384))] * 4
             + [pl.BlockSpec((256, 384), lambda i, at: (i, 0)), whole_spec((384, 384))],
@@ -429,37 +591,33 @@
             shape_of((2, 128, 384), bf16),
             shape_of((16, 128), f32),
         ],
-        compiler_params=params(48),
+        compiler_params=params(20),
         cost_estimate=cost(5_000_000_000, 6_000_000),
         name="attention_backward",
-    )(at, latents, got, mod, qkv_w, gains, cosine, sine, q, k, v, att, d_mid, proj_w)
-
-
-def turn_tables(pos):
-    lane = jnp.arange(128)
-    rates = 10000.0 ** (-(lane % 16).astype(f32) / 16)
-    where_row = (lane % 64) < 32
-    pos = pos.astype(f32)
-    angle = jnp.where(where_row, pos[..., 0:1], pos[..., 1:2]) * rates
-    sign = jnp.where(lane % 32 < 16, -1.0, 1.0)
-    return jnp.cos(angle), jnp.sin(angle) * sign
-
-
-def join_kernel(a_ref, a_got_ref, b_ref, b_got_ref, extra_ref, out_ref):
+    )(at, latents, got, mod, qkv_w, *rest)
+
+
+def join_kernel(
+    a_ref, a_got_ref, b_ref, b_got_ref, sums1_ref, sums2_ref, extra_ref, out_ref, lines
+):
+    lines[:24] = sums1_ref[...]
+    lines[24:40] = sums2_ref[...]
+    lines[37:48] = extra_ref[:11]
     out_ref[:, :288] = (a_ref[...].astype(f32) + a_got_ref[...].astype(f32)).astype(bf16)
     out_ref[:, 288:432] = (b_ref[...].astype(f32) + b_got_ref[...].astype(f32)).astype(bf16)
-    out_ref[:, 432:] = jnp.broadcast_to(extra_ref[...][None], (16, 48, 128))
-
-
-def join_call(keep1, got1, keep2, got2, extra):
+    out_ref[:, 432:] = jnp.broadcast_to(lines[...].astype(bf16)[None], (16, 48, 128))
+
+
+def join_call(keep1, got1, keep2, got2, *lines):
     big, small = (16, 288, 128), (16, 144, 128)
     return pl.pallas_call(
         join_kernel,
         out_shape=shape_of((16, 480, 128), bf16),
-        compiler_params=params(32),
+        scratch_shapes=[pltpu.VMEM((48, 128), f32)],
+        compiler_params=params(14),
         cost_estimate=cost(2_000_000, 6_000_000),
         name="join_messages",
-    )(keep1.reshape(big), got1.reshape(big), keep2.reshape(small), got2.reshape(small), extra)
+    )(keep1.reshape(big), got1.reshape(big), keep2.reshape(small), got2.reshape(small), *lines)
 
 
 def sum_kernel(a_ref, out_ref, extra_ref):
@@ -475,7 +633,7 @@
     return pl.pallas_call(
         sum_kernel,
         out_shape=[shape_of((448, 128), bf16), shape_of((16, 48, 128), bf16)],
-        compiler_params=params(32),
+        compiler_params=params(14),
         cost_estimate=cost(2_000_000, 3_000_000),
         name="sum_xy",
     )(a)
@@ -579,8 +737,8 @@
             ],
         ),
         out_shape=[shape_of(s, f32) for s in shapes],
-        compiler_params=params(56),
-        cost_estimate=cost(4_000_000_000, 12_000_000),
+        compiler_params=params(36),
+        cost_estimate=cost(100_000_000, 100_000),
         name="condition_gradients",
     )(at, own, got, t_w1, t_w2, mod_w)
 
@@ -658,7 +816,7 @@
         out_shape=[
             shape_of(s, f32) for s in ((384, 1152), (384, 384), (384, 2048), (1024, 384))
         ],
-        compiler_params=params(32),
+        compiler_params=params(14),
         cost_estimate=cost(2_000_000, 11_000_000),
         name="unpack_sums",
     )(at, own, got)
@@ -699,23 +857,6 @@
 
 def core_swap(v):
     return lax.ppermute(v, AXES, CORE_SWAP)
-
-
-def silu(v):
-    return v / (1.0 + jnp.exp(-v))
-
-
-def condition(t_w1, t_w2, label_table, mod_w, tsteps, labs):
-    high = lax.Precision.HIGHEST
-    freqs = jnp.exp(-math.log(10000.0) * jnp.arange(128, dtype=f32) / 128)
-    angle = tsteps.astype(f32)[:, None] * freqs[None, :]
-    emb = jnp.concatenate([jnp.cos(angle), jnp.sin(angle)], axis=-1)
-    hidden = jax.nn.silu(jnp.dot(emb, t_w1.astype(f32), precision=high))
-    hot = (labs[:, None] == jnp.arange(label_table.shape[0], dtype=jnp.int32)[None, :]).astype(f32)
-    cond = jnp.dot(hidden, t_w2.astype(f32), precision=high) + jnp.dot(
-        hot, label_table.astype(f32), precision=high
-    )
-    return emb, cond, jnp.dot(jax.nn.silu(cond), mod_w.astype(f32), precision=high)
 
 
 def body(
@@ -739,58 +880,39 @@
     band = lax.axis_index("band")
     core = lax.axis_index("img") % 2
     at = jnp.stack([band, core]).astype(jnp.int32)
-    mine = 2 * band
-    other = 2 - mine
-
-    def theirs(v):
-        return lax.dynamic_slice_in_dim(v, other, 2, 0)
-
-    def ours(v):
-        return lax.dynamic_slice_in_dim(v, mine, 2, 0)
-
-    got = swap(theirs(latents))
-    pos = jnp.stack([pos_row, pos_col], axis=-1)
-    pos = jnp.concatenate([ours(pos), swap(theirs(pos))], axis=1)
-    dgot = swap(theirs(out_grad))
-    tsteps, labs = ours(timesteps), ours(labels)
-    emb, cond, mod = condition(t_w1, t_w2, label_table, mod_w, tsteps, labs)
-    mod = mod.reshape(2, 6, 384)
-    gains = jnp.stack([jnp.tile(q_gain, 2), jnp.tile(k_gain, 2)])
-    cosine, sine = turn_tables(pos)
-    q, k, v, att = forward_call(at, latents, got, mod, qkv_w, gains, cosine, sine)
+    send, dsend = pack_call(at, latents, out_grad, pos_row, pos_col)
+    got, dgot = swap(send), swap(dsend)
+    mod, extra = modulation_call(at, timesteps, labels, t_w1, t_w2, label_table, mod_w)
+    turn = (q_gain.reshape(1, 64), k_gain.reshape(1, 64), pos_row, pos_col, turn_table())
+    q, k, v, att = forward_call(at, latents, got, mod, qkv_w, *turn)
     keep1, send1, block_out, out_send, d_mid, sums1 = mlp_call(
         at, latents, got, out_grad, dgot, att.reshape(512, 384), mod, proj_w, gate_up_w, down_w
     )
     got1 = core_swap(send1)
+    out_got = swap(out_send)
     keep2, send2, latents_grad, grad_send, sums2 = backward_call(
-        at, latents, got, mod, qkv_w, gains, cosine, sine, q, k, v, att, d_mid, proj_w
+        at, latents, got, mod, qkv_w, *turn, q, k, v, att, d_mid, proj_w
     )
-    codes = jnp.concatenate([labs // 32, labs % 32]).astype(f32)
-    codes = jnp.pad(codes[None], ((0, 0), (0, 124)))
-    extra = jnp.concatenate(
-        [sums1, sums2[:13], codes, emb.reshape(4, 128), cond.reshape(6, 128)]
-    ).astype(bf16)
+    send2, out_got = lax.optimization_barrier((send2, out_got))
     chunk, extra = sum_call(
-        exchange(join_call(keep1, got1, keep2, core_swap(send2), extra), "xy")
+        exchange(join_call(keep1, got1, keep2, core_swap(send2), sums1, sums2, extra), "xy")
     )
     extra = lax.all_gather(
         extra.reshape(768, 128), AXES, axis=0, tiled=True, axis_index_groups=groups("z")
     )
     chunk = jnp.sum(exchange(chunk.reshape(8, 56, 128), "z").astype(f32), axis=0).astype(bf16)
     chunk = gather(chunk, "z").reshape(448, 128)
-    chunk, extra = lax.optimization_barrier((chunk, extra))
-    summed = gather(chunk, "xy")
+    chunk, grad_got = lax.optimization_barrier((chunk, swap(grad_send)))
+    wide = lax.optimization_barrier(jnp.broadcast_to(chunk[None], (16, 448, 128)))
+    summed = exchange(wide, "xy")
+    extra, _ = lax.optimization_barrier((extra, wide))
     conditioned = condition_call(at, extra, core_swap(extra), t_w1, t_w2, mod_w)
-    out_got, grad_got = swap(out_send), swap(grad_send)
-    summed, conditioned, out_got, grad_got = lax.optimization_barrier(
-        (summed, conditioned, out_got, grad_got)
-    )
+    summed, conditioned = lax.optimization_barrier((summed, conditioned))
     tw1_grad, tw2_grad, table_grad, modw_grad, gain_sums = conditioned
     qkv_sum, proj_sum, gu_sum, down_sum = unpack_call(at, summed, core_swap(summed))
+    other = 2 - 2 * band
     block_out = lax.dynamic_update_slice_in_dim(block_out, out_got, other, 0)
-    latents_grad = lax.dynamic_update_slice_in_dim(
-        latents_grad, grad_got.astype(f32), other, 0
-    )
+    latents_grad = lax.dynamic_update_slice_in_dim(latents_grad, grad_got.astype(f32), other, 0)
     return (
         block_out,
         latents_grad,

time: 199 us -> 165 us (0.83)
  waiting for transfers between devices: 32.3 us -> 18.7 us
  blocking collectives: 56.7 us -> 46.5 us
  other arithmetic: 6.24 us -> 0.13 us
  matrix products: 5.55 us -> 0 us
  starting transfers between devices: 22.6 us -> 26.3 us
    ppermute x5 -> x4, waiting for transfers between devices: 18.7 us -> 5.04 us  [swap(): return lax.ppermute(v, AXES, BAND_SWAP)]
    all_to_all x3 -> x2, blocking collectives: 56.7 us -> 46.5 us  [exchange(): lax.all_to_all(v, AXES, 0, 0, tiled=True, axis_index_groups=groups(axes))]
    all_gather x1, waiting for transfers between devices: 12.9 us -> 3.85 us  [body(): lax.all_gather(extra.reshape(768, 128), AXES, axis=0, tiled=True, axis_in...]
    ppermute x4, starting transfers between devices: 6.04 us -> 13.1 us  [core_swap(): return lax.ppermute(v, AXES, CORE_SWAP)]
    ppermute x4, waiting for transfers between devices: 0.64 us -> 7.09 us  [core_swap(): return lax.ppermute(v, AXES, CORE_SWAP)]
    dot_general x4 -> x0, matrix products: 5.55 us -> none  [the longest x1 2.28 us: condition(): jnp.dot(jax.nn.silu(cond), mod_w.astype(f32), precision=high)]
    unnamed x54, local copies, waits for them, and re-layouts: 7.64 us -> 12.1 us
    ppermute x5 -> x4, starting transfers between devices: 10.1 us -> 5.89 us  [swap(): return lax.ppermute(v, AXES, BAND_SWAP)]
  transfers between devices with their start and end apart: 11 -> 11, of which waited for: 4 -> 6; matrix products, arithmetic and copies ran while one was open for 10% -> 2% of each run, Pallas kernels for 14% -> 15%
where the time goes in v1:
time: 165 us; the launch traced here: 164 us
  blocking collectives  46.5 us (28%)
  Pallas kernels  42.2 us (26%)
  starting transfers between devices  26.3 us (16%)
  waiting for transfers between devices  18.7 us (11%)
  local copies, waits for them, and re-layouts  15.7 us (10%)
  between operations  14.3 us (9%)
    all_to_all x2, blocking collectives, exchange(): lax.all_to_all(v, AXES, 0, 0, tiled=True, axis_index_groups=groups(axes))  46.5 us
    ppermute x4, starting transfers between devices, core_swap(): return lax.ppermute(v, AXES, CORE_SWAP)  13.1 us
    unnamed x54, local copies, waits for them, and re-layouts  12.1 us
    pallas_call x1, Pallas kernels, backward_call(): pl.pallas_call(backward_kernel, grid_spec=pltpu.PrefetchScalarGridSpec(nu...  10 us
    pallas_call x1, Pallas kernels, mlp_call(): pl.pallas_call(mlp_kernel, grid_spec=pltpu.PrefetchScalarGridSpec(num_sca...  8.6 us
    pallas_call x1, Pallas kernels, condition_call(): pl.pallas_call(condition_kernel, grid_spec=pltpu.PrefetchScalarGridSpec(n...  7.67 us
    all_to_all x2, starting transfers between devices, exchange(): lax.all_to_all(v, AXES, 0, 0, tiled=True, axis_index_groups=groups(axes))  7.21 us
    ppermute x4, waiting for transfers between devices, core_swap(): return lax.ppermute(v, AXES, CORE_SWAP)  7.09 us
  transfers between devices with their start and end apart: 11, of which 6 were waited for; matrix products, arithmetic and copies ran while one was open for 2% of the time, Pallas kernels for 15%

profile of v1, /device:TPU:1, one launch (start us, length us, event | category | flops | bytes accessed | tf_op | source)
XLA Modules:
  0.0 164.0 jit_solution(10305073650867791886)
XLA Ops:
  11.3 3.7 %collective-permute-start = (bf16[2,144,384]{2,1,0:T(8,128)(2,1)S(1)}, bf16[2,144,384]{2,1,0:T(8,128)(2,1)S(1)}, u32[]{:S(2)}, u32[]{:S(2)}) collective-permute-start(bf16[2,144,384]{2,1,0:T(8,128)(2,1)S(1)} %get-tuple-element.53), channel_id=1, source_target_pairs={{0,1},{1,0},{2,3},{3,2},{4,5},{5,4},{6,7},{7,6},{8,9},{9,8},{10,11... | collective-permute-start | bytes 663560 | tf_op jit(solution)/shard_map/ppermute | solution.py:855
  15.0 1.5 copy-done
  20.9 1.3 modulation.1
  22.3 5.7 %attention_forward.1 = (bf16[2,256,384]{2,1,0:T(8,128)(2,1)S(1)}, bf16[2,256,384]{2,1,0:T(8,128)(2,1)S(1)}, bf16[2,256,384]{2,1,0:T(8,128)(2,1)S(1)}, bf16[2,256,384]{2,1,0:T(8,128)(2,1)S(1)}) custom-call(s32[2]{0:T(128)S(1)} %pad_add_fusion.at_ref, bf16[4,128,384]{2,1,0:T(8,128)(2,1)S(1)} %copy-done.11, ...), custom_call_target="tpu_custom_call" | custom-call | flops 3000000000 | bytes 4000000 | tf_op jit(solution)/shard_map/attention_forward/pallas_call | solution.py:476
  28.0 8.6 %mlp_both_ways.1 = (bf16[4608,128]{1,0:T(8,128)(2,1)S(1)}, bf16[4608,128]{1,0:T(8,128)(2,1)S(1)}, bf16[4,128,384]{2,1,0:T(8,128)(2,1)}, bf16[2,128,384]{2,1,0:T(...) custom-call(s32[2]{0:T(128)S(1)} %pad_add_fusion.at_ref, bf16[4,128,384]{2,1,0:T(8,128)(2,1)S(1)} %copy-done.11, ...), custom_call_target="tpu_custom_call" | custom-call | flops 6000000000 | bytes 8000000 | tf_op jit(solution)/shard_map/mlp_both_ways/pallas_call | solution.py:502
  36.6 3.1 %collective-permute-start.3 = (bf16[4608,128]{1,0:T(8,128)(2,1)S(1)}, bf16[4608,128]{1,0:T(8,128)(2,1)S(1)}, u32[]{:S(2)}, u32[]{:S(2)}) collective-permute-start(bf16[4608,128]{1,0:T(8,128)(2,1)S(1)} %get-tuple-element.67), channel_id=1, source_target_pairs={{0,2},{1,3},{2,0},{3,1},{4,6},{5,7},{6,4},{7,5},{8,10},{9,11},{10,... | collective-permute-start | bytes 3538952 | tf_op jit(solution)/shard_map/ppermute | solution.py:859
  40.7 10.0 %attention_backward.1 = (bf16[2304,128]{1,0:T(8,128)(2,1)S(1)}, bf16[2304,128]{1,0:T(8,128)(2,1)S(1)}, f32[4,128,384]{2,1,0:T(8,128)}, bf16[2,128,384]{2,1,0:T(8,128)(2,1)S(1)}, f32[16,128]{1,0:T(8,128)S(1)}) custom-call(s32[2]{0:T(128)S(1)} %pad_add_fusion.at_ref, bf16[4,128,384]{2,1,0:T(8,128)(2,1)S(1)} %copy-done.11, ...), custom_call_target="tpu_custom_call" | custom-call | flops 5000000000 | bytes 6000000 | tf_op jit(solution)/shard_map/attention_backward/pallas_call | solution.py:553
  51.0 1.7 %collective-permute-done.4 = bf16[2304,128]{1,0:T(8,128)(2,1)S(1)} collective-permute-done((bf16[2304,128]{1,0:T(8,128)(2,1)S(1)}, bf16[2304,128]{1,0:T(8,128)(2,1)S(1)}, u32[]{:S(2)}, u32[]{:S(2)}) %collective-permute-start.4) | collective-permute-done | bytes 589856 | tf_op jit(solution)/shard_map/ppermute | solution.py:859
  53.7 30.7 %all_to_all.20.a_ref = bf16[16,480,128]{2,1,0:T(8,128)(2,1)S(1)} all-to-all(bf16[16,480,128]{2,1,0:T(8,128)(2,1)S(1)} %join_messages.1), channel_id=1, replica_groups={{0,64,128,192,4,68,132,196,1,65,129,193,5,69,133,197},{2,66,130,194,6,7..., dimensions={0} | all-to-all | bytes 3932160 | tf_op jit(solution)/shard_map/all_to_all | solution.py:842
  85.1 15.9 %all_to_all.21 = bf16[8,56,128]{2,1,0:T(8,128)(2,1)S(1)} all-to-all(bf16[8,56,128]{2,1,0:T(8,128)(2,1)S(1)} %bitcast.20), channel_id=1, replica_groups={{0,8,16,24,32,40,48,56},{2,10,18,26,34,42,50,58},{4,12,20,28,36,44,52,6..., dimensions={0} | all-to-all | bytes 229376 | tf_op jit(solution)/shard_map/all_to_all | solution.py:842
  101.7 3.4 %all-to-all-start.2 = ((bf16[8,56,128]{2,1,0:T(8,128)(2,1)}), bf16[8,56,128]{2,1,0:T(8,128)(2,1)S(1)}, u32[]{:S(2)}, u32[]{:S(2)}) async-start(bf16[8,56,128]{2,1,0:T(8,128)(2,1)} %broadcast_in_dim.4), calls=%async_computation.2 | async-start | bytes 229376 | tf_op jit(solution)/shard_map/all_to_all | solution.py:842
  106.2 5.0 %collective-permute-done.5 = bf16[2,128,384]{2,1,0:T(8,128)(2,1)S(1)} collective-permute-done((bf16[2,128,384]{2,1,0:T(8,128)(2,1)S(1)}, bf16[2,128,384]{2,1,0:T(8,128)(2,1)S(1)}, u32[]{:S(2)}, u32[]{:S(2)}) %collective-permute-start.5) | collective-permute-done | bytes 196640 | tf_op jit(solution)/shard_map/ppermute | solution.py:855
  111.2 2.7 %all-to-all-done.2 = bf16[8,56,128]{2,1,0:T(8,128)(2,1)S(1)} async-done(((bf16[8,56,128]{2,1,0:T(8,128)(2,1)}), bf16[8,56,128]{2,1,0:T(8,128)(2,1)S(1)}, u32[]{:S(2)}, u32[]{:S(2)}) %all-to-all-start.2) | async-done | bytes 114720 | tf_op jit(solution)/shard_map/all_to_all | solution.py:842
  113.9 1.6 broadcast_in_dim.5
  115.5 3.8 %all-to-all-start.3 = ((bf16[16,448,128]{2,1,0:T(8,128)(2,1)}), bf16[16,448,128]{2,1,0:T(8,128)(2,1)S(1)}, u32[]{:S(2)}, u32[]{:S(2)}) async-start(bf16[16,448,128]{2,1,0:T(8,128)(2,1)} %broadcast_in_dim.5), calls=%async_computation.3 | async-start | bytes 3670016 | tf_op jit(solution)/shard_map/all_to_all | solution.py:842
  119.4 3.8 %all-gather.2.cloned.1.call-done.own_ref = bf16[6144,128]{1,0:T(8,128)(2,1)} async-done(((bf16[768,128]{1,0:T(8,128)(2,1)}), bf16[6144,128]{1,0:T(8,128)(2,1)}) %all-gather.2.cloned.1.call-update) | async-done | bytes 1572880 | tf_op jit(solution)/shard_map/all_gather | solution.py:900
  123.2 4.3 %collective-permute-start.6 = (bf16[6144,128]{1,0:T(8,128)(2,1)}, bf16[6144,128]{1,0:T(8,128)(2,1)S(1)}, u32[]{:S(2)}, u32[]{:S(2)}) collective-permute-start(bf16[6144,128]{1,0:T(8,128)(2,1)} %all-gather.2.cloned.1.call-done.own_ref), channel_id=1, source_target_pairs={{0,2},{1,3},{2,0},{3,1},{4,6},{5,7},{6,4},{7,5},{8,10},{9,11},{10,... | collective-permute-start | bytes 4718600 | tf_op jit(solution)/shard_map/ppermute | solution.py:859
  127.5 3.2 %collective-permute-done.6.got_ref = bf16[6144,128]{1,0:T(8,128)(2,1)S(1)} collective-permute-done((bf16[6144,128]{1,0:T(8,128)(2,1)}, bf16[6144,128]{1,0:T(8,128)(2,1)S(1)}, u32[]{:S(2)}, u32[]{:S(2)}) %collective-permute-start.6) | collective-permute-done | bytes 1572896 | tf_op jit(solution)/shard_map/ppermute | solution.py:859
  130.8 1.5 copy-done.1
  132.2 1.4 copy-done.3
  133.6 7.7 %condition_gradients.1 = (f32[256,384]{1,0:T(8,128)}, f32[384,384]{1,0:T(8,128)}, f32[1001,384]{1,0:T(8,128)}, f32[384,2304]{1,0:T(8,128)}, f32[1,128]{1,0:T(1,128)S(1)}) custom-call(s32[2]{0:T(128)S(1)} %pad_add_fusion.at_ref, bf16[6144,128]{1,0:T(8,128)(2,1)S(1)} %copy-done.3, bf16[6144,128]{1,0:T(8,128)(2,1)S(1)} %collective-permute-done.6.got_ref, ...), custom_call_target="tpu_custom_call" | custom-call | flops 100000000 | bytes 100000 | tf_op jit(solution)/shard_map/condition_gradients/pallas_call | solution.py:722
  141.3 5.5 %collective-permute-start.7 = (bf16[16,448,128]{2,1,0:T(8,128)(2,1)S(1)}, bf16[16,448,128]{2,1,0:T(8,128)(2,1)}, u32[]{:S(2)}, u32[]{:S(2)}) collective-permute-start(bf16[16,448,128]{2,1,0:T(8,128)(2,1)S(1)} %all-to-all-done.3.own_ref), channel_id=1, source_target_pairs={{0,2},{1,3},{2,0},{3,1},{4,6},{5,7},{6,4},{7,5},{8,10},{9,11},{10,... | collective-permute-start | bytes 5505032 | tf_op jit(solution)/shard_map/ppermute | solution.py:859
  148.2 2.1 %collective-permute-done.7.got_ref = bf16[16,448,128]{2,1,0:T(8,128)(2,1)} collective-permute-done((bf16[16,448,128]{2,1,0:T(8,128)(2,1)S(1)}, bf16[16,448,128]{2,1,0:T(8,128)(2,1)}, u32[]{:S(2)}, u32[]{:S(2)}) %collective-permute-start.7) | collective-permute-done | bytes 1835040 | tf_op jit(solution)/shard_map/ppermute | solution.py:859
  150.4 6.7 %unpack_sums.1 = (f32[384,1152]{1,0:T(8,128)}, f32[384,384]{1,0:T(8,128)}, f32[384,2048]{1,0:T(8,128)}, f32[1024,384]{1,0:T(8,128)}) custom-call(s32[2]{0:T(128)S(1)} %pad_add_fusion.at_ref, bf16[16,448,128]{2,1,0:T(8,128)(2,1)S(1)} %all-to-all-done.3.own_ref, bf16[16,448,128]{2,1,0:T(8,128)(2,1)} %collective-permute-done.7.got_ref), custom_call_target="tpu_custom_call" | custom-call | flops 2000000 | bytes 11000000 | tf_op jit(solution)/shard_map/unpack_sums/pallas_call | solution.py:799
  (71 shorter events, 14.7 us)
Async XLA Ops:
  7.2 116.1 %all-gather.2.cloned.1.call-start = ((), (), s32[]{:S(2)}) async-start(), calls=%async_computation.4 | async-start | bytes 1769472 | tf_op jit(solution)/shard_map/all_gather | solution.py:900
  11.3 10.9 %collective-permute-start = (bf16[2,144,384]{2,1,0:T(8,128)(2,1)S(1)}, bf16[2,144,384]{2,1,0:T(8,128)(2,1)S(1)}, u32[]{:S(2)}, u32[]{:S(2)}) collective-permute-start(bf16[2,144,384]{2,1,0:T(8,128)(2,1)S(1)} %get-tuple-element.53), channel_id=1, source_target_pairs={{0,1},{1,0},{2,3},{3,2},{4,5},{5,4},{6,7},{7,6},{8,9},{9,8},{10,11... | collective-permute-start | bytes 663560 | tf_op jit(solution)/shard_map/ppermute | solution.py:855
  14.9 13.1 %collective-permute-start.1 = (bf16[2,128,384]{2,1,0:T(8,128)(2,1)S(1)}, bf16[2,128,384]{2,1,0:T(8,128)(2,1)S(1)}, u32[]{:S(2)}, u32[]{:S(2)}) collective-permute-start(bf16[2,128,384]{2,1,0:T(8,128)(2,1)S(1)} %get-tuple-element.54), channel_id=1, source_target_pairs={{0,1},{1,0},{2,3},{3,2},{4,5},{5,4},{6,7},{7,6},{8,9},{9,8},{10,11... | collective-permute-start | bytes 589832 | tf_op jit(solution)/shard_map/ppermute | solution.py:855
  15.0 1.5 copy-start
  20.8 1.4 copy-start.22
  20.8 1.4 copy-start.23
  22.3 5.7 %copy-start.9 = (bf16[4,128,384]{2,1,0:T(8,128)(2,1)S(1)}, bf16[4,128,384]{2,1,0:T(8,128)(2,1)}, u32[]{:S(2)}) copy-start(bf16[4,128,384]{2,1,0:T(8,128)(2,1)} %dkept_ref.1) | copy-start | bytes 1179652
  22.3 5.7 %copy-start.18 = (bf16[384,2048]{1,0:T(8,128)(2,1)S(1)}, bf16[384,2048]{1,0:T(8,128)(2,1)}, u32[]{:S(2)}) copy-start(bf16[384,2048]{1,0:T(8,128)(2,1)} %wu_ref.1) | copy-start | bytes 4718596
  22.3 5.7 %copy-start.20 = (bf16[1024,384]{1,0:T(8,128)(2,1)S(1)}, bf16[1024,384]{1,0:T(8,128)(2,1)}, u32[]{:S(2)}) copy-start(bf16[1024,384]{1,0:T(8,128)(2,1)} %wd_ref.1) | copy-start | bytes 2359300
  22.3 5.7 %copy-start.21 = (bf16[384,384]{1,0:T(8,128)(2,1)S(1)}, bf16[384,384]{1,0:T(8,128)(2,1)}, u32[]{:S(2)}) copy-start(bf16[384,384]{1,0:T(8,128)(2,1)} %proj_ref.3) | copy-start | bytes 884740
  36.6 16.1 %collective-permute-start.3 = (bf16[4608,128]{1,0:T(8,128)(2,1)S(1)}, bf16[4608,128]{1,0:T(8,128)(2,1)S(1)}, u32[]{:S(2)}, u32[]{:S(2)}) collective-permute-start(bf16[4608,128]{1,0:T(8,128)(2,1)S(1)} %get-tuple-element.67), channel_id=1, source_target_pairs={{0,2},{1,3},{2,0},{3,1},{4,6},{5,7},{6,4},{7,5},{8,10},{9,11},{10,... | collective-permute-start | bytes 3538952 | tf_op jit(solution)/shard_map/ppermute | solution.py:859
  39.7 11.0 %collective-permute-start.2 = (bf16[2,128,384]{2,1,0:T(8,128)(2,1)S(1)}, bf16[2,128,384]{2,1,0:T(8,128)(2,1)S(1)}, u32[]{:S(2)}, u32[]{:S(2)}) collective-permute-start(bf16[2,128,384]{2,1,0:T(8,128)(2,1)S(1)} %get-tuple-element.63), channel_id=1, source_target_pairs={{0,1},{1,0},{2,3},{3,2},{4,5},{5,4},{6,7},{7,6},{8,9},{9,8},{10,11... | collective-permute-start | bytes 589832 | tf_op jit(solution)/shard_map/ppermute | solution.py:855
  50.8 2.0 %collective-permute-start.4 = (bf16[2304,128]{1,0:T(8,128)(2,1)S(1)}, bf16[2304,128]{1,0:T(8,128)(2,1)S(1)}, u32[]{:S(2)}, u32[]{:S(2)}) collective-permute-start(bf16[2304,128]{1,0:T(8,128)(2,1)S(1)} %get-tuple-element.69), channel_id=1, source_target_pairs={{0,2},{1,3},{2,0},{3,1},{4,6},{5,7},{6,4},{7,5},{8,10},{9,11},{10,... | collective-permute-start | bytes 1769480 | tf_op jit(solution)/shard_map/ppermute | solution.py:859
  101.7 12.3 %all-to-all-start.2 = ((bf16[8,56,128]{2,1,0:T(8,128)(2,1)}), bf16[8,56,128]{2,1,0:T(8,128)(2,1)S(1)}, u32[]{:S(2)}, u32[]{:S(2)}) async-start(bf16[8,56,128]{2,1,0:T(8,128)(2,1)} %broadcast_in_dim.4), calls=%async_computation.2 | async-start | bytes 229376 | tf_op jit(solution)/shard_map/all_to_all | solution.py:842
  105.0 6.2 %collective-permute-start.5 = (bf16[2,128,384]{2,1,0:T(8,128)(2,1)S(1)}, bf16[2,128,384]{2,1,0:T(8,128)(2,1)S(1)}, u32[]{:S(2)}, u32[]{:S(2)}) collective-permute-start(bf16[2,128,384]{2,1,0:T(8,128)(2,1)S(1)} %get-tuple-element.74), channel_id=1, source_target_pairs={{0,1},{1,0},{2,3},{3,2},{4,5},{5,4},{6,7},{7,6},{8,9},{9,8},{10,11... | collective-permute-start | bytes 589832 | tf_op jit(solution)/shard_map/ppermute | solution.py:855
  115.5 15.2 %copy-start.5 = (bf16[384,384]{1,0:T(8,128)(2,1)S(1)}, bf16[384,384]{1,0:T(8,128)(2,1)}, u32[]{:S(2)}) copy-start(bf16[384,384]{1,0:T(8,128)(2,1)} %tw2_ref.3) | copy-start | bytes 884740
  115.5 15.2 %copy-start.7 = (bf16[256,384]{1,0:T(8,128)(2,1)S(1)}, bf16[256,384]{1,0:T(8,128)(2,1)}, u32[]{:S(2)}) copy-start(bf16[256,384]{1,0:T(8,128)(2,1)} %tw1_ref.3) | copy-start | bytes 589828
  115.5 32.0 %copy-start.25 = (f32[4,128,384]{2,1,0:T(8,128)S(1)}, f32[4,128,384]{2,1,0:T(8,128)}, u32[]{:S(2)}) copy-start(f32[4,128,384]{2,1,0:T(8,128)} %get-tuple-element.65) | copy-start | bytes 2359300
  115.5 25.8 %all-to-all-start.3 = ((bf16[16,448,128]{2,1,0:T(8,128)(2,1)}), bf16[16,448,128]{2,1,0:T(8,128)(2,1)S(1)}, u32[]{:S(2)}, u32[]{:S(2)}) async-start(bf16[16,448,128]{2,1,0:T(8,128)(2,1)} %broadcast_in_dim.5), calls=%async_computation.3 | async-start | bytes 3670016 | tf_op jit(solution)/shard_map/all_to_all | solution.py:842
  123.2 7.5 %collective-permute-start.6 = (bf16[6144,128]{1,0:T(8,128)(2,1)}, bf16[6144,128]{1,0:T(8,128)(2,1)S(1)}, u32[]{:S(2)}, u32[]{:S(2)}) collective-permute-start(bf16[6144,128]{1,0:T(8,128)(2,1)} %all-gather.2.cloned.1.call-done.own_ref), channel_id=1, source_target_pairs={{0,2},{1,3},{2,0},{3,1},{4,6},{5,7},{6,4},{7,5},{8,10},{9,11},{10,... | collective-permute-start | bytes 4718600 | tf_op jit(solution)/shard_map/ppermute | solution.py:859
  130.7 1.5 copy-start.1
  132.2 1.4 copy-start.3
  141.3 9.0 %collective-permute-start.7 = (bf16[16,448,128]{2,1,0:T(8,128)(2,1)S(1)}, bf16[16,448,128]{2,1,0:T(8,128)(2,1)}, u32[]{:S(2)}, u32[]{:S(2)}) collective-permute-start(bf16[16,448,128]{2,1,0:T(8,128)(2,1)S(1)} %all-to-all-done.3.own_ref), channel_id=1, source_target_pairs={{0,2},{1,3},{2,0},{3,1},{4,6},{5,7},{6,4},{7,5},{8,10},{9,11},{10,... | collective-permute-start | bytes 5505032 | tf_op jit(solution)/shard_map/ppermute | solution.py:859
  147.6 9.5 %copy-start.26 = (f32[4,128,384]{2,1,0:T(8,128)}, f32[4,128,384]{2,1,0:T(8,128)S(1)}, u32[]{:S(2)}) copy-start(f32[4,128,384]{2,1,0:T(8,128)S(1)} %convert_dynamic-update-slice_fusion) | copy-start | bytes 2359300
  (14 other events, 14.6 us)
Sparse Core Ops, SparseCore 0:
  85.2 37.9 all-gather.1

commit v2 on v1

v2 whole, which is shorter than its diff:
```python
import itertools
import math

import jax
import jax.numpy as jnp
from jax import lax
from jax.experimental import pallas as pl
from jax.experimental.pallas import tpu as pltpu
from jax.sharding import PartitionSpec as P
import ml_dtypes
import numpy as np

AXES = ("img", "band")
SIZES = {"y": 4, "z": 8, "x": 4, "c": 2}
f32 = jnp.float32
bf16 = jnp.bfloat16
EPS = 1e-06
MIB = 1024 * 1024
CHUNK = 256


def dot(a, b):
    return jnp.dot(a, b, preferred_element_type=f32)


def dot_nt(a, b):
    return lax.dot_general(a, b, (((1,), (1,)), ((), ())), preferred_element_type=f32)


def dot_tn(a, b):
    return lax.dot_general(a, b, (((0,), (0,)), ((), ())), preferred_element_type=f32)


def inv_rms(v):
    return lax.rsqrt(jnp.mean(v * v, axis=-1, keepdims=True) + EPS)


def lane_iota(shape):
    return lax.broadcasted_iota(jnp.int32, shape, len(shape) - 1)


def head_mean(v):
    r = lax.broadcasted_iota(jnp.int32, (256, 256), 0) >> 6
    c = lax.broadcasted_iota(jnp.int32, (256, 256), 1) >> 6
    same = jnp.where(r == c, 1.0 / 64, 0.0).astype(bf16)
    v = v.astype(bf16)
    return jnp.concatenate(
        [dot(v[:, n : n + 256], same) for n in range(0, v.shape[1], 256)], axis=1
    )


def partner(v):
    first = (lane_iota((1, 128)) % 32) < 16
    return jnp.where(first, pltpu.roll(v, 112, 1), pltpu.roll(v, 16, 1))


def head_masks():
    low = (lane_iota((1, 128)) < 64).astype(f32)
    return low.astype(bf16), (1.0 - low).astype(bf16)


def both(at_ref, a_ref, b_ref, i):
    return jnp.concatenate([a_ref[2 * at_ref[0] + i], b_ref[i, :128]], axis=0).astype(f32)


def turns(at_ref, image, row_ref, col_ref, got, table_ref):
    here = pl.ds(2 * at_ref[0] + image, 1)
    hot = []
    for n, ref in enumerate((row_ref, col_ref)):
        kept = ref[here, :].astype(f32)
        pos = jnp.concatenate([kept, got[0:1, n * 128 : n * 128 + 128].astype(f32)], axis=1)
        spots = lax.broadcasted_iota(jnp.int32, (16, 256), 0).astype(f32)
        hot.append(jnp.where(spots == pos, 1.0, 0.0))
    hot = jnp.concatenate(hot, axis=0).astype(bf16)
    return [dot_tn(hot, table_ref[n]) + dot_tn(hot, table_ref[n + 1]) for n in (0, 2)]


def turn_table():
    lane = np.arange(128)
    rates = 10000.0 ** (-(lane % 16) / 16)
    angle = np.arange(16)[:, None] * rates
    row_lane = (lane % 64) < 32
    out = []
    for v in (np.cos(angle), np.sin(angle) * np.where(lane % 32 < 16, -1.0, 1.0)):
        v = np.concatenate([np.where(row_lane, v, 0.0), np.where(row_lane, 0.0, v)])
        high = v.astype(ml_dtypes.bfloat16)
        out += [high, (v - high.astype(np.float64)).astype(ml_dtypes.bfloat16)]
    return np.stack(out)


def pack_kernel(at_ref, lat_ref, dy_ref, row_ref, col_ref, lat_out, dy_out):
    other = 2 - 2 * at_ref[0]
    dy_out[...] = dy_ref[...]
    for i in range(2):
        lat_out[i, :128] = lat_ref[i]
        here = pl.ds(other + i, 1)
        line = jnp.concatenate(
            [row_ref[here, :].astype(f32), col_ref[here, :].astype(f32), jnp.zeros((1, 128), f32)],
            axis=1,
        )
        lat_out[i, 128:] = jnp.broadcast_to(line, (16, 384)).astype(bf16)


def split(v):
    hi = v.astype(bf16)
    return jnp.concatenate([hi, (v - hi.astype(f32)).astype(bf16)], axis=0)


def fine_dot(v, w):
    n = v.shape[0]
    out = dot(split(v), w)
    return out[:n] + out[n:]


def silu(v):
    return v / (1.0 + jnp.exp(-v))


def modulation_kernel(
    at_ref, t_ref, l_ref, tw1_ref, tw2_ref, row0_ref, row1_ref, modw_ref, mod_ref, extra_ref
):
    first = 2 * at_ref[0]
    freqs = jnp.exp(lane_iota((1, 128)).astype(f32) * (-math.log(10000.0) / 128))
    spot = lax.broadcasted_iota(jnp.int32, (16, 1), 0)
    steps = jnp.where(
        spot == 0,
        t_ref[first].astype(f32),
        jnp.where(spot == 1, t_ref[first + 1].astype(f32), 0.0),
    )
    angle = steps * freqs
    emb = jnp.concatenate([jnp.cos(angle), jnp.sin(angle)], axis=1)
    hidden = silu(fine_dot(emb, tw1_ref[...]))
    cond = fine_dot(hidden, tw2_ref[...])
    for i, ref in enumerate((row0_ref, row1_ref)):
        label = l_ref[first + i]
        row = jnp.sum(
            jnp.where(spot == (label & 15), ref[...].astype(f32), 0.0), axis=0, keepdims=True
        )
        cond = cond + jnp.where(spot == i, row, 0.0)
    mod = fine_dot(silu(cond), modw_ref[...])
    lane = lane_iota((1, 128))
    codes = jnp.zeros((1, 128), f32)
    for i in range(2):
        label = l_ref[first + i]
        codes = jnp.where(lane == i, (label >> 5).astype(f32), codes)
        codes = jnp.where(lane == 2 + i, (label & 31).astype(f32), codes)
        for k in range(6):
            mod_ref[i, k : k + 1] = mod[i : i + 1, k * 384 : k * 384 + 384]
        for b in range(2):
            extra_ref[1 + i * 2 + b : 2 + i * 2 + b] = emb[i : i + 1, b * 128 : b * 128 + 128]
        for b, p in enumerate(pairs()):
            extra_ref[5 + i * 3 + b : 6 + i * 3 + b] = cond[i : i + 1, p]
    extra_ref[0:1] = codes
    extra_ref[11:] = jnp.zeros((5, 128), f32)


def pairs(width=384):
    return [slice(j, j + 128) for j in range(0, width, 128)]


def forward_kernel(
    at_ref,
    kept_ref,
    got_ref,
    mod_ref,
    w_ref,
    qgain_ref,
    kgain_ref,
    row_ref,
    col_ref,
    table_ref,
    q_ref,
    k_ref,
    v_ref,
    att_ref,
):
    gains = [jnp.concatenate([r[...], r[...]], axis=1) for r in (qgain_ref, kgain_ref)]
    masks = head_masks()
    for i in range(2):
        x = both(at_ref, kept_ref, got_ref, i)
        h1 = (x * inv_rms(x) * (1.0 + mod_ref[i, 1:2]) + mod_ref[i, 0:1]).astype(bf16)
        z = dot(h1, w_ref[:, :768])
        v_ref[i] = dot(h1, w_ref[:, 768:]).astype(bf16)
        z = z * lax.rsqrt(head_mean(z * z) + EPS)
        cosine, sine = turns(at_ref, i, row_ref, col_ref, got_ref[i, 128:144], table_ref)
        for p in pairs():
            turned = []
            for part in range(2):
                n = z[:, part * 384 + p.start : part * 384 + p.stop] * gains[part]
                turned.append(n * cosine + partner(n) * sine)
            q = (turned[0].astype(bf16).astype(f32) * 0.125).astype(bf16)
            k = turned[1].astype(bf16)
            q_ref[i, :, p], k_ref[i, :, p] = q, k
            v = v_ref[i, :, p]
            out = None
            for m in masks:
                e = jnp.exp(dot_nt(q * m, k))
                part_out = dot(e.astype(bf16), v * m) / jnp.sum(e, axis=-1, keepdims=True)
                out = part_out if out is None else out + part_out
            att_ref[i * 256 : i * 256 + 256, p] = out.astype(bf16)


def mlp_kernel(
    at_ref,
    kept_ref,
    got_ref,
    dkept_ref,
    dgot_ref,
    att_ref,
    mod_ref,
    proj_ref,
    wgu_ref,
    wd_ref,
    keep_ref,
    send_ref,
    out_ref,
    outsend_ref,
    dmid_ref,
    sums_ref,
    branch_s,
    mid_s,
    h2_s,
    h2t_s,
    dmlp_s,
    mlp_s,
    dh2_s,
):
    images = range(2)

    def rows(i):
        return slice(i * 256, (i + 1) * 256)

    branch_s[...] = dot(att_ref[...], proj_ref[...])
    for i in images:
        mid = both(at_ref, kept_ref, got_ref, i) + mod_ref[i, 2:3] * branch_s[rows(i)]
        mid_s[rows(i)] = mid
        h2_s[rows(i)] = (mid * inv_rms(mid) * (1.0 + mod_ref[i, 4:5]) + mod_ref[i, 3:4]).astype(
            bf16
        )
        dmlp_s[rows(i)] = (mod_ref[i, 5:6] * both(at_ref, dkept_ref, dgot_ref, i)).astype(bf16)
    h2t_s[...] = h2_s[...].T
    h2 = h2_s[...]
    d_mlp = dmlp_s[...]
    first = True
    for ref, half in ((send_ref, 1 - at_ref[1]), (keep_ref, at_ref[1])):
        for n in range(2):
            base = half * 512 + n * CHUNK
            wg = wgu_ref[:, pl.ds(pl.multiple_of(base, CHUNK), CHUNK)]
            wu = wgu_ref[:, pl.ds(pl.multiple_of(base + 1024, CHUNK), CHUNK)]
            wd = wd_ref[pl.ds(pl.multiple_of(base, CHUNK), CHUNK), :]
            g = dot(h2, wg)
            u = dot(h2, wu)
            d_hid = dot_nt(d_mlp, wd)
            sig = 1.0 / (1.0 + jnp.exp(-g))
            act = g * sig
            hid = (act * u).astype(bf16)
            du = (d_hid * act).astype(bf16)
            dg = (d_hid * u * (sig + act * (1.0 - sig))).astype(bf16)
            mlp = dot(hid, wd)
            d_h2 = dot_nt(dg, wg) + dot_nt(du, wu)
            mlp_s[...] = mlp if first else mlp_s[...] + mlp
            dh2_s[...] = d_h2 if first else dh2_s[...] + d_h2
            first = False
            for m, d in ((0, dg), (4, du)):
                grad = dot(h2t_s[...], d).astype(bf16)
                for b in range(2):
                    ref[pl.ds((m + 2 * n + b) * 384, 384)] = grad[:, b * 128 : b * 128 + 128]
            down = dot_tn(hid, d_mlp).astype(bf16)
            for b in range(2):
                for c in range(3):
                    ref[pl.ds((8 + 2 * n + b) * 384 + c * 128, 128)] = down[
                        b * 128 : b * 128 + 128, c * 128 : c * 128 + 128
                    ]
    for i in images:
        mid, mlp, dh2 = mid_s[rows(i)], mlp_s[rows(i)], dh2_s[rows(i)]
        dy = both(at_ref, dkept_ref, dgot_ref, i)
        out = (mid + mod_ref[i, 5:6] * mlp).astype(bf16)
        out_ref[2 * at_ref[0] + i] = out[:128]
        outsend_ref[i] = out[128:]
        s = inv_rms(mid)
        n = mid * s
        e2 = dh2 * (1.0 + mod_ref[i, 4:5])
        d_mid = dy + s * (e2 - n * jnp.mean(e2 * n, axis=-1, keepdims=True))
        dmid_ref[rows(i)] = d_mid
        for k, v in enumerate((d_mid * branch_s[rows(i)], dh2, dh2 * n, dy * mlp)):
            total = jnp.sum(v, axis=0, keepdims=True)
            for b, p in enumerate(pairs()):
                sums_ref[pl.ds(i * 12 + k * 3 + b, 1)] = total[:, p]


def backward_kernel(
    at_ref,
    kept_ref,
    got_ref,
    mod_ref,
    w_ref,
    qgain_ref,
    kgain_ref,
    row_ref,
    col_ref,
    table_ref,
    q_ref,
    k_ref,
    v_ref,
    att_ref,
    dmid_ref,
    proj_ref,
    outsend_ref,
    keep_ref,
    send_ref,
    grad_ref,
    swap_ref,
    sums_ref,
    h1_s,
    dqkv_s,
    dbranch_s,
    units_s,
):
    gains = [jnp.concatenate([r[...], r[...]], axis=1) for r in (qgain_ref, kgain_ref)]
    masks = head_masks()
    gain_sums = [0.0, 0.0]
    for i in range(2):
        here = slice(i * 256, i * 256 + 256)
        x = both(at_ref, kept_ref, got_ref, i)
        s1 = inv_rms(x)
        n1 = x * s1
        h1 = (n1 * (1.0 + mod_ref[i, 1:2]) + mod_ref[i, 0:1]).astype(bf16)
        h1_s[here] = h1
        d_mid = dmid_ref[here]
        d_branch = (mod_ref[i, 2:3] * d_mid).astype(bf16)
        dbranch_s[here] = d_branch
        d_att = dot_nt(d_branch, proj_ref[...]).astype(bf16)
        z = dot(h1, w_ref[:, :768])
        r = lax.rsqrt(head_mean(z * z) + EPS)
        z = z * r
        cosine, sine = turns(at_ref, i, row_ref, col_ref, got_ref[i, 128:144], table_ref)
        turned = [[], []]
        for p in pairs():
            q, k, v, do = q_ref[i, :, p], k_ref[i, :, p], v_ref[i, :, p], d_att[:, p]
            dq = dk = dv = 0.0
            for m in masks:
                qm, km, dom = q * m, k * m, do * m
                e = jnp.exp(dot_nt(k, qm))
                soft = e * (1.0 / jnp.sum(e, axis=0, keepdims=True))
                d_probs = dot_nt(v, dom)
                delta = jnp.sum(soft * d_probs, axis=0, keepdims=True)
                ds = (soft * (d_probs - delta)).astype(bf16)
                dq = dq + dot_tn(ds, km)
                dk = dk + dot(ds, qm)
                dv = dv + dot(soft.astype(bf16), dom)
            for part, d in enumerate((dq * 0.125, dk)):
                n = z[:, part * 384 + p.start : part * 384 + p.stop]
                dn = d * cosine - partner(d) * sine
                gain_sums[part] = gain_sums[part] + jnp.sum(dn * n, axis=0, keepdims=True)
                turned[part].append(dn * gains[part])
            dqkv_s[here, 768 + p.start : 768 + p.stop] = dv.astype(bf16)
        e = jnp.concatenate(turned[0] + turned[1], axis=1)
        dqkv_s[here, :768] = (r * (e - z * head_mean(e * z))).astype(bf16)
        d_h1 = dot_nt(dqkv_s[here], w_ref[...])
        e1 = d_h1 * (1.0 + mod_ref[i, 1:2])
        grad = d_mid + s1 * (e1 - n1 * jnp.mean(e1 * n1, axis=-1, keepdims=True))
        grad_ref[2 * at_ref[0] + i] = grad[:128]
        swap_ref[i, 0] = outsend_ref[i]
        swap_ref[i, 1] = grad[128:].astype(bf16)
        for k, v in enumerate((d_h1, d_h1 * n1)):
            total = jnp.sum(v, axis=0, keepdims=True)
            for b, p in enumerate(pairs()):
                sums_ref[pl.ds(i * 6 + k * 3 + b, 1)] = total[:, p]
    gain_sums = [g + pltpu.roll(g, 64, 1) for g in gain_sums]
    sums_ref[pl.ds(12, 1)] = jnp.where(lane_iota((1, 128)) < 64, gain_sums[0], gain_sums[1])
    sums_ref[pl.ds(13, 3)] = jnp.zeros((3, 128), f32)
    h1t = h1_s[...].T
    for part in range(3):
        w = dot(h1t, dqkv_s[:, part * 384 : part * 384 + 384]).astype(bf16)
        for b, p in enumerate(pairs()):
            n = part * 3 + b
            units_s[n // 6, pl.ds(n % 6 * 384, 384)] = w[:, p]
    w = dot_tn(att_ref[...], dbranch_s[...]).astype(bf16)
    for b, p in enumerate(pairs()):
        units_s[1, pl.ds((3 + b) * 384, 384)] = w[:, p]
    keep_ref[...] = units_s[at_ref[1]]
    send_ref[...] = units_s[1 - at_ref[1]]


def whole_spec(shape):
    return pl.BlockSpec(shape, lambda *_: (0,) * len(shape))


def params(mib):
    return pltpu.CompilerParams(vmem_limit_bytes=mib * MIB)


def shape_of(shape, dtype):
    return jax.ShapeDtypeStruct(shape, dtype)


def cost(flops, nbytes):
    return pl.CostEstimate(flops=flops, bytes_accessed=nbytes, transcendentals=0)


def pack_call(at, latents, out_grad, pos_row, pos_col):
    theirs = pl.BlockSpec((2, 128, 384), lambda j, at: (1 - at[0], 0, 0))
    shapes = [(2, 144, 384), (2, 128, 384)]
    return pl.pallas_call(
        pack_kernel,
        grid_spec=pltpu.PrefetchScalarGridSpec(
            num_scalar_prefetch=1,
            grid=(1,),
            in_specs=[theirs, theirs, whole_spec((4, 128)), whole_spec((4, 128))],
            out_specs=[whole_spec(s) for s in shapes],
        ),
        out_shape=[shape_of(s, bf16) for s in shapes],
        compiler_params=params(56),
        cost_estimate=cost(200_000, 800_000),
        name="pack_swaps",
    )(at, latents, out_grad, pos_row, pos_col)


def modulation_call(at, timesteps, labels, t_w1, t_w2, label_table, mod_w):
    def row_spec(i):
        return pl.BlockSpec((16, 384), lambda j, at, t, l: (l[2 * at[0] + i] >> 4, 0))

    shapes = [(2, 6, 384), (16, 128)]
    return pl.pallas_call(
        modulation_kernel,
        grid_spec=pltpu.PrefetchScalarGridSpec(
            num_scalar_prefetch=3,
            grid=(1,),
            in_specs=[
                whole_spec((256, 384)),
                whole_spec((384, 384)),
                row_spec(0),
                row_spec(1),
                whole_spec((384, 2304)),
            ],
            out_specs=[whole_spec(s) for s in shapes],
        ),
        out_shape=[shape_of(s, f32) for s in shapes],
        compiler_params=params(56),
        cost_estimate=cost(1_000_000_000, 3_000_000),
        name="modulation",
    )(at, timesteps, labels, t_w1, t_w2, label_table, label_table, mod_w)


SCALARS = pl.BlockSpec(memory_space=pltpu.SMEM)
RESIDENT = pl.BlockSpec(memory_space=pltpu.VMEM)


def resident_call(kernel, name, outs, estimate, mib, scratch=(), loose=(), loose_out=()):
    def spec(is_loose, shape):
        return whole_spec(shape) if is_loose else RESIDENT

    def call(at, *arrays):
        return pl.pallas_call(
            kernel,
            grid=(1,),
            in_specs=[SCALARS] + [spec(n in loose, a.shape) for n, a in enumerate(arrays)],
            out_specs=[spec(n in loose_out, o[0]) for n, o in enumerate(outs)],
            out_shape=[shape_of(*o) for o in outs],
            scratch_shapes=[pltpu.VMEM(*o) for o in scratch],
            compiler_params=params(mib),
            cost_estimate=estimate,
            name=name,
        )(at, *arrays)

    return call


forward_call = resident_call(
    forward_kernel,
    "attention_forward",
    [((2, 256, 384), bf16)] * 3 + [((512, 384), bf16)],
    cost(3_000_000_000, 4_000_000),
    12,
    loose_out=range(4),
)
mlp_call = resident_call(
    mlp_kernel,
    "mlp_both_ways",
    [
        ((4608, 128), bf16),
        ((4608, 128), bf16),
        ((4, 128, 384), bf16),
        ((2, 128, 384), bf16),
        ((512, 384), f32),
        ((24, 128), f32),
    ],
    cost(6_000_000_000, 8_000_000),
    24,
    [
        ((512, 384), f32),
        ((512, 384), f32),
        ((512, 384), bf16),
        ((384, 512), bf16),
        ((512, 384), bf16),
        ((512, 384), f32),
        ((512, 384), f32),
    ],
    loose=(4,),
    loose_out=(2, 3, 4, 5),
)
backward_call = resident_call(
    backward_kernel,
    "attention_backward",
    [
        ((2304, 128), bf16),
        ((2304, 128), bf16),
        ((4, 128, 384), f32),
        ((2, 2, 128, 384), bf16),
        ((16, 128), f32),
    ],
    cost(5_000_000_000, 6_000_000),
    24,
    [((512, 384), bf16), ((512, 1152), bf16), ((512, 384), bf16), ((2, 2304, 128), bf16)],
    loose=range(9, 16),
    loose_out=(2, 3, 4),
)


def join_kernel(
    a_ref, a_got_ref, b_ref, b_got_ref, sums1_ref, sums2_ref, extra_ref, out_ref, lines
):
    lines[:24] = sums1_ref[...]
    lines[24:40] = sums2_ref[...]
    lines[37:48] = extra_ref[:11]
    out_ref[:, :288] = (a_ref[...].astype(f32) + a_got_ref[...].astype(f32)).astype(bf16)
    out_ref[:, 288:432] = (b_ref[...].astype(f32) + b_got_ref[...].astype(f32)).astype(bf16)
    out_ref[:, 432:] = jnp.broadcast_to(lines[...].astype(bf16)[None], (16, 48, 128))


def join_call(keep1, got1, keep2, got2, *lines):
    big, small = (16, 288, 128), (16, 144, 128)
    return pl.pallas_call(
        join_kernel,
        out_shape=shape_of((16, 480, 128), bf16),
        scratch_shapes=[pltpu.VMEM((48, 128), f32)],
        compiler_params=params(14),
        cost_estimate=cost(2_000_000, 6_000_000),
        name="join_messages",
    )(keep1.reshape(big), got1.reshape(big), keep2.reshape(small), got2.reshape(small), *lines)


def sum_kernel(a_ref, out_ref, extra_ref):
    total = a_ref[0, :432].astype(f32)
    for n in range(1, 16):
        total = total + a_ref[n, :432].astype(f32)
    out_ref[:432] = total.astype(bf16)
    out_ref[432:] = jnp.zeros((16, 128), bf16)
    extra_ref[...] = a_ref[:, 432:]


def sum_call(a):
    return pl.pallas_call(
        sum_kernel,
        out_shape=[shape_of((448, 128), bf16), shape_of((16, 48, 128), bf16)],
        compiler_params=params(14),
        cost_estimate=cost(2_000_000, 3_000_000),
        name="sum_xy",
    )(a)


def fetch(at_ref, own_ref, got_ref, slots, sems):
    c = at_ref[1]
    copies = [
        pltpu.make_async_copy(own_ref, slots.at[c], sems.at[0]),
        pltpu.make_async_copy(got_ref, slots.at[1 - c], sems.at[1]),
    ]
    for copy in copies:
        copy.start()
    for copy in copies:
        copy.wait()


def condition_kernel(
    at_ref,
    own_ref,
    got_ref,
    tw1_ref,
    tw2_ref,
    modw_ref,
    tw1g_ref,
    tw2g_ref,
    tableg_ref,
    modwg_ref,
    gains_ref,
    slots,
    rows_s,
    dmod_s,
    cond_s,
    emb_s,
    sems,
):
    fetch(at_ref, own_ref, got_ref, slots, sems)
    for h in range(2):
        for n in range(8):
            part = slots[h, pl.ds(n * 768, 768)]
            rows_s[pl.ds(h * 6144 + n * 768, 768)] = part.astype(f32)

    def line(r):
        return rows_s[pl.ds(r, 256, stride=48), :]

    for i in range(2):
        here = slice(i * 256, i * 256 + 256)
        for k in range(6):
            for b in range(3):
                r = 24 + i * 6 + k * 3 + b if k < 2 else i * 12 + (k - 2) * 3 + b
                at = k * 384 + b * 128
                dmod_s[here, at : at + 128] = line(r).astype(bf16)
        for b in range(2):
            emb_s[here, b * 128 : b * 128 + 128] = line(38 + i * 2 + b).astype(bf16)
        for b in range(3):
            cond_s[here, b * 128 : b * 128 + 128] = line(42 + i * 3 + b)
    gains_ref[...] = jnp.sum(line(36), axis=0, keepdims=True)
    codes = line(37)
    labels = jnp.concatenate([codes[:, i : i + 1] * 32.0 + codes[:, i + 2 : i + 3] for i in range(2)])
    cond = cond_s[...]
    sig = 1.0 / (1.0 + jnp.exp(-cond))
    act_t = (cond * sig).astype(bf16).T
    for k in range(6):
        cols = slice(k * 384, k * 384 + 384)
        modwg_ref[:, cols] = dot(act_t, dmod_s[:, cols])
    d_cond = dot_nt(dmod_s[...], modw_ref[...]) * (sig + cond * sig * (1.0 - sig))
    dc = d_cond.astype(bf16)
    labels = labels.astype(jnp.int32)
    for n in range(4):
        hot = jnp.where(lane_iota((512, 256)) + n * 256 == labels, 1.0, 0.0).astype(bf16)
        rows = dot_tn(hot, dc)
        top = min(256, 1001 - n * 256)
        tableg_ref[n * 256 : n * 256 + top] = rows[:top]
    emb = emb_s[...]
    pre = dot(emb, tw1_ref[...])
    sig = 1.0 / (1.0 + jnp.exp(-pre))
    hid = pre * sig
    tw2g_ref[...] = dot_tn(hid.astype(bf16), dc)
    d_pre = (dot_nt(dc, tw2_ref[...]) * (sig + hid * (1.0 - sig))).astype(bf16)
    tw1g_ref[...] = dot_tn(emb, d_pre)


def condition_call(at, own, got, t_w1, t_w2, mod_w):
    anywhere = pl.BlockSpec(memory_space=pl.ANY)
    shapes = [(256, 384), (384, 384), (1001, 384), (384, 2304), (1, 128)]
    return pl.pallas_call(
        condition_kernel,
        grid_spec=pltpu.PrefetchScalarGridSpec(
            num_scalar_prefetch=1,
            grid=(1,),
            in_specs=[anywhere, anywhere]
            + [whole_spec(s) for s in ((256, 384), (384, 384), (384, 2304))],
            out_specs=[whole_spec(s) for s in shapes],
            scratch_shapes=[
                pltpu.VMEM((2, 6144, 128), bf16),
                pltpu.VMEM((12288, 128), f32),
                pltpu.VMEM((512, 2304), bf16),
                pltpu.VMEM((512, 384), f32),
                pltpu.VMEM((512, 256), bf16),
                pltpu.SemaphoreType.DMA((2,)),
            ],
        ),
        out_shape=[shape_of(s, f32) for s in shapes],
        compiler_params=params(36),
        cost_estimate=cost(100_000_000, 100_000),
        name="condition_gradients",
    )(at, own, got, t_w1, t_w2, mod_w)


def cuts(start, chunk):
    out, at = [], start
    while at < start + 384:
        n = at // chunk
        stop = min((n + 1) * chunk, start + 384)
        out.append((n, at - n * chunk, stop - n * chunk))
        at = stop
    return out


def unpack_kernel(own, at_ref, sums_ref, *refs):
    qkv_ref, proj_ref, gu_ref, down_ref = refs[-4:]
    t = pl.program_id(0)
    half = at_ref[1] if own else 1 - at_ref[1]

    def first(u):
        rows = [sums_ref[n, a:b] for n, a, b in cuts(u * 384, 288)]
        return jnp.concatenate(rows).astype(f32)

    def second(u):
        rows = [sums_ref[n, 288 + a : 288 + b] for n, a, b in cuts(u * 384, 144)]
        return jnp.concatenate(rows).astype(f32)

    @pl.when(t == 0)
    def _():
        for b in range(4):
            gu_ref[:, b * 128 : b * 128 + 128] = first(b)
        for b, p in enumerate(pairs()):
            qkv_ref[:, p] = second(b)

    @pl.when(t == 1)
    def _():
        for n in range(4):
            gu_ref[:, n * 128 : n * 128 + 128] = first(4 + n)
            rows = first(8 + n)
            for b, p in enumerate(pairs()):
                down_ref[n * 128 : n * 128 + 128, p] = rows[b * 128 : b * 128 + 128]

        @pl.when(half == 0)
        def _():
            for b, p in enumerate(pairs()):
                qkv_ref[:, p] = second(3 + b)
            proj_ref[...] = jnp.zeros((384, 384), f32) if own else refs[0][...]

        @pl.when(half == 1)
        def _():
            for b, p in enumerate(pairs()):
                proj_ref[:, p] = second(3 + b)


def unpack_call(own, at, sums, earlier=()):
    def half_of(at):
        return at[1] if own else 1 - at[1]

    shapes = [(384, 1152), (384, 384), (384, 2048), (1024, 384)]
    anywhere = pl.BlockSpec(memory_space=pl.ANY)
    kept = [whole_spec((384, 384))] + [anywhere] * 3 if earlier else []
    earlier = [earlier[n] for n in (1, 0, 2, 3)] if earlier else []
    return pl.pallas_call(
        lambda *refs: unpack_kernel(own, *refs),
        grid_spec=pltpu.PrefetchScalarGridSpec(
            num_scalar_prefetch=1,
            grid=(2,),
            in_specs=[RESIDENT] + kept,
            out_specs=[
                pl.BlockSpec((384, 384), lambda t, at: (0, half_of(at) * (2 - t) + t)),
                whole_spec((384, 384)),
                pl.BlockSpec((384, 512), lambda t, at: (0, 2 * t + half_of(at))),
                pl.BlockSpec((512, 384), lambda t, at: (half_of(at), 0)),
            ],
        ),
        out_shape=[shape_of(s, f32) for s in shapes],
        input_output_aliases={2: 1, 3: 0, 4: 2, 5: 3} if earlier else {},
        compiler_params=params(20),
        cost_estimate=cost(2_000_000, 6_000_000),
        name="unpack_own" if own else "unpack_other",
    )(at, sums, *earlier)


def flat(y, z, x, c):
    return ((((y * 8 + z) * 2 + x % 2) * 2 + c) * 2) + x // 2


def groups(axes):
    rest = [a for a in "yzxc" if a not in axes]
    out = []
    for fixed in itertools.product(*[range(SIZES[a]) for a in rest]):
        place = dict(zip(rest, fixed))
        row = []
        for moving in itertools.product(*[range(SIZES[a]) for a in axes]):
            row.append(flat(**{**place, **dict(zip(axes, moving))}))
        out.append(row)
    return out


def exchange(v, axes):
    return lax.all_to_all(v, AXES, 0, 0, tiled=True, axis_index_groups=groups(axes))


def gather(v, axes):
    n = math.prod(SIZES[a] for a in axes)
    return exchange(jnp.broadcast_to(v[None], (n,) + v.shape), axes)


BAND_SWAP = [(n, n ^ 1) for n in range(256)]
CORE_SWAP = [(n, n ^ 2) for n in range(256)]


def swap(v):
    return lax.ppermute(v, AXES, BAND_SWAP)


def core_swap(v):
    return lax.ppermute(v, AXES, CORE_SWAP)


def body(
    latents,
    pos_row,
    pos_col,
    timesteps,
    labels,
    t_w1,
    t_w2,
    label_table,
    mod_w,
    qkv_w,
    q_gain,
    k_gain,
    proj_w,
    gate_up_w,
    down_w,
    out_grad,
):
    band = lax.axis_index("band")
    core = lax.axis_index("img") % 2
    at = jnp.stack([band, core]).astype(jnp.int32)
    send, dsend = pack_call(at, latents, out_grad, pos_row, pos_col)
    got = swap(send)
    mod, extra = modulation_call(at, timesteps, labels, t_w1, t_w2, label_table, mod_w)
    mod, dsend = lax.optimization_barrier((mod, dsend))
    dgot = swap(dsend)
    turn = (q_gain.reshape(1, 64), k_gain.reshape(1, 64), pos_row, pos_col, turn_table())
    q, k, v, att = forward_call(at, latents, got, mod, qkv_w, *turn)
    keep1, send1, block_out, out_send, d_mid, sums1 = mlp_call(
        at, latents, got, out_grad, dgot, att, mod, proj_w, gate_up_w, down_w
    )
    got1 = core_swap(send1)
    keep2, send2, latents_grad, swaps, sums2 = backward_call(
        at, latents, got, mod, qkv_w, *turn, q, k, v, att, d_mid, proj_w, out_send
    )
    joined = join_call(keep1, got1, keep2, core_swap(send2), sums1, sums2, extra)
    chunk, extra = sum_call(exchange(joined, "xy"))
    extra = lax.all_gather(
        extra.reshape(768, 128), AXES, axis=0, tiled=True, axis_index_groups=groups("z")
    )
    chunk = jnp.sum(exchange(chunk.reshape(8, 56, 128), "z").astype(f32), axis=0).astype(bf16)
    chunk = gather(chunk, "z").reshape(448, 128)
    chunk, swaps = lax.optimization_barrier((chunk, swap(swaps)))
    wide = lax.optimization_barrier(jnp.broadcast_to(chunk[None], (16, 448, 128)))
    summed = exchange(wide, "xy")
    extra, _ = lax.optimization_barrier((extra, wide))
    conditioned = condition_call(at, extra, core_swap(extra), t_w1, t_w2, mod_w)
    summed, conditioned = lax.optimization_barrier((summed, conditioned))
    tw1_grad, tw2_grad, table_grad, modw_grad, gain_sums = conditioned
    sums = unpack_call(True, at, summed)
    qkv_sum, proj_sum, gu_sum, down_sum = unpack_call(False, at, core_swap(summed), sums)
    other = 2 - 2 * band
    block_out = lax.dynamic_update_slice_in_dim(block_out, swaps[:, 0], other, 0)
    latents_grad = lax.dynamic_update_slice_in_dim(latents_grad, swaps[:, 1].astype(f32), other, 0)
    return (
        block_out,
        latents_grad,
        tw1_grad,
        tw2_grad,
        table_grad,
        modw_grad,
        qkv_sum,
        gain_sums[0, :64],
        gain_sums[0, 64:],
        proj_sum,
        gu_sum,
        down_sum,
    )


def solution(mesh):
    split = P("img", "band", None)
    return jax.shard_map(
        body,
        mesh=mesh,
        in_specs=(split, P("img", "band"), P("img", "band"), P("img"), P("img"))
        + (P(),) * 10
        + (split,),
        out_specs=(split, split) + (P(),) * 10,
        check_vma=False,
    )
```

time: 165 us -> 154 us (0.933)
  blocking collectives: 46.5 us -> 31.5 us
  waiting for transfers between devices: 18.7 us -> 27.7 us
  local copies, waits for them, and re-layouts: 15.7 us -> 7.23 us
  starting transfers between devices: 26.3 us -> 32.1 us
  Pallas kernels: 42.2 us -> 39.7 us
    all_to_all x2 -> x1, blocking collectives: 46.5 us -> 31.5 us  [exchange(): lax.all_to_all(v, AXES, 0, 0, tiled=True, axis_index_groups=groups(axes))]
    all_to_all x2 -> x3, waiting for transfers between devices: 2.74 us -> 15.4 us  [exchange(): lax.all_to_all(v, AXES, 0, 0, tiled=True, axis_index_groups=groups(axes))]
    unnamed x54 -> x44, local copies, waits for them, and re-layouts: 12.1 us -> 3.71 us
    all_to_all x2 -> x3, starting transfers between devices: 7.21 us -> 15.4 us  [exchange(): lax.all_to_all(v, AXES, 0, 0, tiled=True, axis_index_groups=groups(axes))]
    pallas_call x4 -> x5, Pallas kernels: 31 us -> 24 us  [the longest x3 17.1 us: call(): pl.pallas_call(kernel, grid=(1,), in_specs=[SCALARS] + [spec(n in loose,...]
    pallas_call x1, Pallas kernels: 1.3 us -> 3.78 us  [modulation_call(): pl.pallas_call(modulation_kernel, grid_spec=pltpu.PrefetchScalarGridSpec(...]
    ppermute x4 -> x3, waiting for transfers between devices: 5.04 us -> 2.71 us  [swap(): return lax.ppermute(v, AXES, BAND_SWAP)]
    pallas_call x1, Pallas kernels: 0.58 us -> 2.47 us  [pack_call(): pl.pallas_call(pack_kernel, grid_spec=pltpu.PrefetchScalarGridSpec(num_sc...]
  transfers between devices with their start and end apart: 11 -> 11, of which waited for: 6 -> 7; matrix products, arithmetic and copies ran while one was open for 2% -> 2% of each run, Pallas kernels for 15% -> 16%
where the time goes in v2:
time: 154 us; the launch traced here: 153 us
  Pallas kernels  39.7 us (26%)
  starting transfers between devices  32.1 us (21%)
  blocking collectives  31.5 us (20%)
  waiting for transfers between devices  27.7 us (18%)
  between operations  14.3 us (9%)
  local copies, waits for them, and re-layouts  7.23 us (5%)
    all_to_all x1, blocking collectives, exchange(): lax.all_to_all(v, AXES, 0, 0, tiled=True, axis_index_groups=groups(axes))  31.5 us
    pallas_call x3, Pallas kernels, call(): pl.pallas_call(kernel, grid=(1,), in_specs=[SCALARS] + [spec(n in loose,...  17.1 us
    all_to_all x3, waiting for transfers between devices, exchange(): lax.all_to_all(v, AXES, 0, 0, tiled=True, axis_index_groups=groups(axes))  15.4 us
    all_to_all x3, starting transfers between devices, exchange(): lax.all_to_all(v, AXES, 0, 0, tiled=True, axis_index_groups=groups(axes))  15.4 us
    ppermute x4, starting transfers between devices, core_swap(): return lax.ppermute(v, AXES, CORE_SWAP)  11.6 us
    pallas_call x1, Pallas kernels, condition_call(): pl.pallas_call(condition_kernel, grid_spec=pltpu.PrefetchScalarGridSpec(n...  7.67 us
    pallas_call x2, Pallas kernels, unpack_call(): pl.pallas_call(lambda *refs: unpack_kernel(own, *refs), grid_spec=pltpu.P...  6.89 us
    ppermute x4, waiting for transfers between devices, core_swap(): return lax.ppermute(v, AXES, CORE_SWAP)  5.21 us
  transfers between devices with their start and end apart: 11, of which 7 were waited for; matrix products, arithmetic and copies ran while one was open for 2% of the time, Pallas kernels for 16%

profile of v2, /device:TPU:1, one launch (start us, length us, event | category | flops | bytes accessed | tf_op | source)
XLA Modules:
  0.0 153.1 jit_solution(14990246745310663752)
XLA Ops:
  7.8 2.5 %pack_swaps.1 = (bf16[2,144,384]{2,1,0:T(8,128)(2,1)}, bf16[2,128,384]{2,1,0:T(8,128)(2,1)}) custom-call(s32[2]{0:T(128)} %pad_add_fusion.at_ref.refs_0_, bf16[4,128,384]{2,1,0:T(8,128)(2,1)} %kept_ref.5, bf16[4,128,384]{2,1,0:T(8,128)(2,1)} %dkept_ref.1, s32[4,128]{1,0:T(4,128)} %row_ref.5, s32[4,128]{1,0:T(4,128)} %col_ref.5), custom_call_target="tpu_custom_call" | custom-call | flops 200000 | bytes 800000 | tf_op jit(solution)/shard_map/pack_swaps/pallas_call | solution.py:404
  10.4 3.7 %collective-permute-start = (bf16[2,144,384]{2,1,0:T(8,128)(2,1)}, bf16[2,144,384]{2,1,0:T(8,128)(2,1)S(1)}, u32[]{:S(2)}, u32[]{:S(2)}) collective-permute-start(bf16[2,144,384]{2,1,0:T(8,128)(2,1)} %get-tuple-element.57), channel_id=1, source_target_pairs={{0,1},{1,0},{2,3},{3,2},{4,5},{5,4},{6,7},{7,6},{8,9},{9,8},{10,11... | collective-permute-start | bytes 663560 | tf_op jit(solution)/shard_map/ppermute | solution.py:775
  14.0 3.8 %modulation.1 = (f32[2,6,384]{2,1,0:T(8,128)}, f32[16,128]{1,0:T(8,128)}) custom-call(s32[2]{0:T(128)} %pad_add_fusion.at_ref.refs_0_, s32[4]{0:T(128)} %t_ref.1, s32[4]{0:T(128)} %l_ref.1, bf16[256,384]{1,0:T(8,128)(2,1)} %tw1_ref.3, bf16[384,384]{1,0:T(8,128)(2,1)} %tw2_ref.3, bf16[1001,384]{1,0:T(8,128)(2,1)} %row1_ref.1, bf16[1001,384]{1,0:T(8,128)(2,1)} %row1_ref.1, ...), custom_call_target="tpu_custom_call" | custom-call | flops 1000000000 | bytes 3000000 | tf_op jit(solution)/shard_map/modulation/pallas_call | solution.py:424
  19.3 3.3 %attention_forward.1 = (bf16[2,256,384]{2,1,0:T(8,128)(2,1)S(1)}, bf16[2,256,384]{2,1,0:T(8,128)(2,1)S(1)}, bf16[2,256,384]{2,1,0:T(8,128)(2,1)S(1)}, bf16[512,384]{1,0:T(8,128)(2,1)S(1)}) custom-call(s32[2]{0:T(128)S(1)} %copy-done.6, bf16[4,128,384]{2,1,0:T(8,128)(2,1)S(1)} %copy-done.5, bf16[2,144,384]{2,1,0:T(8,128)(2,1)S(1)} %collective-permute-done.got_ref, ...), custom_call_target="tpu_custom_call" | custom-call | flops 3000000000 | bytes 4000000 | tf_op jit(solution)/shard_map/attention_forward/pallas_call | solution.py:454
  22.5 2.2 %collective-permute-done.1.dgot_ref = bf16[2,128,384]{2,1,0:T(8,128)(2,1)S(1)} collective-permute-done((bf16[2,128,384]{2,1,0:T(8,128)(2,1)S(1)}, bf16[2,128,384]{2,1,0:T(8,128)(2,1)S(1)}, u32[]{:S(2)}, u32[]{:S(2)}) %collective-permute-start.1) | collective-permute-done | bytes 196640 | tf_op jit(solution)/shard_map/ppermute | solution.py:775
  24.8 6.1 %mlp_both_ways.1 = (bf16[4608,128]{1,0:T(8,128)(2,1)S(1)}, bf16[4608,128]{1,0:T(8,128)(2,1)S(1)}, bf16[4,128,384]{2,1,0:T(8,128)(2,1)}, bf16[2,128,384]{2,1,0:T(...) custom-call(s32[2]{0:T(128)S(1)} %copy-done.6, bf16[4,128,384]{2,1,0:T(8,128)(2,1)S(1)} %copy-done.5, ...), custom_call_target="tpu_custom_call" | custom-call | flops 6000000000 | bytes 8000000 | tf_op jit(solution)/shard_map/mlp_both_ways/pallas_call | solution.py:454
  30.9 2.1 %collective-permute-start.2 = (bf16[4608,128]{1,0:T(8,128)(2,1)S(1)}, bf16[4608,128]{1,0:T(8,128)(2,1)S(1)}, u32[]{:S(2)}, u32[]{:S(2)}) collective-permute-start(bf16[4608,128]{1,0:T(8,128)(2,1)S(1)} %get-tuple-element.65), channel_id=1, source_target_pairs={{0,2},{1,3},{2,0},{3,1},{4,6},{5,7},{6,4},{7,5},{8,10},{9,11},{10,... | collective-permute-start | bytes 3538952 | tf_op jit(solution)/shard_map/ppermute | solution.py:779
  33.0 7.7 %attention_backward.1 = (bf16[2304,128]{1,0:T(8,128)(2,1)S(1)}, bf16[2304,128]{1,0:T(8,128)(2,1)S(1)}, f32[4,128,384]{2,1,0:T(8,128)}, bf16[2,2,128,384]{3,2,1,0:T(8,128)(2,1)S(1)}, f32[16,128]{1,0:T(8,128)S(1)}) custom-call(s32[2]{0:T(128)S(1)} %copy-done.6, bf16[4,128,384]{2,1,0:T(8,128)(2,1)S(1)} %copy-done.5, ...), custom_call_target="tpu_custom_call" | custom-call | flops 5000000000 | bytes 6000000 | tf_op jit(solution)/shard_map/attention_backward/pallas_call | solution.py:454
  40.8 2.0 %collective-permute-done.3 = bf16[2304,128]{1,0:T(8,128)(2,1)S(1)} collective-permute-done((bf16[2304,128]{1,0:T(8,128)(2,1)S(1)}, bf16[2304,128]{1,0:T(8,128)(2,1)S(1)}, u32[]{:S(2)}, u32[]{:S(2)}) %collective-permute-start.3) | collective-permute-done | bytes 589856 | tf_op jit(solution)/shard_map/ppermute | solution.py:779
  43.7 31.5 %all_to_all.20.a_ref = bf16[16,480,128]{2,1,0:T(8,128)(2,1)S(1)} all-to-all(bf16[16,480,128]{2,1,0:T(8,128)(2,1)S(1)} %join_messages.1), channel_id=1, replica_groups={{0,64,128,192,4,68,132,196,1,65,129,193,5,69,133,197},{2,66,130,194,6,7..., dimensions={0} | all-to-all | bytes 3932160 | tf_op jit(solution)/shard_map/all_to_all | solution.py:762
  76.1 8.2 %all-to-all-start.1 = ((bf16[8,56,128]{2,1,0:T(8,128)(2,1)}), bf16[8,56,128]{2,1,0:T(8,128)(2,1)S(1)}, u32[]{:S(2)}, u32[]{:S(2)}) async-start(bf16[8,56,128]{2,1,0:T(8,128)(2,1)} %bitcast.8), calls=%async_computation.1 | async-start | bytes 229376 | tf_op jit(solution)/shard_map/all_to_all | solution.py:762
  85.6 6.6 %all-to-all-done.1 = bf16[8,56,128]{2,1,0:T(8,128)(2,1)S(1)} async-done(((bf16[8,56,128]{2,1,0:T(8,128)(2,1)}), bf16[8,56,128]{2,1,0:T(8,128)(2,1)S(1)}, u32[]{:S(2)}, u32[]{:S(2)}) %all-to-all-start.1) | async-done | bytes 114720 | tf_op jit(solution)/shard_map/all_to_all | solution.py:762
  92.8 3.4 %all-to-all-start.2 = ((bf16[8,56,128]{2,1,0:T(8,128)(2,1)}), bf16[8,56,128]{2,1,0:T(8,128)(2,1)S(1)}, u32[]{:S(2)}, u32[]{:S(2)}) async-start(bf16[8,56,128]{2,1,0:T(8,128)(2,1)} %broadcast_in_dim.4), calls=%async_computation.2 | async-start | bytes 229376 | tf_op jit(solution)/shard_map/all_to_all | solution.py:762
  96.2 8.9 %all-to-all-done.2 = bf16[8,56,128]{2,1,0:T(8,128)(2,1)S(1)} async-done(((bf16[8,56,128]{2,1,0:T(8,128)(2,1)}), bf16[8,56,128]{2,1,0:T(8,128)(2,1)S(1)}, u32[]{:S(2)}, u32[]{:S(2)}) %all-to-all-start.2) | async-done | bytes 114720 | tf_op jit(solution)/shard_map/all_to_all | solution.py:762
  105.1 1.6 %broadcast_in_dim.5 = bf16[16,448,128]{2,1,0:T(8,128)(2,1)} broadcast(bf16[448,128]{1,0:T(8,128)(2,1)S(1)} %bitcast.28), dimensions={1,2} | broadcast | bytes 1949696 | tf_op jit(solution)/shard_map/broadcast_in_dim | solution.py:825
  106.7 3.8 %all-to-all-start.3 = ((bf16[16,448,128]{2,1,0:T(8,128)(2,1)}), bf16[16,448,128]{2,1,0:T(8,128)(2,1)S(1)}, u32[]{:S(2)}, u32[]{:S(2)}) async-start(bf16[16,448,128]{2,1,0:T(8,128)(2,1)} %broadcast_in_dim.5), calls=%async_computation.3 | async-start | bytes 3670016 | tf_op jit(solution)/shard_map/all_to_all | solution.py:762
  110.5 4.3 %all-gather.2.cloned.1.call-done.own_ref = bf16[6144,128]{1,0:T(8,128)(2,1)} async-done(((bf16[768,128]{1,0:T(8,128)(2,1)}), bf16[6144,128]{1,0:T(8,128)(2,1)}) %all-gather.2.cloned.1.call-update) | async-done | bytes 1572880 | tf_op jit(solution)/shard_map/all_gather | solution.py:819
  114.8 3.9 %collective-permute-start.5 = (bf16[6144,128]{1,0:T(8,128)(2,1)}, bf16[6144,128]{1,0:T(8,128)(2,1)S(1)}, u32[]{:S(2)}, u32[]{:S(2)}) collective-permute-start(bf16[6144,128]{1,0:T(8,128)(2,1)} %all-gather.2.cloned.1.call-done.own_ref), channel_id=1, source_target_pairs={{0,2},{1,3},{2,0},{3,1},{4,6},{5,7},{6,4},{7,5},{8,10},{9,11},{10,... | collective-permute-start | bytes 4718600 | tf_op jit(solution)/shard_map/ppermute | solution.py:779
  118.7 3.2 %collective-permute-done.5.got_ref = bf16[6144,128]{1,0:T(8,128)(2,1)S(1)} collective-permute-done((bf16[6144,128]{1,0:T(8,128)(2,1)}, bf16[6144,128]{1,0:T(8,128)(2,1)S(1)}, u32[]{:S(2)}, u32[]{:S(2)}) %collective-permute-start.5) | collective-permute-done | bytes 1572896 | tf_op jit(solution)/shard_map/ppermute | solution.py:779
  122.0 1.5 copy-done
  124.9 7.7 %condition_gradients.1 = (f32[256,384]{1,0:T(8,128)}, f32[384,384]{1,0:T(8,128)}, f32[1001,384]{1,0:T(8,128)}, f32[384,2304]{1,0:T(8,128)}, f32[1,128]{1,0:T(1,128)S(1)}) custom-call(s32[2]{0:T(128)S(1)} %copy-done.6, bf16[6144,128]{1,0:T(8,128)(2,1)S(1)} %copy-done.1, bf16[6144,128]{1,0:T(8,128)(2,1)S(1)} %collective-permute-done.5.got_ref, ...), custom_call_target="tpu_custom_call" | custom-call | flops 100000000 | bytes 100000 | tf_op jit(solution)/shard_map/condition_gradients/pallas_call | solution.py:642
  132.5 5.5 %collective-permute-start.6 = (bf16[16,448,128]{2,1,0:T(8,128)(2,1)S(1)}, bf16[16,448,128]{2,1,0:T(8,128)(2,1)}, u32[]{:S(2)}, u32[]{:S(2)}) collective-permute-start(bf16[16,448,128]{2,1,0:T(8,128)(2,1)S(1)} %all-to-all-done.3.refs_1_), channel_id=1, source_target_pairs={{0,2},{1,3},{2,0},{3,1},{4,6},{5,7},{6,4},{7,5},{8,10},{9,11},{10,... | collective-permute-start | bytes 5505032 | tf_op jit(solution)/shard_map/ppermute | solution.py:779
  138.8 2.5 %unpack_own.1 = (f32[384,1152]{1,0:T(8,128)}, f32[384,384]{1,0:T(8,128)}, f32[384,2048]{1,0:T(8,128)}, f32[1024,384]{1,0:T(8,128)}) custom-call(s32[2]{0:T(128)S(1)} %copy-done.6, bf16[16,448,128]{2,1,0:T(8,128)(2,1)S(1)} %all-to-all-done.3.refs_1_), custom_call_target="tpu_custom_call" | custom-call | flops 2000000 | bytes 6000000 | tf_op jit(solution)/shard_map/unpack_own/pallas_call | solution.py:724
  141.9 4.3 %unpack_other.1 = (f32[384,1152]{1,0:T(8,128)}, f32[384,384]{1,0:T(8,128)}, f32[384,2048]{1,0:T(8,128)}, f32[1024,384]{1,0:T(8,128)}) custom-call(s32[2]{0:T(128)S(1)} %copy-done.6, bf16[16,448,128]{2,1,0:T(8,128)(2,1)} %collective-permute-done.6.refs_1_, ...), custom_call_target="tpu_custom_call", output_to_operand_aliasing={{1}: (2, {}), {0}: (3, {}), {2}: (4, {}), {3}: (5, {})} | custom-call | flops 2000000 | bytes 6000000 | tf_op jit(solution)/shard_map/unpack_other/pallas_call | solution.py:724
  (61 shorter events, 8.7 us)
Async XLA Ops:
  7.2 107.6 %all-gather.2.cloned.1.call-start = ((), (), s32[]{:S(2)}) async-start(), calls=%async_computation.4 | async-start | bytes 1769472 | tf_op jit(solution)/shard_map/all_gather | solution.py:819
  10.3 7.5 %copy-start.21 = (bf16[2,128,384]{2,1,0:T(8,128)(2,1)S(1)}, bf16[2,128,384]{2,1,0:T(8,128)(2,1)}, u32[]{:S(2)}) copy-start(bf16[2,128,384]{2,1,0:T(8,128)(2,1)} %get-tuple-element.60) | copy-start | bytes 589828
  10.3 8.2 %copy-start.5 = (bf16[4,128,384]{2,1,0:T(8,128)(2,1)S(1)}, bf16[4,128,384]{2,1,0:T(8,128)(2,1)}, u32[]{:S(2)}) copy-start(bf16[4,128,384]{2,1,0:T(8,128)(2,1)} %kept_ref.5) | copy-start | bytes 1179652
  10.3 8.2 %copy-start.6 = (s32[2]{0:T(128)S(1)}, s32[2]{0:T(128)}, u32[]{:S(2)}) copy-start(s32[2]{0:T(128)} %pad_add_fusion.at_ref.refs_0_) | copy-start | bytes 28
  10.3 8.2 %copy-start.8 = (s32[4,128]{1,0:T(4,128)S(1)}, s32[4,128]{1,0:T(4,128)}, u32[]{:S(2)}) copy-start(s32[4,128]{1,0:T(4,128)} %row_ref.5) | copy-start | bytes 6148
  10.3 8.1 %copy-start.9 = (s32[4,128]{1,0:T(4,128)S(1)}, s32[4,128]{1,0:T(4,128)}, u32[]{:S(2)}) copy-start(s32[4,128]{1,0:T(4,128)} %col_ref.5) | copy-start | bytes 6148
  10.3 8.1 %copy-start.11 = (bf16[384,1152]{1,0:T(8,128)(2,1)S(1)}, bf16[384,1152]{1,0:T(8,128)(2,1)}, u32[]{:S(2)}) copy-start(bf16[384,1152]{1,0:T(8,128)(2,1)} %w_ref.3) | copy-start | bytes 2654212
  10.3 8.1 %copy-start.16 = (f32[64]{0:T(128)S(1)}, f32[64]{0:T(128)}, u32[]{:S(2)}) copy-start(f32[64]{0:T(128)} %param.27) | copy-start | bytes 772
  10.4 8.1 %copy-start.17 = (f32[64]{0:T(128)S(1)}, f32[64]{0:T(128)}, u32[]{:S(2)}) copy-start(f32[64]{0:T(128)} %param.28) | copy-start | bytes 772
  10.4 8.1 %copy-start.18 = (bf16[4,32,128]{2,1,0:T(8,128)(2,1)S(1)}, bf16[4,32,128]{2,1,0:T(8,128)(2,1)}, u32[]{:S(2)}) copy-start(bf16[4,32,128]{2,1,0:T(8,128)(2,1)} %constant.30.clone.table_ref) | copy-start | bytes 98308
  10.4 8.1 %collective-permute-start = (bf16[2,144,384]{2,1,0:T(8,128)(2,1)}, bf16[2,144,384]{2,1,0:T(8,128)(2,1)S(1)}, u32[]{:S(2)}, u32[]{:S(2)}) collective-permute-start(bf16[2,144,384]{2,1,0:T(8,128)(2,1)} %get-tuple-element.57), channel_id=1, source_target_pairs={{0,1},{1,0},{2,3},{3,2},{4,5},{5,4},{6,7},{7,6},{8,9},{9,8},{10,11... | collective-permute-start | bytes 663560 | tf_op jit(solution)/shard_map/ppermute | solution.py:775
  17.8 7.0 %collective-permute-start.1 = (bf16[2,128,384]{2,1,0:T(8,128)(2,1)S(1)}, bf16[2,128,384]{2,1,0:T(8,128)(2,1)S(1)}, u32[]{:S(2)}, u32[]{:S(2)}) collective-permute-start(bf16[2,128,384]{2,1,0:T(8,128)(2,1)S(1)} %copy-done.21), channel_id=1, source_target_pairs={{0,1},{1,0},{2,3},{3,2},{4,5},{5,4},{6,7},{7,6},{8,9},{9,8},{10,11... | collective-permute-start | bytes 589832 | tf_op jit(solution)/shard_map/ppermute | solution.py:775
  30.9 11.8 %collective-permute-start.2 = (bf16[4608,128]{1,0:T(8,128)(2,1)S(1)}, bf16[4608,128]{1,0:T(8,128)(2,1)S(1)}, u32[]{:S(2)}, u32[]{:S(2)}) collective-permute-start(bf16[4608,128]{1,0:T(8,128)(2,1)S(1)} %get-tuple-element.65), channel_id=1, source_target_pairs={{0,2},{1,3},{2,0},{3,1},{4,6},{5,7},{6,4},{7,5},{8,10},{9,11},{10,... | collective-permute-start | bytes 3538952 | tf_op jit(solution)/shard_map/ppermute | solution.py:779
  33.0 9.7 %copy-start.7 = (f32[16,128]{1,0:T(8,128)S(1)}, f32[16,128]{1,0:T(8,128)}, u32[]{:S(2)}) copy-start(f32[16,128]{1,0:T(8,128)} %get-tuple-element.75.extra_ref) | copy-start | bytes 24580
  40.7 2.0 %collective-permute-start.3 = (bf16[2304,128]{1,0:T(8,128)(2,1)S(1)}, bf16[2304,128]{1,0:T(8,128)(2,1)S(1)}, u32[]{:S(2)}, u32[]{:S(2)}) collective-permute-start(bf16[2304,128]{1,0:T(8,128)(2,1)S(1)} %get-tuple-element.72), channel_id=1, source_target_pairs={{0,2},{1,3},{2,0},{3,1},{4,6},{5,7},{6,4},{7,5},{8,10},{9,11},{10,... | collective-permute-start | bytes 1769480 | tf_op jit(solution)/shard_map/ppermute | solution.py:779
  76.1 16.1 %all-to-all-start.1 = ((bf16[8,56,128]{2,1,0:T(8,128)(2,1)}), bf16[8,56,128]{2,1,0:T(8,128)(2,1)S(1)}, u32[]{:S(2)}, u32[]{:S(2)}) async-start(bf16[8,56,128]{2,1,0:T(8,128)(2,1)} %bitcast.8), calls=%async_computation.1 | async-start | bytes 229376 | tf_op jit(solution)/shard_map/all_to_all | solution.py:762
  84.3 11.9 %collective-permute-start.4 = (bf16[2,2,128,384]{3,2,1,0:T(8,128)(2,1)S(1)}, bf16[2,2,128,384]{3,2,1,0:T(8,128)(2,1)S(1)}, u32[]{:S(2)}, u32[]{:S(2)}) collective-permute-start(bf16[2,2,128,384]{3,2,1,0:T(8,128)(2,1)S(1)} %get-tuple-element.77), channel_id=1, source_target_pairs={{0,1},{1,0},{2,3},{3,2},{4,5},{5,4},{6,7},{7,6},{8,9},{9,8},{10,11... | collective-permute-start | bytes 1179656 | tf_op jit(solution)/shard_map/ppermute | solution.py:775
  92.8 12.3 %all-to-all-start.2 = ((bf16[8,56,128]{2,1,0:T(8,128)(2,1)}), bf16[8,56,128]{2,1,0:T(8,128)(2,1)S(1)}, u32[]{:S(2)}, u32[]{:S(2)}) async-start(bf16[8,56,128]{2,1,0:T(8,128)(2,1)} %broadcast_in_dim.4), calls=%async_computation.2 | async-start | bytes 229376 | tf_op jit(solution)/shard_map/all_to_all | solution.py:762
  106.7 15.3 %copy-start.2 = (bf16[384,384]{1,0:T(8,128)(2,1)S(1)}, bf16[384,384]{1,0:T(8,128)(2,1)}, u32[]{:S(2)}) copy-start(bf16[384,384]{1,0:T(8,128)(2,1)} %tw2_ref.3) | copy-start | bytes 884740
  106.7 15.3 %copy-start.3 = (bf16[256,384]{1,0:T(8,128)(2,1)S(1)}, bf16[256,384]{1,0:T(8,128)(2,1)}, u32[]{:S(2)}) copy-start(bf16[256,384]{1,0:T(8,128)(2,1)} %tw1_ref.3) | copy-start | bytes 589828
  106.7 32.1 %copy-start.19 = (f32[4,128,384]{2,1,0:T(8,128)S(1)}, f32[4,128,384]{2,1,0:T(8,128)}, u32[]{:S(2)}) copy-start(f32[4,128,384]{2,1,0:T(8,128)} %get-tuple-element.79) | copy-start | bytes 2359300
  106.7 25.9 %all-to-all-start.3 = ((bf16[16,448,128]{2,1,0:T(8,128)(2,1)}), bf16[16,448,128]{2,1,0:T(8,128)(2,1)S(1)}, u32[]{:S(2)}, u32[]{:S(2)}) async-start(bf16[16,448,128]{2,1,0:T(8,128)(2,1)} %broadcast_in_dim.5), calls=%async_computation.3 | async-start | bytes 3670016 | tf_op jit(solution)/shard_map/all_to_all | solution.py:762
  114.8 7.1 %collective-permute-start.5 = (bf16[6144,128]{1,0:T(8,128)(2,1)}, bf16[6144,128]{1,0:T(8,128)(2,1)S(1)}, u32[]{:S(2)}, u32[]{:S(2)}) collective-permute-start(bf16[6144,128]{1,0:T(8,128)(2,1)} %all-gather.2.cloned.1.call-done.own_ref), channel_id=1, source_target_pairs={{0,2},{1,3},{2,0},{3,1},{4,6},{5,7},{6,4},{7,5},{8,10},{9,11},{10,... | collective-permute-start | bytes 4718600 | tf_op jit(solution)/shard_map/ppermute | solution.py:779
  132.5 9.4 %collective-permute-start.6 = (bf16[16,448,128]{2,1,0:T(8,128)(2,1)S(1)}, bf16[16,448,128]{2,1,0:T(8,128)(2,1)}, u32[]{:S(2)}, u32[]{:S(2)}) collective-permute-start(bf16[16,448,128]{2,1,0:T(8,128)(2,1)S(1)} %all-to-all-done.3.refs_1_), channel_id=1, source_target_pairs={{0,2},{1,3},{2,0},{3,1},{4,6},{5,7},{6,4},{7,5},{8,10},{9,11},{10,... | collective-permute-start | bytes 5505032 | tf_op jit(solution)/shard_map/ppermute | solution.py:779
  (9 other events, 38.8 us)
Sparse Core Ops, SparseCore 0:
  76.2 38.5 all-gather.1

commit v3 on v2

--- a/solution.py
+++ b/solution.py
@@ -11,7 +11,6 @@
 import numpy as np
 
 AXES = ("img", "band")
-SIZES = {"y": 4, "z": 8, "x": 4, "c": 2}
 f32 = jnp.float32
 bf16 = jnp.bfloat16
 EPS = 1e-06
@@ -394,6 +393,11 @@
     return jax.ShapeDtypeStruct(shape, dtype)
 
 
+SCALARS = pl.BlockSpec(memory_space=pltpu.SMEM)
+RESIDENT = pl.BlockSpec(memory_space=pltpu.VMEM)
+IN_HBM = pl.BlockSpec(memory_space=pltpu.HBM)
+
+
 def cost(flops, nbytes):
     return pl.CostEstimate(flops=flops, bytes_accessed=nbytes, transcendentals=0)
 
@@ -440,10 +444,6 @@
         cost_estimate=cost(1_000_000_000, 3_000_000),
         name="modulation",
     )(at, timesteps, labels, t_w1, t_w2, label_table, label_table, mod_w)
-
-
-SCALARS = pl.BlockSpec(memory_space=pltpu.SMEM)
-RESIDENT = pl.BlockSpec(memory_space=pltpu.VMEM)
 
 
 def resident_call(kernel, name, outs, estimate, mib, scratch=(), loose=(), loose_out=()):
@@ -540,127 +540,175 @@
     )(keep1.reshape(big), got1.reshape(big), keep2.reshape(small), got2.reshape(small), *lines)
 
 
-def sum_kernel(a_ref, out_ref, extra_ref):
+def extra_kernel(a_ref, out_ref):
+    out_ref[...] = a_ref[:, 432:]
+
+
+def extra_call(a):
+    return pl.pallas_call(
+        extra_kernel,
+        in_specs=[RESIDENT],
+        out_specs=RESIDENT,
+        out_shape=shape_of((16, 48, 128), bf16),
+        compiler_params=params(4),
+        cost_estimate=cost(1_000, 200_000),
+        name="extra_rows",
+    )(a)
+
+
+def sum_kernel(at_ref, a_ref, keep_ref, send_ref, total_s):
     total = a_ref[0, :432].astype(f32)
     for n in range(1, 16):
         total = total + a_ref[n, :432].astype(f32)
-    out_ref[:432] = total.astype(bf16)
-    out_ref[432:] = jnp.zeros((16, 128), bf16)
-    extra_ref[...] = a_ref[:, 432:]
-
-
-def sum_call(a):
+    total = total.astype(bf16)
+    total_s[0] = total[:224]
+    total_s[1, :208] = total[224:]
+    total_s[1, 208:] = jnp.zeros((16, 128), bf16)
+    keep_ref[...] = total_s[at_ref[2]]
+    send_ref[...] = total_s[1 - at_ref[2]]
+
+
+def sum_call(at, a):
     return pl.pallas_call(
         sum_kernel,
-        out_shape=[shape_of((448, 128), bf16), shape_of((16, 48, 128), bf16)],
+        in_specs=[SCALARS, RESIDENT],
+        out_specs=[RESIDENT] * 2,
+        out_shape=[shape_of((224, 128), bf16)] * 2,
+        scratch_shapes=[pltpu.VMEM((2, 224, 128), bf16)],
         compiler_params=params(14),
         cost_estimate=cost(2_000_000, 3_000_000),
-        name="sum_xy",
-    )(a)
-
-
-def fetch(at_ref, own_ref, got_ref, slots, sems):
-    c = at_ref[1]
-    copies = [
-        pltpu.make_async_copy(own_ref, slots.at[c], sems.at[0]),
-        pltpu.make_async_copy(got_ref, slots.at[1 - c], sems.at[1]),
-    ]
-    for copy in copies:
-        copy.start()
-    for copy in copies:
-        copy.wait()
-
-
-def condition_kernel(
-    at_ref,
-    own_ref,
-    got_ref,
-    tw1_ref,
-    tw2_ref,
-    modw_ref,
-    tw1g_ref,
-    tw2g_ref,
-    tableg_ref,
-    modwg_ref,
-    gains_ref,
-    slots,
-    rows_s,
-    dmod_s,
-    cond_s,
-    emb_s,
-    sems,
-):
-    fetch(at_ref, own_ref, got_ref, slots, sems)
-    for h in range(2):
-        for n in range(8):
-            part = slots[h, pl.ds(n * 768, 768)]
-            rows_s[pl.ds(h * 6144 + n * 768, 768)] = part.astype(f32)
+        name="sum_layer",
+    )(at, a)
+
+
+def pick_lines(rows_ref, rows_s, here, dmod_ref, cond_ref, emb_ref, codes_ref, gains_ref):
+    for n in range(8):
+        rows_s[pl.ds(n * 768, 768)] = rows_ref[pl.ds(n * 768, 768)].astype(f32)
 
     def line(r):
-        return rows_s[pl.ds(r, 256, stride=48), :]
+        return rows_s[pl.ds(r, 128, stride=48), :]
 
     for i in range(2):
-        here = slice(i * 256, i * 256 + 256)
+        spot = pl.ds(pl.multiple_of(here + i * 128, 128), 128)
         for k in range(6):
             for b in range(3):
                 r = 24 + i * 6 + k * 3 + b if k < 2 else i * 12 + (k - 2) * 3 + b
                 at = k * 384 + b * 128
-                dmod_s[here, at : at + 128] = line(r).astype(bf16)
+                dmod_ref[spot, at : at + 128] = line(r).astype(bf16)
         for b in range(2):
-            emb_s[here, b * 128 : b * 128 + 128] = line(38 + i * 2 + b).astype(bf16)
+            emb_ref[spot, b * 128 : b * 128 + 128] = line(38 + i * 2 + b).astype(bf16)
         for b in range(3):
-            cond_s[here, b * 128 : b * 128 + 128] = line(42 + i * 3 + b)
+            cond_ref[spot, b * 128 : b * 128 + 128] = line(42 + i * 3 + b)
+        codes = line(37)
+        label = codes[:, i : i + 1] * 32.0 + codes[:, i + 2 : i + 3]
+        codes_ref[spot, :] = jnp.broadcast_to(label, (128, 128)).astype(jnp.int32)
     gains_ref[...] = jnp.sum(line(36), axis=0, keepdims=True)
-    codes = line(37)
-    labels = jnp.concatenate([codes[:, i : i + 1] * 32.0 + codes[:, i + 2 : i + 3] for i in range(2)])
+
+
+def lines(rows):
+    return [
+        ((rows, 2304), bf16),
+        ((rows, 384), f32),
+        ((rows, 256), bf16),
+        ((rows, 128), jnp.int32),
+    ]
+
+
+GAINS = ((1, 128), f32)
+
+
+def line_kernel(rows_ref, modw_ref, *refs):
+    outs, rows_s = refs[:5], refs[5]
+    pick_lines(rows_ref, rows_s, 0, *outs)
+
+
+def line_call(rows, mod_w):
+    return pl.pallas_call(
+        line_kernel,
+        in_specs=[RESIDENT] * 2,
+        out_shape=[shape_of(*o) for o in lines(256) + [GAINS]],
+        scratch_shapes=[pltpu.VMEM((6144, 128), f32)],
+        compiler_params=params(14),
+        cost_estimate=cost(100_000, 100_000),
+        name="image_lines",
+    )(rows, mod_w)
+
+
+CONDITIONS = [(256, 384), (384, 384), (1001, 384), (384, 2304), (1, 64), (1, 64)]
+
+
+def condition_kernel(at_ref, *refs):
+    own, got_ref, (tw1_ref, tw2_ref, modw_ref) = refs[:5], refs[5], refs[6:9]
+    stages = refs[9:15]
+    whole, gains_s, rows_s = refs[15:19], refs[19], refs[20]
+    tw1g, tw2g, tableg, modwg, qgain, kgain = stages
+    mine = pl.ds(pl.multiple_of(at_ref[1] * 256, 256), 256)
+    for ref, own_ref in zip(whole, own):
+        ref[mine, :] = own_ref[...]
+    pick_lines(got_ref, rows_s, (1 - at_ref[1]) * 256, *whole, gains_s)
+    dmod_s, cond_s, emb_s, label_s = whole
+    gain_sums = own[4][...] + gains_s[...]
+    qgain[...], kgain[...] = gain_sums[:, :64], gain_sums[:, 64:]
     cond = cond_s[...]
     sig = 1.0 / (1.0 + jnp.exp(-cond))
     act_t = (cond * sig).astype(bf16).T
     for k in range(6):
         cols = slice(k * 384, k * 384 + 384)
-        modwg_ref[:, cols] = dot(act_t, dmod_s[:, cols])
+        modwg[:, cols] = dot(act_t, dmod_s[:, cols])
     d_cond = dot_nt(dmod_s[...], modw_ref[...]) * (sig + cond * sig * (1.0 - sig))
     dc = d_cond.astype(bf16)
-    labels = labels.astype(jnp.int32)
+    label = label_s[...]
+    label = jnp.concatenate([label, label], axis=1)
     for n in range(4):
-        hot = jnp.where(lane_iota((512, 256)) + n * 256 == labels, 1.0, 0.0).astype(bf16)
+        hot = jnp.where(lane_iota((512, 256)) + n * 256 == label, 1.0, 0.0).astype(bf16)
         rows = dot_tn(hot, dc)
         top = min(256, 1001 - n * 256)
-        tableg_ref[n * 256 : n * 256 + top] = rows[:top]
+        tableg[n * 256 : n * 256 + top] = rows[:top]
     emb = emb_s[...]
     pre = dot(emb, tw1_ref[...])
     sig = 1.0 / (1.0 + jnp.exp(-pre))
     hid = pre * sig
-    tw2g_ref[...] = dot_tn(hid.astype(bf16), dc)
+    tw2g[...] = dot_tn(hid.astype(bf16), dc)
     d_pre = (dot_nt(dc, tw2_ref[...]) * (sig + hid * (1.0 - sig))).astype(bf16)
-    tw1g_ref[...] = dot_tn(emb, d_pre)
+    tw1g[...] = dot_tn(emb, d_pre)
 
 
 def condition_call(at, own, got, t_w1, t_w2, mod_w):
-    anywhere = pl.BlockSpec(memory_space=pl.ANY)
-    shapes = [(256, 384), (384, 384), (1001, 384), (384, 2304), (1, 128)]
     return pl.pallas_call(
         condition_kernel,
+        grid=(1,),
+        in_specs=[SCALARS] + [RESIDENT] * 9,
+        out_specs=[whole_spec(v) for v in CONDITIONS],
+        out_shape=[shape_of(s, f32) for s in CONDITIONS],
+        scratch_shapes=[pltpu.VMEM(*o) for o in lines(512) + [GAINS, ((6144, 128), f32)]],
+        compiler_params=params(36),
+        cost_estimate=cost(100_000_000, 100_000),
+        name="condition_gradients",
+    )(at, *own, got, t_w1, t_w2, mod_w)
+
+
+def place_kernel(at_ref, swaps_ref, out_in, grad_in, out_ref, grad_ref):
+    out_ref[...] = swaps_ref[:, 0]
+    grad_ref[...] = swaps_ref[:, 1].astype(f32)
+
+
+def place_call(at, swaps, block_out, latents_grad):
+    anywhere = pl.BlockSpec(memory_space=pl.ANY)
+    theirs = pl.BlockSpec((2, 128, 384), lambda j, at: (1 - at[0], 0, 0))
+    return pl.pallas_call(
+        place_kernel,
         grid_spec=pltpu.PrefetchScalarGridSpec(
             num_scalar_prefetch=1,
             grid=(1,),
-            in_specs=[anywhere, anywhere]
-            + [whole_spec(s) for s in ((256, 384), (384, 384), (384, 2304))],
-            out_specs=[whole_spec(s) for s in shapes],
-            scratch_shapes=[
-                pltpu.VMEM((2, 6144, 128), bf16),
-                pltpu.VMEM((12288, 128), f32),
-                pltpu.VMEM((512, 2304), bf16),
-                pltpu.VMEM((512, 384), f32),
-                pltpu.VMEM((512, 256), bf16),
-                pltpu.SemaphoreType.DMA((2,)),
-            ],
+            in_specs=[whole_spec((2, 2, 128, 384)), anywhere, anywhere],
+            out_specs=[theirs, theirs],
         ),
-        out_shape=[shape_of(s, f32) for s in shapes],
-        compiler_params=params(36),
-        cost_estimate=cost(100_000_000, 100_000),
-        name="condition_gradients",
-    )(at, own, got, t_w1, t_w2, mod_w)
+        out_shape=[shape_of((4, 128, 384), bf16), shape_of((4, 128, 384), f32)],
+        input_output_aliases={2: 0, 3: 1},
+        compiler_params=params(8),
+        cost_estimate=cost(200_000, 1_500_000),
+        name="place_swaps",
+    )(at, swaps, block_out, latents_grad)
 
 
 def cuts(start, chunk):
@@ -674,43 +722,52 @@
 
 
 def unpack_kernel(own, at_ref, sums_ref, *refs):
-    qkv_ref, proj_ref, gu_ref, down_ref = refs[-4:]
+    qkv_ref, proj_ref, gu_ref, down_ref, proj_s, sem = refs[-6:]
     t = pl.program_id(0)
     half = at_ref[1] if own else 1 - at_ref[1]
 
+    def piece(n, a, b):
+        low = [sums_ref[n, a : min(b, 224)]] if a < 224 else []
+        return low + ([sums_ref[16 + n, max(a, 224) - 224 : b - 224]] if b > 224 else [])
+
     def first(u):
-        rows = [sums_ref[n, a:b] for n, a, b in cuts(u * 384, 288)]
+        rows = [v for n, a, b in cuts(u * 384, 288) for v in piece(n, a, b)]
         return jnp.concatenate(rows).astype(f32)
 
     def second(u):
-        rows = [sums_ref[n, 288 + a : 288 + b] for n, a, b in cuts(u * 384, 144)]
+        rows = [v for n, a, b in cuts(u * 384, 144) for v in piece(n, 288 + a, 288 + b)]
         return jnp.concatenate(rows).astype(f32)
+
+    proj_copy = pltpu.make_async_copy(proj_s, proj_ref, sem)
+    for n in range(4):
+
+        @pl.when(t == n)
+        def _():
+            for b in range(2):
+                gu_ref[:, b * 128 : b * 128 + 128] = first(2 * n + b)
+            rows = first(8 + n)
+            for b, p in enumerate(pairs()):
+                down_ref[:, p] = rows[b * 128 : b * 128 + 128]
+
+    @pl.when((t == 0) & (half == 1))
+    def _():
+        for b, p in enumerate(pairs()):
+            proj_s[:, p] = second(3 + b)
+        proj_copy.start()
 
     @pl.when(t == 0)
     def _():
-        for b in range(4):
-            gu_ref[:, b * 128 : b * 128 + 128] = first(b)
         for b, p in enumerate(pairs()):
             qkv_ref[:, p] = second(b)
 
-    @pl.when(t == 1)
+    @pl.when((t == 2) & (half == 0))
     def _():
-        for n in range(4):
-            gu_ref[:, n * 128 : n * 128 + 128] = first(4 + n)
-            rows = first(8 + n)
-            for b, p in enumerate(pairs()):
-                down_ref[n * 128 : n * 128 + 128, p] = rows[b * 128 : b * 128 + 128]
-
-        @pl.when(half == 0)
-        def _():
-            for b, p in enumerate(pairs()):
-                qkv_ref[:, p] = second(3 + b)
-            proj_ref[...] = jnp.zeros((384, 384), f32) if own else refs[0][...]
-
-        @pl.when(half == 1)
-        def _():
-            for b, p in enumerate(pairs()):
-                proj_ref[:, p] = second(3 + b)
+        for b, p in enumerate(pairs()):
+            qkv_ref[:, p] = second(3 + b)
+
+    @pl.when((t == 3) & (half == 1))
+    def _():
+        proj_copy.wait()
 
 
 def unpack_call(own, at, sums, earlier=()):
@@ -718,24 +775,26 @@
         return at[1] if own else 1 - at[1]
 
     shapes = [(384, 1152), (384, 384), (384, 2048), (1024, 384)]
-    anywhere = pl.BlockSpec(memory_space=pl.ANY)
-    kept = [whole_spec((384, 384))] + [anywhere] * 3 if earlier else []
-    earlier = [earlier[n] for n in (1, 0, 2, 3)] if earlier else []
     return pl.pallas_call(
         lambda *refs: unpack_kernel(own, *refs),
         grid_spec=pltpu.PrefetchScalarGridSpec(
             num_scalar_prefetch=1,
-            grid=(2,),
-            in_specs=[RESIDENT] + kept,
+            grid=(4,),
+            in_specs=[RESIDENT] + [pl.BlockSpec(memory_space=pl.ANY)] * len(earlier),
             out_specs=[
-                pl.BlockSpec((384, 384), lambda t, at: (0, half_of(at) * (2 - t) + t)),
-                whole_spec((384, 384)),
-                pl.BlockSpec((384, 512), lambda t, at: (0, 2 * t + half_of(at))),
-                pl.BlockSpec((512, 384), lambda t, at: (half_of(at), 0)),
+                pl.BlockSpec(
+                    (384, 384), lambda t, at: (0, half_of(at) * 2 + (1 - half_of(at)) * (t >> 1))
+                ),
+                IN_HBM,
+                pl.BlockSpec(
+                    (384, 256), lambda t, at: (0, 4 * (t >> 1) + 2 * half_of(at) + (t & 1))
+                ),
+                pl.BlockSpec((128, 384), lambda t, at: (4 * half_of(at) + t, 0)),
             ],
+            scratch_shapes=[pltpu.VMEM((384, 384), f32), pltpu.SemaphoreType.DMA],
         ),
         out_shape=[shape_of(s, f32) for s in shapes],
-        input_output_aliases={2: 1, 3: 0, 4: 2, 5: 3} if earlier else {},
+        input_output_aliases={2 + n: n for n in range(len(earlier))},
         compiler_params=params(20),
         cost_estimate=cost(2_000_000, 6_000_000),
         name="unpack_own" if own else "unpack_other",
@@ -746,25 +805,41 @@
     return ((((y * 8 + z) * 2 + x % 2) * 2 + c) * 2) + x // 2
 
 
-def groups(axes):
-    rest = [a for a in "yzxc" if a not in axes]
-    out = []
-    for fixed in itertools.product(*[range(SIZES[a]) for a in rest]):
-        place = dict(zip(rest, fixed))
-        row = []
-        for moving in itertools.product(*[range(SIZES[a]) for a in axes]):
-            row.append(flat(**{**place, **dict(zip(axes, moving))}))
-        out.append(row)
-    return out
-
-
-def exchange(v, axes):
-    return lax.all_to_all(v, AXES, 0, 0, tiled=True, axis_index_groups=groups(axes))
-
-
-def gather(v, axes):
-    n = math.prod(SIZES[a] for a in axes)
-    return exchange(jnp.broadcast_to(v[None], (n,) + v.shape), axes)
+PLACES = [(y, z, x, c) for z, y, x, c in itertools.product(range(8), range(4), range(4), range(2))]
+
+
+def groups(key):
+    found = {}
+    for place in PLACES:
+        found.setdefault(key(*place), []).append(flat(*place))
+    return list(found.values())
+
+
+PLANE = groups(lambda y, z, x, c: (z // 2, c))
+LAYER = groups(lambda y, z, x, c: (z, c))
+RING = groups(lambda y, z, x, c: (y, x, c))
+
+
+def moves(to):
+    return [(flat(*place), flat(*to(*place))) for place in PLACES]
+
+
+def exchange(v, lists):
+    return lax.all_to_all(v, AXES, 0, 0, tiled=True, axis_index_groups=lists)
+
+
+def plus(a, b):
+    return (a.astype(f32) + b.astype(f32)).astype(bf16)
+
+
+def column_sum(keep, send):
+    v = plus(keep, lax.ppermute(send, AXES, moves(lambda y, z, x, c: (y, z ^ 1, x, c))))
+    for to in (
+        lambda y, z, x, c: (y, z ^ 2, x, c),
+        lambda y, z, x, c: (y, (6 - (z & 6)) + (z & 1), x, c),
+    ):
+        v = plus(v, lax.ppermute(v, AXES, moves(to)))
+    return v
 
 
 BAND_SWAP = [(n, n ^ 1) for n in range(256)]
@@ -797,14 +872,11 @@
     down_w,
     out_grad,
 ):
-    band = lax.axis_index("band")
-    core = lax.axis_index("img") % 2
-    at = jnp.stack([band, core]).astype(jnp.int32)
+    band, img = lax.axis_index("band"), lax.axis_index("img")
+    at = jnp.stack([band, img % 2, img // 4 % 2]).astype(jnp.int32)
     send, dsend = pack_call(at, latents, out_grad, pos_row, pos_col)
-    got = swap(send)
+    got, dgot = swap(send), swap(dsend)
     mod, extra = modulation_call(at, timesteps, labels, t_w1, t_w2, label_table, mod_w)
-    mod, dsend = lax.optimization_barrier((mod, dsend))
-    dgot = swap(dsend)
     turn = (q_gain.reshape(1, 64), k_gain.reshape(1, 64), pos_row, pos_col, turn_table())
     q, k, v, att = forward_call(at, latents, got, mod, qkv_w, *turn)
     keep1, send1, block_out, out_send, d_mid, sums1 = mlp_call(
@@ -815,24 +887,25 @@
         at, latents, got, mod, qkv_w, *turn, q, k, v, att, d_mid, proj_w, out_send
     )
     joined = join_call(keep1, got1, keep2, core_swap(send2), sums1, sums2, extra)
-    chunk, extra = sum_call(exchange(joined, "xy"))
+    joined = exchange(joined, LAYER)
+    joined, extra = lax.optimization_barrier((joined, extra_call(joined)))
+    keep, send = sum_call(at, joined)
     extra = lax.all_gather(
-        extra.reshape(768, 128), AXES, axis=0, tiled=True, axis_index_groups=groups("z")
+        extra.reshape(768, 128), AXES, axis=0, tiled=True, axis_index_groups=RING
     )
-    chunk = jnp.sum(exchange(chunk.reshape(8, 56, 128), "z").astype(f32), axis=0).astype(bf16)
-    chunk = gather(chunk, "z").reshape(448, 128)
+    chunk = column_sum(keep, send)
     chunk, swaps = lax.optimization_barrier((chunk, swap(swaps)))
-    wide = lax.optimization_barrier(jnp.broadcast_to(chunk[None], (16, 448, 128)))
-    summed = exchange(wide, "xy")
-    extra, _ = lax.optimization_barrier((extra, wide))
-    conditioned = condition_call(at, extra, core_swap(extra), t_w1, t_w2, mod_w)
+    wide = lax.optimization_barrier(jnp.broadcast_to(chunk[None], (32, 224, 128)))
+    summed = exchange(wide, PLANE)
+    block_out, latents_grad = place_call(at, swaps, block_out, latents_grad)
+    extra, block_out, latents_grad, _ = lax.optimization_barrier(
+        (extra, block_out, latents_grad, wide)
+    )
+    conditioned = condition_call(at, line_call(extra, mod_w), core_swap(extra), t_w1, t_w2, mod_w)
     summed, conditioned = lax.optimization_barrier((summed, conditioned))
-    tw1_grad, tw2_grad, table_grad, modw_grad, gain_sums = conditioned
+    tw1_grad, tw2_grad, table_grad, modw_grad, q_sum, k_sum = conditioned
     sums = unpack_call(True, at, summed)
     qkv_sum, proj_sum, gu_sum, down_sum = unpack_call(False, at, core_swap(summed), sums)
-    other = 2 - 2 * band
-    block_out = lax.dynamic_update_slice_in_dim(block_out, swaps[:, 0], other, 0)
-    latents_grad = lax.dynamic_update_slice_in_dim(latents_grad, swaps[:, 1].astype(f32), other, 0)
     return (
         block_out,
         latents_grad,
@@ -841,8 +914,8 @@
         table_grad,
         modw_grad,
         qkv_sum,
-        gain_sums[0, :64],
-        gain_sums[0, 64:],
+        q_sum.reshape(64),
+        k_sum.reshape(64),
         proj_sum,
         gu_sum,
         down_sum,

time: 154 us -> 149 us (0.968)
  Pallas kernels: 39.7 us -> 43.8 us
  local copies, waits for them, and re-layouts: 7.23 us -> 3.68 us
  waiting for transfers between devices: 27.7 us -> 24.9 us
  starting transfers between devices: 32.1 us -> 30 us
    all_to_all x3 -> x1, waiting for transfers between devices: 15.4 us -> 0.01 us  [exchange(): return lax.all_to_all(v, AXES, 0, 0, tiled=True, axis_index_groups=lists)]
    all_gather x1, waiting for transfers between devices: 4.29 us -> 17.6 us  [body(): lax.all_gather(extra.reshape(768, 128), AXES, axis=0, tiled=True, axis_in...]
    ppermute x0 -> x3, starting transfers between devices: none -> 10.2 us  [the longest x2 8.48 us: column_sum(): v = plus(v, lax.ppermute(v, AXES, moves(to)))]
    all_to_all x3 -> x1, starting transfers between devices: 15.4 us -> 5.34 us  [exchange(): return lax.all_to_all(v, AXES, 0, 0, tiled=True, axis_index_groups=lists)]
    ppermute x0 -> x3, waiting for transfers between devices: none -> 3.78 us  [the longest x2 2.24 us: column_sum(): v = plus(v, lax.ppermute(v, AXES, moves(to)))]
    pallas_call x2 -> x5, Pallas kernels: 8.56 us -> 11.8 us  [the longest x1 7.48 us: condition_call(): pl.pallas_call(condition_kernel, grid=(1,), in_specs=[SCALARS] + [RESIDEN...]
    ppermute x4, waiting for transfers between devices: 5.21 us -> 2.48 us  [core_swap(): return lax.ppermute(v, AXES, CORE_SWAP)]
    ppermute x4, starting transfers between devices: 11.6 us -> 9.52 us  [core_swap(): return lax.ppermute(v, AXES, CORE_SWAP)]
  transfers between devices with their start and end apart: 11 -> 12, of which waited for: 7 -> 9; matrix products, arithmetic and copies ran while one was open for 2% -> 1% of each run, Pallas kernels for 16% -> 20%
where the time goes in v3:
time: 149 us
  Pallas kernels  43.8 us (29%)
  blocking collectives  31.6 us (21%)
  starting transfers between devices  30 us (20%)
  waiting for transfers between devices  24.9 us (17%)
  between operations  14.3 us (10%)
  local copies, waits for them, and re-layouts  3.68 us (2%)
    all_to_all x1, blocking collectives, exchange(): return lax.all_to_all(v, AXES, 0, 0, tiled=True, axis_index_groups=lists)  31.6 us
    all_gather x1, waiting for transfers between devices, body(): lax.all_gather(extra.reshape(768, 128), AXES, axis=0, tiled=True, axis_in...  17.6 us
    pallas_call x3, Pallas kernels, call(): pl.pallas_call(kernel, grid=(1,), in_specs=[SCALARS] + [spec(n in loose,...  17.2 us
    ppermute x4, starting transfers between devices, core_swap(): return lax.ppermute(v, AXES, CORE_SWAP)  9.52 us
    ppermute x2, starting transfers between devices, column_sum(): v = plus(v, lax.ppermute(v, AXES, moves(to)))  8.48 us
    pallas_call x1, Pallas kernels, condition_call(): pl.pallas_call(condition_kernel, grid=(1,), in_specs=[SCALARS] + [RESIDEN...  7.48 us
    pallas_call x2, Pallas kernels, unpack_call(): pl.pallas_call(lambda *refs: unpack_kernel(own, *refs), grid_spec=pltpu.P...  7.48 us
    all_to_all x1, starting transfers between devices, exchange(): return lax.all_to_all(v, AXES, 0, 0, tiled=True, axis_index_groups=lists)  5.34 us
  transfers between devices with their start and end apart: 12, of which 9 were waited for; matrix products, arithmetic and copies ran while one was open for 1% of the time, Pallas kernels for 20%

profile of v3, /device:TPU:1, one launch (start us, length us, event | category | flops | bytes accessed | tf_op | source)
XLA Modules:
  0.0 148.8 jit_solution(6331911477998413866)
XLA Ops:
  7.8 2.5 %pack_swaps.1 = (bf16[2,144,384]{2,1,0:T(8,128)(2,1)}, bf16[2,128,384]{2,1,0:T(8,128)(2,1)}) custom-call(s32[3]{0:T(128)} %pad_add_fusion.at_ref.refs_0_, bf16[4,128,384]{2,1,0:T(8,128)(2,1)} %kept_ref.5, bf16[4,128,384]{2,1,0:T(8,128)(2,1)} %dkept_ref.1, s32[4,128]{1,0:T(4,128)} %row_ref.5, s32[4,128]{1,0:T(4,128)} %col_ref.5), custom_call_target="tpu_custom_call" | custom-call | flops 200000 | bytes 800000 | tf_op jit(solution)/shard_map/pack_swaps/pallas_call | solution.py:408
  10.3 3.6 %collective-permute-start = (bf16[2,144,384]{2,1,0:T(8,128)(2,1)}, bf16[2,144,384]{2,1,0:T(8,128)(2,1)S(1)}, u32[]{:S(2)}, u32[]{:S(2)}) collective-permute-start(bf16[2,144,384]{2,1,0:T(8,128)(2,1)} %get-tuple-element.68), channel_id=1, source_target_pairs={{0,1},{1,0},{2,3},{3,2},{4,5},{5,4},{6,7},{7,6},{8,9},{9,8},{10,11... | collective-permute-start | bytes 663560 | tf_op jit(solution)/shard_map/ppermute | solution.py:850
  14.1 3.9 %modulation.1 = (f32[2,6,384]{2,1,0:T(8,128)}, f32[16,128]{1,0:T(8,128)}) custom-call(s32[3]{0:T(128)} %pad_add_fusion.at_ref.refs_0_, s32[4]{0:T(128)} %t_ref.1, s32[4]{0:T(128)} %l_ref.1, bf16[256,384]{1,0:T(8,128)(2,1)} %refs_6_.1, bf16[384,384]{1,0:T(8,128)(2,1)} %refs_7_.1, bf16[1001,384]{1,0:T(8,128)(2,1)} %row1_ref.1, bf16[1001,384]{1,0:T(8,128)(2,1)} %row1_ref.1, ...), custom_call_target="tpu_custom_call" | custom-call | flops 1000000000 | bytes 3000000 | tf_op jit(solution)/shard_map/modulation/pallas_call | solution.py:428
  19.1 3.3 %attention_forward.1 = (bf16[2,256,384]{2,1,0:T(8,128)(2,1)S(1)}, bf16[2,256,384]{2,1,0:T(8,128)(2,1)S(1)}, bf16[2,256,384]{2,1,0:T(8,128)(2,1)S(1)}, bf16[512,384]{1,0:T(8,128)(2,1)S(1)}) custom-call(s32[3]{0:T(128)S(1)} %copy-done.6, bf16[4,128,384]{2,1,0:T(8,128)(2,1)S(1)} %copy-done.5, bf16[2,144,384]{2,1,0:T(8,128)(2,1)S(1)} %collective-permute-done.got_ref, ...), custom_call_target="tpu_custom_call" | custom-call | flops 3000000000 | bytes 4000000 | tf_op jit(solution)/shard_map/attention_forward/pallas_call | solution.py:454
  22.7 6.1 %mlp_both_ways.1 = (bf16[4608,128]{1,0:T(8,128)(2,1)S(1)}, bf16[4608,128]{1,0:T(8,128)(2,1)S(1)}, bf16[4,128,384]{2,1,0:T(8,128)(2,1)}, bf16[2,128,384]{2,1,0:T(...) custom-call(s32[3]{0:T(128)S(1)} %copy-done.6, bf16[4,128,384]{2,1,0:T(8,128)(2,1)S(1)} %copy-done.5, ...), custom_call_target="tpu_custom_call" | custom-call | flops 6000000000 | bytes 8000000 | tf_op jit(solution)/shard_map/mlp_both_ways/pallas_call | solution.py:454
  28.8 5.1 %collective-permute-start.2 = (bf16[4608,128]{1,0:T(8,128)(2,1)S(1)}, bf16[4608,128]{1,0:T(8,128)(2,1)S(1)}, u32[]{:S(2)}, u32[]{:S(2)}) collective-permute-start(bf16[4608,128]{1,0:T(8,128)(2,1)S(1)} %get-tuple-element.73), channel_id=1, source_target_pairs={{0,2},{1,3},{2,0},{3,1},{4,6},{5,7},{6,4},{7,5},{8,10},{9,11},{10,... | collective-permute-start | bytes 3538952 | tf_op jit(solution)/shard_map/ppermute | solution.py:854
  33.8 7.8 %attention_backward.1 = (bf16[2304,128]{1,0:T(8,128)(2,1)S(1)}, bf16[2304,128]{1,0:T(8,128)(2,1)S(1)}, f32[4,128,384]{2,1,0:T(8,128)}, bf16[2,2,128,384]{3,2,1,0:T(8,128)(2,1)S(1)}, f32[16,128]{1,0:T(8,128)S(1)}) custom-call(s32[3]{0:T(128)S(1)} %copy-done.6, bf16[4,128,384]{2,1,0:T(8,128)(2,1)S(1)} %copy-done.5, ...), custom_call_target="tpu_custom_call" | custom-call | flops 5000000000 | bytes 6000000 | tf_op jit(solution)/shard_map/attention_backward/pallas_call | solution.py:454
  41.7 2.0 %collective-permute-done.3 = bf16[2304,128]{1,0:T(8,128)(2,1)S(1)} collective-permute-done((bf16[2304,128]{1,0:T(8,128)(2,1)S(1)}, bf16[2304,128]{1,0:T(8,128)(2,1)S(1)}, u32[]{:S(2)}, u32[]{:S(2)}) %collective-permute-start.3) | collective-permute-done | bytes 589856 | tf_op jit(solution)/shard_map/ppermute | solution.py:854
  44.6 31.6 %all_to_all.10.a_ref = bf16[16,480,128]{2,1,0:T(8,128)(2,1)S(1)} all-to-all(bf16[16,480,128]{2,1,0:T(8,128)(2,1)S(1)} %join_messages.1), channel_id=1, replica_groups={{0,4,1,5,64,68,65,69,128,132,129,133,192,196,193,197},{2,6,3,7,66,70,67..., dimensions={0} | all-to-all | bytes 3932160 | tf_op jit(solution)/shard_map/all_to_all | solution.py:828
  77.8 1.7 %collective-permute-start.4 = (bf16[224,128]{1,0:T(8,128)(2,1)S(1)}, bf16[224,128]{1,0:T(8,128)(2,1)S(1)}, u32[]{:S(2)}, u32[]{:S(2)}) collective-permute-start(bf16[224,128]{1,0:T(8,128)(2,1)S(1)} %get-tuple-element.87), channel_id=1, source_target_pairs={{0,8},{2,10},{4,12},{6,14},{1,9},{3,11},{5,13},{7,15},{64,72},{66,... | collective-permute-start | bytes 172040 | tf_op jit(solution)/shard_map/ppermute | solution.py:836
  79.5 1.5 %collective-permute-done.4 = bf16[224,128]{1,0:T(8,128)(2,1)S(1)} collective-permute-done((bf16[224,128]{1,0:T(8,128)(2,1)S(1)}, bf16[224,128]{1,0:T(8,128)(2,1)S(1)}, u32[]{:S(2)}, u32[]{:S(2)}) %collective-permute-start.4) | collective-permute-done | bytes 57376 | tf_op jit(solution)/shard_map/ppermute | solution.py:836
  81.1 3.1 %collective-permute-start.5 = (bf16[224,128]{1,0:T(8,128)(2,1)S(1)}, bf16[224,128]{1,0:T(8,128)(2,1)S(1)}, u32[]{:S(2)}, u32[]{:S(2)}) collective-permute-start(bf16[224,128]{1,0:T(8,128)(2,1)S(1)} %add_convert_fusion.2), channel_id=1, source_target_pairs={{0,16},{2,18},{4,20},{6,22},{1,17},{3,19},{5,21},{7,23},{64,80},{6... | collective-permute-start | bytes 172040 | tf_op jit(solution)/shard_map/ppermute | solution.py:841
  85.7 5.4 %collective-permute-start.6 = (bf16[224,128]{1,0:T(8,128)(2,1)S(1)}, bf16[224,128]{1,0:T(8,128)(2,1)S(1)}, u32[]{:S(2)}, u32[]{:S(2)}) collective-permute-start(bf16[224,128]{1,0:T(8,128)(2,1)S(1)} %add_convert_fusion.1), channel_id=1, source_target_pairs={{0,48},{2,50},{4,52},{6,54},{1,49},{3,51},{5,53},{7,55},{64,112},{... | collective-permute-start | bytes 172040 | tf_op jit(solution)/shard_map/ppermute | solution.py:841
  91.1 1.9 %collective-permute-done.6 = bf16[224,128]{1,0:T(8,128)(2,1)S(1)} collective-permute-done((bf16[224,128]{1,0:T(8,128)(2,1)S(1)}, bf16[224,128]{1,0:T(8,128)(2,1)S(1)}, u32[]{:S(2)}, u32[]{:S(2)}) %collective-permute-start.6) | collective-permute-done | bytes 57376 | tf_op jit(solution)/shard_map/ppermute | solution.py:841
  93.4 1.5 broadcast_in_dim.2
  94.9 5.3 %all-to-all-start.1 = ((bf16[32,224,128]{2,1,0:T(8,128)(2,1)}), bf16[32,224,128]{2,1,0:T(8,128)(2,1)}, u32[]{:S(2)}, u32[]{:S(2)}) async-start(bf16[32,224,128]{2,1,0:T(8,128)(2,1)} %broadcast_in_dim.2), calls=%async_computation.1 | async-start | bytes 3670016 | tf_op jit(solution)/shard_map/all_to_all | solution.py:828
  100.3 1.4 place_swaps.1
  101.7 17.6 %all-gather.2.cloned.1.call-done.rows_ref = bf16[6144,128]{1,0:T(8,128)(2,1)} async-done(((bf16[768,128]{1,0:T(8,128)(2,1)}), bf16[6144,128]{1,0:T(8,128)(2,1)}) %all-gather.2.cloned.1.call-update) | async-done | bytes 1572880 | tf_op jit(solution)/shard_map/all_gather | solution.py:893
  119.3 2.9 %collective-permute-start.8 = (bf16[6144,128]{1,0:T(8,128)(2,1)}, bf16[6144,128]{1,0:T(8,128)(2,1)S(1)}, u32[]{:S(2)}, u32[]{:S(2)}) collective-permute-start(bf16[6144,128]{1,0:T(8,128)(2,1)} %all-gather.2.cloned.1.call-done.rows_ref), channel_id=1, source_target_pairs={{0,2},{1,3},{2,0},{3,1},{4,6},{5,7},{6,4},{7,5},{8,10},{9,11},{10,... | collective-permute-start | bytes 4718600 | tf_op jit(solution)/shard_map/ppermute | solution.py:854
  122.2 1.4 copy-done.1
  125.4 7.5 %condition_gradients.1 = (f32[256,384]{1,0:T(8,128)}, f32[384,384]{1,0:T(8,128)}, f32[1001,384]{1,0:T(8,128)}, f32[384,2304]{1,0:T(8,128)}, f32[1,64]{1,0:T(1,128)}, /*index=5*/f32[1,64]{1,0:T(1,128)}) custom-call(s32[3]{0:T(128)S(1)} %copy-done.6, bf16[256,2304]{1,0:T(8,128)(2,1)S(1)} %get-tuple-element.98.refs_0_, ...), custom_call_target="tpu_custom_call" | custom-call | flops 100000000 | bytes 100000 | tf_op jit(solution)/shard_map/condition_gradients/pallas_call | solution.py:677
  132.9 1.5 %collective-permute-start.9 = (bf16[32,224,128]{2,1,0:T(8,128)(2,1)}, bf16[32,224,128]{2,1,0:T(8,128)(2,1)S(1)}, u32[]{:S(2)}, u32[]{:S(2)}) collective-permute-start(bf16[32,224,128]{2,1,0:T(8,128)(2,1)} %all-to-all-done.1.refs_1_), channel_id=1, source_target_pairs={{0,2},{1,3},{2,0},{3,1},{4,6},{5,7},{6,4},{7,5},{8,10},{9,11},{10,... | collective-permute-start | bytes 5505032 | tf_op jit(solution)/shard_map/ppermute | solution.py:854
  134.4 4.5 %unpack_own.1 = (f32[384,1152]{1,0:T(8,128)}, f32[384,384]{1,0:T(8,128)}, f32[384,2048]{1,0:T(8,128)}, f32[1024,384]{1,0:T(8,128)}) custom-call(s32[3]{0:T(128)S(1)} %copy-done.6, bf16[32,224,128]{2,1,0:T(8,128)(2,1)} %all-to-all-done.1.refs_1_), custom_call_target="tpu_custom_call" | custom-call | flops 2000000 | bytes 6000000 | tf_op jit(solution)/shard_map/unpack_own/pallas_call | solution.py:778
  138.9 3.0 %unpack_other.1 = (f32[384,1152]{1,0:T(8,128)}, f32[384,384]{1,0:T(8,128)}, f32[384,2048]{1,0:T(8,128)}, f32[1024,384]{1,0:T(8,128)}) custom-call(s32[3]{0:T(128)S(1)} %copy-done.6, bf16[32,224,128]{2,1,0:T(8,128)(2,1)S(1)} %collective-permute-done.9.refs_1_, ...), custom_call_target="tpu_custom_call", output_to_operand_aliasing={{0}: (2, {}), {1}: (3, {}), {2}: (4, {}), {3}: (5, {})} | custom-call | flops 2000000 | bytes 6000000 | tf_op jit(solution)/shard_map/unpack_other/pallas_call | solution.py:778
  (56 shorter events, 8.5 us)
Async XLA Ops:
  7.2 112.1 %all-gather.2.cloned.1.call-start = ((), (), s32[]{:S(2)}) async-start(), calls=%async_computation.2 | async-start | bytes 1769472 | tf_op jit(solution)/shard_map/all_gather | solution.py:893
  10.3 8.0 %collective-permute-start = (bf16[2,144,384]{2,1,0:T(8,128)(2,1)}, bf16[2,144,384]{2,1,0:T(8,128)(2,1)S(1)}, u32[]{:S(2)}, u32[]{:S(2)}) collective-permute-start(bf16[2,144,384]{2,1,0:T(8,128)(2,1)} %get-tuple-element.68), channel_id=1, source_target_pairs={{0,1},{1,0},{2,3},{3,2},{4,5},{5,4},{6,7},{7,6},{8,9},{9,8},{10,11... | collective-permute-start | bytes 663560 | tf_op jit(solution)/shard_map/ppermute | solution.py:850
  13.9 4.4 %copy-start.5 = (bf16[4,128,384]{2,1,0:T(8,128)(2,1)S(1)}, bf16[4,128,384]{2,1,0:T(8,128)(2,1)}, u32[]{:S(2)}) copy-start(bf16[4,128,384]{2,1,0:T(8,128)(2,1)} %kept_ref.5) | copy-start | bytes 1179652
  13.9 4.4 %copy-start.6 = (s32[3]{0:T(128)S(1)}, s32[3]{0:T(128)}, u32[]{:S(2)}) copy-start(s32[3]{0:T(128)} %pad_add_fusion.at_ref.refs_0_) | copy-start | bytes 40
  13.9 4.4 %copy-start.8 = (s32[4,128]{1,0:T(4,128)S(1)}, s32[4,128]{1,0:T(4,128)}, u32[]{:S(2)}) copy-start(s32[4,128]{1,0:T(4,128)} %row_ref.5) | copy-start | bytes 6148
  13.9 4.4 %copy-start.9 = (s32[4,128]{1,0:T(4,128)S(1)}, s32[4,128]{1,0:T(4,128)}, u32[]{:S(2)}) copy-start(s32[4,128]{1,0:T(4,128)} %col_ref.5) | copy-start | bytes 6148
  13.9 4.4 %copy-start.11 = (bf16[384,1152]{1,0:T(8,128)(2,1)S(1)}, bf16[384,1152]{1,0:T(8,128)(2,1)}, u32[]{:S(2)}) copy-start(bf16[384,1152]{1,0:T(8,128)(2,1)} %w_ref.3) | copy-start | bytes 2654212
  13.9 4.4 %copy-start.15 = (f32[64]{0:T(128)S(1)}, f32[64]{0:T(128)}, u32[]{:S(2)}) copy-start(f32[64]{0:T(128)} %param.27) | copy-start | bytes 772
  13.9 4.4 %copy-start.16 = (f32[64]{0:T(128)S(1)}, f32[64]{0:T(128)}, u32[]{:S(2)}) copy-start(f32[64]{0:T(128)} %param.28) | copy-start | bytes 772
  13.9 4.4 %copy-start.17 = (bf16[4,32,128]{2,1,0:T(8,128)(2,1)S(1)}, bf16[4,32,128]{2,1,0:T(8,128)(2,1)}, u32[]{:S(2)}) copy-start(bf16[4,32,128]{2,1,0:T(8,128)(2,1)} %constant.40.clone.table_ref) | copy-start | bytes 98308
  14.0 8.7 %collective-permute-start.1 = (bf16[2,128,384]{2,1,0:T(8,128)(2,1)}, bf16[2,128,384]{2,1,0:T(8,128)(2,1)S(1)}, u32[]{:S(2)}, u32[]{:S(2)}) collective-permute-start(bf16[2,128,384]{2,1,0:T(8,128)(2,1)} %get-tuple-element.69), channel_id=1, source_target_pairs={{0,1},{1,0},{2,3},{3,2},{4,5},{5,4},{6,7},{7,6},{8,9},{9,8},{10,11... | collective-permute-start | bytes 589832 | tf_op jit(solution)/shard_map/ppermute | solution.py:850
  28.8 14.9 %collective-permute-start.2 = (bf16[4608,128]{1,0:T(8,128)(2,1)S(1)}, bf16[4608,128]{1,0:T(8,128)(2,1)S(1)}, u32[]{:S(2)}, u32[]{:S(2)}) collective-permute-start(bf16[4608,128]{1,0:T(8,128)(2,1)S(1)} %get-tuple-element.73), channel_id=1, source_target_pairs={{0,2},{1,3},{2,0},{3,1},{4,6},{5,7},{6,4},{7,5},{8,10},{9,11},{10,... | collective-permute-start | bytes 3538952 | tf_op jit(solution)/shard_map/ppermute | solution.py:854
  33.8 9.8 %copy-start.7 = (f32[16,128]{1,0:T(8,128)S(1)}, f32[16,128]{1,0:T(8,128)}, u32[]{:S(2)}) copy-start(f32[16,128]{1,0:T(8,128)} %get-tuple-element.83.extra_ref) | copy-start | bytes 24580
  41.7 2.0 %collective-permute-start.3 = (bf16[2304,128]{1,0:T(8,128)(2,1)S(1)}, bf16[2304,128]{1,0:T(8,128)(2,1)S(1)}, u32[]{:S(2)}, u32[]{:S(2)}) collective-permute-start(bf16[2304,128]{1,0:T(8,128)(2,1)S(1)} %get-tuple-element.80), channel_id=1, source_target_pairs={{0,2},{1,3},{2,0},{3,1},{4,6},{5,7},{6,4},{7,5},{8,10},{9,11},{10,... | collective-permute-start | bytes 1769480 | tf_op jit(solution)/shard_map/ppermute | solution.py:854
  77.8 3.3 %collective-permute-start.4 = (bf16[224,128]{1,0:T(8,128)(2,1)S(1)}, bf16[224,128]{1,0:T(8,128)(2,1)S(1)}, u32[]{:S(2)}, u32[]{:S(2)}) collective-permute-start(bf16[224,128]{1,0:T(8,128)(2,1)S(1)} %get-tuple-element.87), channel_id=1, source_target_pairs={{0,8},{2,10},{4,12},{6,14},{1,9},{3,11},{5,13},{7,15},{64,72},{66,... | collective-permute-start | bytes 172040 | tf_op jit(solution)/shard_map/ppermute | solution.py:836
  81.1 4.6 %collective-permute-start.5 = (bf16[224,128]{1,0:T(8,128)(2,1)S(1)}, bf16[224,128]{1,0:T(8,128)(2,1)S(1)}, u32[]{:S(2)}, u32[]{:S(2)}) collective-permute-start(bf16[224,128]{1,0:T(8,128)(2,1)S(1)} %add_convert_fusion.2), channel_id=1, source_target_pairs={{0,16},{2,18},{4,20},{6,22},{1,17},{3,19},{5,21},{7,23},{64,80},{6... | collective-permute-start | bytes 172040 | tf_op jit(solution)/shard_map/ppermute | solution.py:841
  84.1 9.3 %collective-permute-start.7 = (bf16[2,2,128,384]{3,2,1,0:T(8,128)(2,1)S(1)}, bf16[2,2,128,384]{3,2,1,0:T(8,128)(2,1)S(1)}, u32[]{:S(2)}, u32[]{:S(2)}) collective-permute-start(bf16[2,2,128,384]{3,2,1,0:T(8,128)(2,1)S(1)} %get-tuple-element.88), channel_id=1, source_target_pairs={{0,1},{1,0},{2,3},{3,2},{4,5},{5,4},{6,7},{7,6},{8,9},{9,8},{10,11... | collective-permute-start | bytes 1179656 | tf_op jit(solution)/shard_map/ppermute | solution.py:850
  85.7 7.3 %collective-permute-start.6 = (bf16[224,128]{1,0:T(8,128)(2,1)S(1)}, bf16[224,128]{1,0:T(8,128)(2,1)S(1)}, u32[]{:S(2)}, u32[]{:S(2)}) collective-permute-start(bf16[224,128]{1,0:T(8,128)(2,1)S(1)} %add_convert_fusion.1), channel_id=1, source_target_pairs={{0,48},{2,50},{4,52},{6,54},{1,49},{3,51},{5,53},{7,55},{64,112},{... | collective-permute-start | bytes 172040 | tf_op jit(solution)/shard_map/ppermute | solution.py:841
  94.9 27.3 %copy-start = (bf16[384,2304]{1,0:T(8,128)(2,1)S(1)}, bf16[384,2304]{1,0:T(8,128)(2,1)}, u32[]{:S(2)}) copy-start(bf16[384,2304]{1,0:T(8,128)(2,1)} %refs_8_.1) | copy-start | bytes 5308420
  94.9 38.0 %all-to-all-start.1 = ((bf16[32,224,128]{2,1,0:T(8,128)(2,1)}), bf16[32,224,128]{2,1,0:T(8,128)(2,1)}, u32[]{:S(2)}, u32[]{:S(2)}) async-start(bf16[32,224,128]{2,1,0:T(8,128)(2,1)} %broadcast_in_dim.2), calls=%async_computation.1 | async-start | bytes 3670016 | tf_op jit(solution)/shard_map/all_to_all | solution.py:828
  100.2 25.2 %copy-start.2 = (bf16[384,384]{1,0:T(8,128)(2,1)S(1)}, bf16[384,384]{1,0:T(8,128)(2,1)}, u32[]{:S(2)}) copy-start(bf16[384,384]{1,0:T(8,128)(2,1)} %refs_7_.1) | copy-start | bytes 884740
  100.2 25.2 %copy-start.3 = (bf16[256,384]{1,0:T(8,128)(2,1)S(1)}, bf16[256,384]{1,0:T(8,128)(2,1)}, u32[]{:S(2)}) copy-start(bf16[256,384]{1,0:T(8,128)(2,1)} %refs_6_.1) | copy-start | bytes 589828
  119.3 6.1 %collective-permute-start.8 = (bf16[6144,128]{1,0:T(8,128)(2,1)}, bf16[6144,128]{1,0:T(8,128)(2,1)S(1)}, u32[]{:S(2)}, u32[]{:S(2)}) collective-permute-start(bf16[6144,128]{1,0:T(8,128)(2,1)} %all-gather.2.cloned.1.call-done.rows_ref), channel_id=1, source_target_pairs={{0,2},{1,3},{2,0},{3,1},{4,6},{5,7},{6,4},{7,5},{8,10},{9,11},{10,... | collective-permute-start | bytes 4718600 | tf_op jit(solution)/shard_map/ppermute | solution.py:854
  132.9 6.0 %collective-permute-start.9 = (bf16[32,224,128]{2,1,0:T(8,128)(2,1)}, bf16[32,224,128]{2,1,0:T(8,128)(2,1)S(1)}, u32[]{:S(2)}, u32[]{:S(2)}) collective-permute-start(bf16[32,224,128]{2,1,0:T(8,128)(2,1)} %all-to-all-done.1.refs_1_), channel_id=1, source_target_pairs={{0,2},{1,3},{2,0},{3,1},{4,6},{5,7},{6,4},{7,5},{8,10},{9,11},{10,... | collective-permute-start | bytes 5505032 | tf_op jit(solution)/shard_map/ppermute | solution.py:854
  (6 other events, 16.5 us)
Sparse Core Ops, SparseCore 0:
  79.6 39.6 all-gather.1

commit v4 on v3

--- a/solution.py
+++ b/solution.py
@@ -53,9 +53,9 @@
     return jnp.where(first, pltpu.roll(v, 112, 1), pltpu.roll(v, 16, 1))
 
 
-def head_masks():
+def by_head(v):
     low = (lane_iota((1, 128)) < 64).astype(f32)
-    return low.astype(bf16), (1.0 - low).astype(bf16)
+    return jnp.concatenate([v * low.astype(bf16), v * (1.0 - low).astype(bf16)], axis=0)
 
 
 def both(at_ref, a_ref, b_ref, i):
@@ -174,7 +174,6 @@
     att_ref,
 ):
     gains = [jnp.concatenate([r[...], r[...]], axis=1) for r in (qgain_ref, kgain_ref)]
-    masks = head_masks()
     for i in range(2):
         x = both(at_ref, kept_ref, got_ref, i)
         h1 = (x * inv_rms(x) * (1.0 + mod_ref[i, 1:2]) + mod_ref[i, 0:1]).astype(bf16)
@@ -191,11 +190,9 @@
             k = turned[1].astype(bf16)
             q_ref[i, :, p], k_ref[i, :, p] = q, k
             v = v_ref[i, :, p]
-            out = None
-            for m in masks:
-                e = jnp.exp(dot_nt(q * m, k))
-                part_out = dot(e.astype(bf16), v * m) / jnp.sum(e, axis=-1, keepdims=True)
-                out = part_out if out is None else out + part_out
+            e = jnp.exp(dot_nt(by_head(q), k))
+            out = dot(e.astype(bf16), v) / jnp.sum(e, axis=-1, keepdims=True)
+            out = jnp.where(lane_iota((1, 128)) < 64, out[:256], out[256:])
             att_ref[i * 256 : i * 256 + 256, p] = out.astype(bf16)
 
 
@@ -250,7 +247,7 @@
             g = dot(h2, wg)
             u = dot(h2, wu)
             d_hid = dot_nt(d_mlp, wd)
-            sig = 1.0 / (1.0 + jnp.exp(-g))
+            sig = 0.5 * jnp.tanh(0.5 * g) + 0.5
             act = g * sig
             hid = (act * u).astype(bf16)
             du = (d_hid * act).astype(bf16)
@@ -316,7 +313,6 @@
     units_s,
 ):
     gains = [jnp.concatenate([r[...], r[...]], axis=1) for r in (qgain_ref, kgain_ref)]
-    masks = head_masks()
     gain_sums = [0.0, 0.0]
     for i in range(2):
         here = slice(i * 256, i * 256 + 256)
@@ -336,17 +332,16 @@
         turned = [[], []]
         for p in pairs():
             q, k, v, do = q_ref[i, :, p], k_ref[i, :, p], v_ref[i, :, p], d_att[:, p]
-            dq = dk = dv = 0.0
-            for m in masks:
-                qm, km, dom = q * m, k * m, do * m
-                e = jnp.exp(dot_nt(k, qm))
-                soft = e * (1.0 / jnp.sum(e, axis=0, keepdims=True))
-                d_probs = dot_nt(v, dom)
-                delta = jnp.sum(soft * d_probs, axis=0, keepdims=True)
-                ds = (soft * (d_probs - delta)).astype(bf16)
-                dq = dq + dot_tn(ds, km)
-                dk = dk + dot(ds, qm)
-                dv = dv + dot(soft.astype(bf16), dom)
+            q2, do2 = by_head(q), by_head(do)
+            e = jnp.exp(dot_nt(k, q2))
+            soft = e * (1.0 / jnp.sum(e, axis=0, keepdims=True))
+            d_probs = dot_nt(v, do2)
+            delta = jnp.sum(soft * d_probs, axis=0, keepdims=True)
+            ds = (soft * (d_probs - delta)).astype(bf16)
+            dq = dot_tn(ds, k)
+            dq = jnp.where(lane_iota((1, 128)) < 64, dq[:256], dq[256:])
+            dk = dot(ds, q2)
+            dv = dot(soft.astype(bf16), do2)
             for part, d in enumerate((dq * 0.125, dk)):
                 n = z[:, part * 384 + p.start : part * 384 + p.stop]
                 dn = d * cosine - partner(d) * sine
@@ -411,7 +406,7 @@
             num_scalar_prefetch=1,
             grid=(1,),
             in_specs=[theirs, theirs, whole_spec((4, 128)), whole_spec((4, 128))],
-            out_specs=[whole_spec(s) for s in shapes],
+            out_specs=[RESIDENT] * 2,
         ),
         out_shape=[shape_of(s, bf16) for s in shapes],
         compiler_params=params(56),
@@ -437,7 +432,7 @@
                 row_spec(1),
                 whole_spec((384, 2304)),
             ],
-            out_specs=[whole_spec(s) for s in shapes],
+            out_specs=[RESIDENT] * 2,
         ),
         out_shape=[shape_of(s, f32) for s in shapes],
         compiler_params=params(56),
@@ -739,15 +734,16 @@
         return jnp.concatenate(rows).astype(f32)
 
     proj_copy = pltpu.make_async_copy(proj_s, proj_ref, sem)
-    for n in range(4):
+    for n in range(2):
 
         @pl.when(t == n)
         def _():
-            for b in range(2):
-                gu_ref[:, b * 128 : b * 128 + 128] = first(2 * n + b)
-            rows = first(8 + n)
-            for b, p in enumerate(pairs()):
-                down_ref[:, p] = rows[b * 128 : b * 128 + 128]
+            for b in range(4):
+                gu_ref[:, b * 128 : b * 128 + 128] = first(4 * n + b)
+            for m in range(2):
+                rows = first(8 + 2 * n + m)
+                for b, p in enumerate(pairs()):
+                    down_ref[m * 128 : m * 128 + 128, p] = rows[b * 128 : b * 128 + 128]
 
     @pl.when((t == 0) & (half == 1))
     def _():
@@ -760,12 +756,12 @@
         for b, p in enumerate(pairs()):
             qkv_ref[:, p] = second(b)
 
-    @pl.when((t == 2) & (half == 0))
+    @pl.when((t == 1) & (half == 0))
     def _():
         for b, p in enumerate(pairs()):
             qkv_ref[:, p] = second(3 + b)
 
-    @pl.when((t == 3) & (half == 1))
+    @pl.when((t == 1) & (half == 1))
     def _():
         proj_copy.wait()
 
@@ -779,17 +775,15 @@
         lambda *refs: unpack_kernel(own, *refs),
         grid_spec=pltpu.PrefetchScalarGridSpec(
             num_scalar_prefetch=1,
-            grid=(4,),
+            grid=(2,),
             in_specs=[RESIDENT] + [pl.BlockSpec(memory_space=pl.ANY)] * len(earlier),
             out_specs=[
                 pl.BlockSpec(
-                    (384, 384), lambda t, at: (0, half_of(at) * 2 + (1 - half_of(at)) * (t >> 1))
+                    (384, 384), lambda t, at: (0, half_of(at) * 2 + (1 - half_of(at)) * t)
                 ),
                 IN_HBM,
-                pl.BlockSpec(
-                    (384, 256), lambda t, at: (0, 4 * (t >> 1) + 2 * half_of(at) + (t & 1))
-                ),
-                pl.BlockSpec((128, 384), lambda t, at: (4 * half_of(at) + t, 0)),
+                pl.BlockSpec((384, 512), lambda t, at: (0, 2 * t + half_of(at))),
+                pl.BlockSpec((256, 384), lambda t, at: (2 * half_of(at) + t, 0)),
             ],
             scratch_shapes=[pltpu.VMEM((384, 384), f32), pltpu.SemaphoreType.DMA],
         ),

time: 149 us -> 148 us (level)
  no operation moved by 1% of the time
where the time goes in v4:
time: 148 us
  Pallas kernels  42.6 us (29%)
  blocking collectives  31.5 us (21%)
  starting transfers between devices  30.1 us (20%)
  waiting for transfers between devices  24.8 us (17%)
  between operations  14.3 us (10%)
  local copies, waits for them, and re-layouts  3.68 us (2%)
    all_to_all x1, blocking collectives, exchange(): return lax.all_to_all(v, AXES, 0, 0, tiled=True, axis_index_groups=lists)  31.5 us
    all_gather x1, waiting for transfers between devices, body(): lax.all_gather(extra.reshape(768, 128), AXES, axis=0, tiled=True, axis_in...  17.5 us
    pallas_call x3, Pallas kernels, call(): pl.pallas_call(kernel, grid=(1,), in_specs=[SCALARS] + [spec(n in loose,...  16.7 us
    ppermute x4, starting transfers between devices, core_swap(): return lax.ppermute(v, AXES, CORE_SWAP)  9.61 us
    ppermute x2, starting transfers between devices, column_sum(): v = plus(v, lax.ppermute(v, AXES, moves(to)))  8.47 us
    pallas_call x1, Pallas kernels, condition_call(): pl.pallas_call(condition_kernel, grid=(1,), in_specs=[SCALARS] + [RESIDEN...  7.48 us
    pallas_call x2, Pallas kernels, unpack_call(): pl.pallas_call(lambda *refs: unpack_kernel(own, *refs), grid_spec=pltpu.P...  6.88 us
    all_to_all x1, starting transfers between devices, exchange(): return lax.all_to_all(v, AXES, 0, 0, tiled=True, axis_index_groups=lists)  5.34 us
  transfers between devices with their start and end apart: 12, of which 9 were waited for; matrix products, arithmetic and copies ran while one was open for 1% of the time, Pallas kernels for 20%

profile of v4, /device:TPU:1, one launch (start us, length us, event | category | flops | bytes accessed | tf_op | source)
XLA Modules:
  0.0 147.7 jit_solution(5797283684495340033)
XLA Ops:
  7.8 2.5 %pack_swaps.1 = (bf16[2,144,384]{2,1,0:T(8,128)(2,1)}, bf16[2,128,384]{2,1,0:T(8,128)(2,1)}) custom-call(s32[3]{0:T(128)} %pad_add_fusion.at_ref.refs_0_, bf16[4,128,384]{2,1,0:T(8,128)(2,1)} %kept_ref.5, bf16[4,128,384]{2,1,0:T(8,128)(2,1)} %dkept_ref.1, s32[4,128]{1,0:T(4,128)} %row_ref.5, s32[4,128]{1,0:T(4,128)} %col_ref.5), custom_call_target="tpu_custom_call" | custom-call | flops 200000 | bytes 800000 | tf_op jit(solution)/shard_map/pack_swaps/pallas_call | solution.py:403
  10.3 3.6 %collective-permute-start = (bf16[2,144,384]{2,1,0:T(8,128)(2,1)}, bf16[2,144,384]{2,1,0:T(8,128)(2,1)S(1)}, u32[]{:S(2)}, u32[]{:S(2)}) collective-permute-start(bf16[2,144,384]{2,1,0:T(8,128)(2,1)} %get-tuple-element.68), channel_id=1, source_target_pairs={{0,1},{1,0},{2,3},{3,2},{4,5},{5,4},{6,7},{7,6},{8,9},{9,8},{10,11... | collective-permute-start | bytes 663560 | tf_op jit(solution)/shard_map/ppermute | solution.py:844
  14.1 3.9 %modulation.1 = (f32[2,6,384]{2,1,0:T(8,128)}, f32[16,128]{1,0:T(8,128)}) custom-call(s32[3]{0:T(128)} %pad_add_fusion.at_ref.refs_0_, s32[4]{0:T(128)} %t_ref.1, s32[4]{0:T(128)} %l_ref.1, bf16[256,384]{1,0:T(8,128)(2,1)} %refs_6_.1, bf16[384,384]{1,0:T(8,128)(2,1)} %refs_7_.1, bf16[1001,384]{1,0:T(8,128)(2,1)} %row1_ref.1, bf16[1001,384]{1,0:T(8,128)(2,1)} %row1_ref.1, ...), custom_call_target="tpu_custom_call" | custom-call | flops 1000000000 | bytes 3000000 | tf_op jit(solution)/shard_map/modulation/pallas_call | solution.py:423
  19.1 3.2 %attention_forward.1 = (bf16[2,256,384]{2,1,0:T(8,128)(2,1)S(1)}, bf16[2,256,384]{2,1,0:T(8,128)(2,1)S(1)}, bf16[2,256,384]{2,1,0:T(8,128)(2,1)S(1)}, bf16[512,384]{1,0:T(8,128)(2,1)S(1)}) custom-call(s32[3]{0:T(128)S(1)} %copy-done.6, bf16[4,128,384]{2,1,0:T(8,128)(2,1)S(1)} %copy-done.5, bf16[2,144,384]{2,1,0:T(8,128)(2,1)S(1)} %collective-permute-done.got_ref, ...), custom_call_target="tpu_custom_call" | custom-call | flops 3000000000 | bytes 4000000 | tf_op jit(solution)/shard_map/attention_forward/pallas_call | solution.py:449
  22.7 6.1 %mlp_both_ways.1 = (bf16[4608,128]{1,0:T(8,128)(2,1)S(1)}, bf16[4608,128]{1,0:T(8,128)(2,1)S(1)}, bf16[4,128,384]{2,1,0:T(8,128)(2,1)}, bf16[2,128,384]{2,1,0:T(...) custom-call(s32[3]{0:T(128)S(1)} %copy-done.6, bf16[4,128,384]{2,1,0:T(8,128)(2,1)S(1)} %copy-done.5, ...), custom_call_target="tpu_custom_call" | custom-call | flops 6000000000 | bytes 8000000 | tf_op jit(solution)/shard_map/mlp_both_ways/pallas_call | solution.py:449
  28.8 5.0 %collective-permute-start.2 = (bf16[4608,128]{1,0:T(8,128)(2,1)S(1)}, bf16[4608,128]{1,0:T(8,128)(2,1)S(1)}, u32[]{:S(2)}, u32[]{:S(2)}) collective-permute-start(bf16[4608,128]{1,0:T(8,128)(2,1)S(1)} %get-tuple-element.73), channel_id=1, source_target_pairs={{0,2},{1,3},{2,0},{3,1},{4,6},{5,7},{6,4},{7,5},{8,10},{9,11},{10,... | collective-permute-start | bytes 3538952 | tf_op jit(solution)/shard_map/ppermute | solution.py:848
  33.8 7.4 %attention_backward.1 = (bf16[2304,128]{1,0:T(8,128)(2,1)S(1)}, bf16[2304,128]{1,0:T(8,128)(2,1)S(1)}, f32[4,128,384]{2,1,0:T(8,128)}, bf16[2,2,128,384]{3,2,1,0:T(8,128)(2,1)S(1)}, f32[16,128]{1,0:T(8,128)S(1)}) custom-call(s32[3]{0:T(128)S(1)} %copy-done.6, bf16[4,128,384]{2,1,0:T(8,128)(2,1)S(1)} %copy-done.5, ...), custom_call_target="tpu_custom_call" | custom-call | flops 5000000000 | bytes 6000000 | tf_op jit(solution)/shard_map/attention_backward/pallas_call | solution.py:449
  41.2 2.0 %collective-permute-done.3 = bf16[2304,128]{1,0:T(8,128)(2,1)S(1)} collective-permute-done((bf16[2304,128]{1,0:T(8,128)(2,1)S(1)}, bf16[2304,128]{1,0:T(8,128)(2,1)S(1)}, u32[]{:S(2)}, u32[]{:S(2)}) %collective-permute-start.3) | collective-permute-done | bytes 589856 | tf_op jit(solution)/shard_map/ppermute | solution.py:848
  44.1 31.5 %all_to_all.10.a_ref = bf16[16,480,128]{2,1,0:T(8,128)(2,1)S(1)} all-to-all(bf16[16,480,128]{2,1,0:T(8,128)(2,1)S(1)} %join_messages.1), channel_id=1, replica_groups={{0,4,1,5,64,68,65,69,128,132,129,133,192,196,193,197},{2,6,3,7,66,70,67..., dimensions={0} | all-to-all | bytes 3932160 | tf_op jit(solution)/shard_map/all_to_all | solution.py:822
  77.2 1.7 %collective-permute-start.4 = (bf16[224,128]{1,0:T(8,128)(2,1)S(1)}, bf16[224,128]{1,0:T(8,128)(2,1)S(1)}, u32[]{:S(2)}, u32[]{:S(2)}) collective-permute-start(bf16[224,128]{1,0:T(8,128)(2,1)S(1)} %get-tuple-element.87), channel_id=1, source_target_pairs={{0,8},{2,10},{4,12},{6,14},{1,9},{3,11},{5,13},{7,15},{64,72},{66,... | collective-permute-start | bytes 172040 | tf_op jit(solution)/shard_map/ppermute | solution.py:830
  79.0 1.5 %collective-permute-done.4 = bf16[224,128]{1,0:T(8,128)(2,1)S(1)} collective-permute-done((bf16[224,128]{1,0:T(8,128)(2,1)S(1)}, bf16[224,128]{1,0:T(8,128)(2,1)S(1)}, u32[]{:S(2)}, u32[]{:S(2)}) %collective-permute-start.4) | collective-permute-done | bytes 57376 | tf_op jit(solution)/shard_map/ppermute | solution.py:830
  80.5 3.1 %collective-permute-start.5 = (bf16[224,128]{1,0:T(8,128)(2,1)S(1)}, bf16[224,128]{1,0:T(8,128)(2,1)S(1)}, u32[]{:S(2)}, u32[]{:S(2)}) collective-permute-start(bf16[224,128]{1,0:T(8,128)(2,1)S(1)} %add_convert_fusion.2), channel_id=1, source_target_pairs={{0,16},{2,18},{4,20},{6,22},{1,17},{3,19},{5,21},{7,23},{64,80},{6... | collective-permute-start | bytes 172040 | tf_op jit(solution)/shard_map/ppermute | solution.py:835
  85.2 5.4 %collective-permute-start.6 = (bf16[224,128]{1,0:T(8,128)(2,1)S(1)}, bf16[224,128]{1,0:T(8,128)(2,1)S(1)}, u32[]{:S(2)}, u32[]{:S(2)}) collective-permute-start(bf16[224,128]{1,0:T(8,128)(2,1)S(1)} %add_convert_fusion.1), channel_id=1, source_target_pairs={{0,48},{2,50},{4,52},{6,54},{1,49},{3,51},{5,53},{7,55},{64,112},{... | collective-permute-start | bytes 172040 | tf_op jit(solution)/shard_map/ppermute | solution.py:835
  90.6 1.9 %collective-permute-done.6 = bf16[224,128]{1,0:T(8,128)(2,1)S(1)} collective-permute-done((bf16[224,128]{1,0:T(8,128)(2,1)S(1)}, bf16[224,128]{1,0:T(8,128)(2,1)S(1)}, u32[]{:S(2)}, u32[]{:S(2)}) %collective-permute-start.6) | collective-permute-done | bytes 57376 | tf_op jit(solution)/shard_map/ppermute | solution.py:835
  92.9 1.5 broadcast_in_dim.2
  94.4 5.3 %all-to-all-start.1 = ((bf16[32,224,128]{2,1,0:T(8,128)(2,1)}), bf16[32,224,128]{2,1,0:T(8,128)(2,1)}, u32[]{:S(2)}, u32[]{:S(2)}) async-start(bf16[32,224,128]{2,1,0:T(8,128)(2,1)} %broadcast_in_dim.2), calls=%async_computation.1 | async-start | bytes 3670016 | tf_op jit(solution)/shard_map/all_to_all | solution.py:822
  99.7 1.4 place_swaps.1
  101.1 17.5 %all-gather.2.cloned.1.call-done.rows_ref = bf16[6144,128]{1,0:T(8,128)(2,1)} async-done(((bf16[768,128]{1,0:T(8,128)(2,1)}), bf16[6144,128]{1,0:T(8,128)(2,1)}) %all-gather.2.cloned.1.call-update) | async-done | bytes 1572880 | tf_op jit(solution)/shard_map/all_gather | solution.py:887
  118.6 3.0 %collective-permute-start.8 = (bf16[6144,128]{1,0:T(8,128)(2,1)}, bf16[6144,128]{1,0:T(8,128)(2,1)S(1)}, u32[]{:S(2)}, u32[]{:S(2)}) collective-permute-start(bf16[6144,128]{1,0:T(8,128)(2,1)} %all-gather.2.cloned.1.call-done.rows_ref), channel_id=1, source_target_pairs={{0,2},{1,3},{2,0},{3,1},{4,6},{5,7},{6,4},{7,5},{8,10},{9,11},{10,... | collective-permute-start | bytes 4718600 | tf_op jit(solution)/shard_map/ppermute | solution.py:848
  121.6 1.4 copy-done.1
  124.9 7.5 %condition_gradients.1 = (f32[256,384]{1,0:T(8,128)}, f32[384,384]{1,0:T(8,128)}, f32[1001,384]{1,0:T(8,128)}, f32[384,2304]{1,0:T(8,128)}, f32[1,64]{1,0:T(1,128)}, /*index=5*/f32[1,64]{1,0:T(1,128)}) custom-call(s32[3]{0:T(128)S(1)} %copy-done.6, bf16[256,2304]{1,0:T(8,128)(2,1)S(1)} %get-tuple-element.98.refs_0_, ...), custom_call_target="tpu_custom_call" | custom-call | flops 100000000 | bytes 100000 | tf_op jit(solution)/shard_map/condition_gradients/pallas_call | solution.py:672
  132.4 1.5 %collective-permute-start.9 = (bf16[32,224,128]{2,1,0:T(8,128)(2,1)}, bf16[32,224,128]{2,1,0:T(8,128)(2,1)S(1)}, u32[]{:S(2)}, u32[]{:S(2)}) collective-permute-start(bf16[32,224,128]{2,1,0:T(8,128)(2,1)} %all-to-all-done.1.refs_1_), channel_id=1, source_target_pairs={{0,2},{1,3},{2,0},{3,1},{4,6},{5,7},{6,4},{7,5},{8,10},{9,11},{10,... | collective-permute-start | bytes 5505032 | tf_op jit(solution)/shard_map/ppermute | solution.py:848
  133.9 4.3 %unpack_own.1 = (f32[384,1152]{1,0:T(8,128)}, f32[384,384]{1,0:T(8,128)}, f32[384,2048]{1,0:T(8,128)}, f32[1024,384]{1,0:T(8,128)}) custom-call(s32[3]{0:T(128)S(1)} %copy-done.6, bf16[32,224,128]{2,1,0:T(8,128)(2,1)} %all-to-all-done.1.refs_1_), custom_call_target="tpu_custom_call" | custom-call | flops 2000000 | bytes 6000000 | tf_op jit(solution)/shard_map/unpack_own/pallas_call | solution.py:774
  138.2 2.6 %unpack_other.1 = (f32[384,1152]{1,0:T(8,128)}, f32[384,384]{1,0:T(8,128)}, f32[384,2048]{1,0:T(8,128)}, f32[1024,384]{1,0:T(8,128)}) custom-call(s32[3]{0:T(128)S(1)} %copy-done.6, bf16[32,224,128]{2,1,0:T(8,128)(2,1)S(1)} %collective-permute-done.9.refs_1_, ...), custom_call_target="tpu_custom_call", output_to_operand_aliasing={{0}: (2, {}), {1}: (3, {}), {2}: (4, {}), {3}: (5, {})} | custom-call | flops 2000000 | bytes 6000000 | tf_op jit(solution)/shard_map/unpack_other/pallas_call | solution.py:774
  (56 shorter events, 8.6 us)
Async XLA Ops:
  7.2 111.4 %all-gather.2.cloned.1.call-start = ((), (), s32[]{:S(2)}) async-start(), calls=%async_computation.2 | async-start | bytes 1769472 | tf_op jit(solution)/shard_map/all_gather | solution.py:887
  10.3 8.0 %collective-permute-start = (bf16[2,144,384]{2,1,0:T(8,128)(2,1)}, bf16[2,144,384]{2,1,0:T(8,128)(2,1)S(1)}, u32[]{:S(2)}, u32[]{:S(2)}) collective-permute-start(bf16[2,144,384]{2,1,0:T(8,128)(2,1)} %get-tuple-element.68), channel_id=1, source_target_pairs={{0,1},{1,0},{2,3},{3,2},{4,5},{5,4},{6,7},{7,6},{8,9},{9,8},{10,11... | collective-permute-start | bytes 663560 | tf_op jit(solution)/shard_map/ppermute | solution.py:844
  13.9 4.4 %copy-start.5 = (bf16[4,128,384]{2,1,0:T(8,128)(2,1)S(1)}, bf16[4,128,384]{2,1,0:T(8,128)(2,1)}, u32[]{:S(2)}) copy-start(bf16[4,128,384]{2,1,0:T(8,128)(2,1)} %kept_ref.5) | copy-start | bytes 1179652
  13.9 4.4 %copy-start.6 = (s32[3]{0:T(128)S(1)}, s32[3]{0:T(128)}, u32[]{:S(2)}) copy-start(s32[3]{0:T(128)} %pad_add_fusion.at_ref.refs_0_) | copy-start | bytes 40
  13.9 4.4 %copy-start.8 = (s32[4,128]{1,0:T(4,128)S(1)}, s32[4,128]{1,0:T(4,128)}, u32[]{:S(2)}) copy-start(s32[4,128]{1,0:T(4,128)} %row_ref.5) | copy-start | bytes 6148
  13.9 4.4 %copy-start.9 = (s32[4,128]{1,0:T(4,128)S(1)}, s32[4,128]{1,0:T(4,128)}, u32[]{:S(2)}) copy-start(s32[4,128]{1,0:T(4,128)} %col_ref.5) | copy-start | bytes 6148
  13.9 4.4 %copy-start.11 = (bf16[384,1152]{1,0:T(8,128)(2,1)S(1)}, bf16[384,1152]{1,0:T(8,128)(2,1)}, u32[]{:S(2)}) copy-start(bf16[384,1152]{1,0:T(8,128)(2,1)} %w_ref.3) | copy-start | bytes 2654212
  13.9 4.4 %copy-start.15 = (f32[64]{0:T(128)S(1)}, f32[64]{0:T(128)}, u32[]{:S(2)}) copy-start(f32[64]{0:T(128)} %param.27) | copy-start | bytes 772
  13.9 4.4 %copy-start.16 = (f32[64]{0:T(128)S(1)}, f32[64]{0:T(128)}, u32[]{:S(2)}) copy-start(f32[64]{0:T(128)} %param.28) | copy-start | bytes 772
  13.9 4.4 %copy-start.17 = (bf16[4,32,128]{2,1,0:T(8,128)(2,1)S(1)}, bf16[4,32,128]{2,1,0:T(8,128)(2,1)}, u32[]{:S(2)}) copy-start(bf16[4,32,128]{2,1,0:T(8,128)(2,1)} %constant.40.clone.table_ref) | copy-start | bytes 98308
  14.0 8.7 %collective-permute-start.1 = (bf16[2,128,384]{2,1,0:T(8,128)(2,1)}, bf16[2,128,384]{2,1,0:T(8,128)(2,1)S(1)}, u32[]{:S(2)}, u32[]{:S(2)}) collective-permute-start(bf16[2,128,384]{2,1,0:T(8,128)(2,1)} %get-tuple-element.69), channel_id=1, source_target_pairs={{0,1},{1,0},{2,3},{3,2},{4,5},{5,4},{6,7},{7,6},{8,9},{9,8},{10,11... | collective-permute-start | bytes 589832 | tf_op jit(solution)/shard_map/ppermute | solution.py:844
  28.8 14.4 %collective-permute-start.2 = (bf16[4608,128]{1,0:T(8,128)(2,1)S(1)}, bf16[4608,128]{1,0:T(8,128)(2,1)S(1)}, u32[]{:S(2)}, u32[]{:S(2)}) collective-permute-start(bf16[4608,128]{1,0:T(8,128)(2,1)S(1)} %get-tuple-element.73), channel_id=1, source_target_pairs={{0,2},{1,3},{2,0},{3,1},{4,6},{5,7},{6,4},{7,5},{8,10},{9,11},{10,... | collective-permute-start | bytes 3538952 | tf_op jit(solution)/shard_map/ppermute | solution.py:848
  33.8 9.4 %copy-start.7 = (f32[16,128]{1,0:T(8,128)S(1)}, f32[16,128]{1,0:T(8,128)}, u32[]{:S(2)}) copy-start(f32[16,128]{1,0:T(8,128)} %get-tuple-element.83.extra_ref) | copy-start | bytes 24580
  41.2 2.0 %collective-permute-start.3 = (bf16[2304,128]{1,0:T(8,128)(2,1)S(1)}, bf16[2304,128]{1,0:T(8,128)(2,1)S(1)}, u32[]{:S(2)}, u32[]{:S(2)}) collective-permute-start(bf16[2304,128]{1,0:T(8,128)(2,1)S(1)} %get-tuple-element.80), channel_id=1, source_target_pairs={{0,2},{1,3},{2,0},{3,1},{4,6},{5,7},{6,4},{7,5},{8,10},{9,11},{10,... | collective-permute-start | bytes 1769480 | tf_op jit(solution)/shard_map/ppermute | solution.py:848
  77.2 3.3 %collective-permute-start.4 = (bf16[224,128]{1,0:T(8,128)(2,1)S(1)}, bf16[224,128]{1,0:T(8,128)(2,1)S(1)}, u32[]{:S(2)}, u32[]{:S(2)}) collective-permute-start(bf16[224,128]{1,0:T(8,128)(2,1)S(1)} %get-tuple-element.87), channel_id=1, source_target_pairs={{0,8},{2,10},{4,12},{6,14},{1,9},{3,11},{5,13},{7,15},{64,72},{66,... | collective-permute-start | bytes 172040 | tf_op jit(solution)/shard_map/ppermute | solution.py:830
  80.5 4.6 %collective-permute-start.5 = (bf16[224,128]{1,0:T(8,128)(2,1)S(1)}, bf16[224,128]{1,0:T(8,128)(2,1)S(1)}, u32[]{:S(2)}, u32[]{:S(2)}) collective-permute-start(bf16[224,128]{1,0:T(8,128)(2,1)S(1)} %add_convert_fusion.2), channel_id=1, source_target_pairs={{0,16},{2,18},{4,20},{6,22},{1,17},{3,19},{5,21},{7,23},{64,80},{6... | collective-permute-start | bytes 172040 | tf_op jit(solution)/shard_map/ppermute | solution.py:835
  83.6 9.3 %collective-permute-start.7 = (bf16[2,2,128,384]{3,2,1,0:T(8,128)(2,1)S(1)}, bf16[2,2,128,384]{3,2,1,0:T(8,128)(2,1)S(1)}, u32[]{:S(2)}, u32[]{:S(2)}) collective-permute-start(bf16[2,2,128,384]{3,2,1,0:T(8,128)(2,1)S(1)} %get-tuple-element.88), channel_id=1, source_target_pairs={{0,1},{1,0},{2,3},{3,2},{4,5},{5,4},{6,7},{7,6},{8,9},{9,8},{10,11... | collective-permute-start | bytes 1179656 | tf_op jit(solution)/shard_map/ppermute | solution.py:844
  85.2 7.3 %collective-permute-start.6 = (bf16[224,128]{1,0:T(8,128)(2,1)S(1)}, bf16[224,128]{1,0:T(8,128)(2,1)S(1)}, u32[]{:S(2)}, u32[]{:S(2)}) collective-permute-start(bf16[224,128]{1,0:T(8,128)(2,1)S(1)} %add_convert_fusion.1), channel_id=1, source_target_pairs={{0,48},{2,50},{4,52},{6,54},{1,49},{3,51},{5,53},{7,55},{64,112},{... | collective-permute-start | bytes 172040 | tf_op jit(solution)/shard_map/ppermute | solution.py:835
  94.4 27.3 %copy-start = (bf16[384,2304]{1,0:T(8,128)(2,1)S(1)}, bf16[384,2304]{1,0:T(8,128)(2,1)}, u32[]{:S(2)}) copy-start(bf16[384,2304]{1,0:T(8,128)(2,1)} %refs_8_.1) | copy-start | bytes 5308420
  94.4 38.0 %all-to-all-start.1 = ((bf16[32,224,128]{2,1,0:T(8,128)(2,1)}), bf16[32,224,128]{2,1,0:T(8,128)(2,1)}, u32[]{:S(2)}, u32[]{:S(2)}) async-start(bf16[32,224,128]{2,1,0:T(8,128)(2,1)} %broadcast_in_dim.2), calls=%async_computation.1 | async-start | bytes 3670016 | tf_op jit(solution)/shard_map/all_to_all | solution.py:822
  99.7 25.2 %copy-start.2 = (bf16[384,384]{1,0:T(8,128)(2,1)S(1)}, bf16[384,384]{1,0:T(8,128)(2,1)}, u32[]{:S(2)}) copy-start(bf16[384,384]{1,0:T(8,128)(2,1)} %refs_7_.1) | copy-start | bytes 884740
  99.7 25.2 %copy-start.3 = (bf16[256,384]{1,0:T(8,128)(2,1)S(1)}, bf16[256,384]{1,0:T(8,128)(2,1)}, u32[]{:S(2)}) copy-start(bf16[256,384]{1,0:T(8,128)(2,1)} %refs_6_.1) | copy-start | bytes 589828
  118.6 6.3 %collective-permute-start.8 = (bf16[6144,128]{1,0:T(8,128)(2,1)}, bf16[6144,128]{1,0:T(8,128)(2,1)S(1)}, u32[]{:S(2)}, u32[]{:S(2)}) collective-permute-start(bf16[6144,128]{1,0:T(8,128)(2,1)} %all-gather.2.cloned.1.call-done.rows_ref), channel_id=1, source_target_pairs={{0,2},{1,3},{2,0},{3,1},{4,6},{5,7},{6,4},{7,5},{8,10},{9,11},{10,... | collective-permute-start | bytes 4718600 | tf_op jit(solution)/shard_map/ppermute | solution.py:848
  132.4 5.9 %collective-permute-start.9 = (bf16[32,224,128]{2,1,0:T(8,128)(2,1)}, bf16[32,224,128]{2,1,0:T(8,128)(2,1)S(1)}, u32[]{:S(2)}, u32[]{:S(2)}) collective-permute-start(bf16[32,224,128]{2,1,0:T(8,128)(2,1)} %all-to-all-done.1.refs_1_), channel_id=1, source_target_pairs={{0,2},{1,3},{2,0},{3,1},{4,6},{5,7},{6,4},{7,5},{8,10},{9,11},{10,... | collective-permute-start | bytes 5505032 | tf_op jit(solution)/shard_map/ppermute | solution.py:848
  (6 other events, 16.5 us)
Sparse Core Ops, SparseCore 0:
  79.1 39.4 all-gather.1

commit v5 on v4

--- a/solution.py
+++ b/solution.py
@@ -461,6 +461,22 @@
     return call
 
 
+def relay_kernel(mod_ref, out_ref):
+    out_ref[...] = mod_ref[...]
+
+
+def relay_call(mod):
+    return pl.pallas_call(
+        relay_kernel,
+        in_specs=[RESIDENT],
+        out_specs=RESIDENT,
+        out_shape=shape_of((2, 6, 384), f32),
+        compiler_params=params(2),
+        cost_estimate=cost(1_000, 40_000),
+        name="relay_modulation",
+    )(mod)
+
+
 forward_call = resident_call(
     forward_kernel,
     "attention_forward",
@@ -871,6 +887,7 @@
     send, dsend = pack_call(at, latents, out_grad, pos_row, pos_col)
     got, dgot = swap(send), swap(dsend)
     mod, extra = modulation_call(at, timesteps, labels, t_w1, t_w2, label_table, mod_w)
+    mod = relay_call(mod)
     turn = (q_gain.reshape(1, 64), k_gain.reshape(1, 64), pos_row, pos_col, turn_table())
     q, k, v, att = forward_call(at, latents, got, mod, qkv_w, *turn)
     keep1, send1, block_out, out_send, d_mid, sums1 = mlp_call(

time: 148 us -> 147 us (level)
  transfers between devices with their start and end apart: 12 -> 12, of which waited for: 9 -> 8; matrix products, arithmetic and copies ran while one was open for 1% -> 1% of each run, Pallas kernels for 20% -> 20%
where the time goes in v5:
time: 147 us
  Pallas kernels  42.6 us (29%)
  blocking collectives  31.6 us (21%)
  starting transfers between devices  29.3 us (20%)
  waiting for transfers between devices  24.9 us (17%)
  between operations  14.3 us (10%)
  local copies, waits for them, and re-layouts  3.7 us (3%)
    all_to_all x1, blocking collectives, exchange(): return lax.all_to_all(v, AXES, 0, 0, tiled=True, axis_index_groups=lists)  31.6 us
    all_gather x1, waiting for transfers between devices, body(): lax.all_gather(extra.reshape(768, 128), AXES, axis=0, tiled=True, axis_in...  17.6 us
    pallas_call x3, Pallas kernels, call(): pl.pallas_call(kernel, grid=(1,), in_specs=[SCALARS] + [spec(n in loose,...  16.7 us
    ppermute x4, starting transfers between devices, core_swap(): return lax.ppermute(v, AXES, CORE_SWAP)  8.79 us
    ppermute x2, starting transfers between devices, column_sum(): v = plus(v, lax.ppermute(v, AXES, moves(to)))  8.49 us
    pallas_call x1, Pallas kernels, condition_call(): pl.pallas_call(condition_kernel, grid=(1,), in_specs=[SCALARS] + [RESIDEN...  7.48 us
    pallas_call x2, Pallas kernels, unpack_call(): pl.pallas_call(lambda *refs: unpack_kernel(own, *refs), grid_spec=pltpu.P...  6.88 us
    all_to_all x1, starting transfers between devices, exchange(): return lax.all_to_all(v, AXES, 0, 0, tiled=True, axis_index_groups=lists)  5.34 us
  transfers between devices with their start and end apart: 12, of which 8 were waited for; matrix products, arithmetic and copies ran while one was open for 1% of the time, Pallas kernels for 20%

profile of v5, /device:TPU:1, one launch (start us, length us, event | category | flops | bytes accessed | tf_op | source)
XLA Modules:
  0.0 146.9 jit_solution(847655439999970704)
XLA Ops:
  7.8 2.5 %pack_swaps.1 = (bf16[2,144,384]{2,1,0:T(8,128)(2,1)}, bf16[2,128,384]{2,1,0:T(8,128)(2,1)}) custom-call(s32[3]{0:T(128)} %pad_add_fusion.at_ref.refs_0_, bf16[4,128,384]{2,1,0:T(8,128)(2,1)} %kept_ref.5, bf16[4,128,384]{2,1,0:T(8,128)(2,1)} %dkept_ref.1, s32[4,128]{1,0:T(4,128)} %row_ref.5, s32[4,128]{1,0:T(4,128)} %col_ref.5), custom_call_target="tpu_custom_call" | custom-call | flops 200000 | bytes 800000 | tf_op jit(solution)/shard_map/pack_swaps/pallas_call | solution.py:403
  10.3 3.6 %collective-permute-start = (bf16[2,144,384]{2,1,0:T(8,128)(2,1)}, bf16[2,144,384]{2,1,0:T(8,128)(2,1)S(1)}, u32[]{:S(2)}, u32[]{:S(2)}) collective-permute-start(bf16[2,144,384]{2,1,0:T(8,128)(2,1)} %get-tuple-element.68), channel_id=1, source_target_pairs={{0,1},{1,0},{2,3},{3,2},{4,5},{5,4},{6,7},{7,6},{8,9},{9,8},{10,11... | collective-permute-start | bytes 663560 | tf_op jit(solution)/shard_map/ppermute | solution.py:860
  14.1 3.9 %modulation.1 = (f32[2,6,384]{2,1,0:T(8,128)}, f32[16,128]{1,0:T(8,128)}) custom-call(s32[3]{0:T(128)} %pad_add_fusion.at_ref.refs_0_, s32[4]{0:T(128)} %t_ref.1, s32[4]{0:T(128)} %l_ref.1, bf16[256,384]{1,0:T(8,128)(2,1)} %refs_6_.1, bf16[384,384]{1,0:T(8,128)(2,1)} %refs_7_.1, bf16[1001,384]{1,0:T(8,128)(2,1)} %row1_ref.1, bf16[1001,384]{1,0:T(8,128)(2,1)} %row1_ref.1, ...), custom_call_target="tpu_custom_call" | custom-call | flops 1000000000 | bytes 3000000 | tf_op jit(solution)/shard_map/modulation/pallas_call | solution.py:423
  18.9 3.2 %attention_forward.1 = (bf16[2,256,384]{2,1,0:T(8,128)(2,1)S(1)}, bf16[2,256,384]{2,1,0:T(8,128)(2,1)S(1)}, bf16[2,256,384]{2,1,0:T(8,128)(2,1)S(1)}, bf16[512,384]{1,0:T(8,128)(2,1)S(1)}) custom-call(s32[3]{0:T(128)S(1)} %copy-done.6, bf16[4,128,384]{2,1,0:T(8,128)(2,1)S(1)} %copy-done.5, bf16[2,144,384]{2,1,0:T(8,128)(2,1)S(1)} %collective-permute-done.got_ref, ...), custom_call_target="tpu_custom_call" | custom-call | flops 3000000000 | bytes 4000000 | tf_op jit(solution)/shard_map/attention_forward/pallas_call | solution.py:449
  22.7 6.1 %mlp_both_ways.1 = (bf16[4608,128]{1,0:T(8,128)(2,1)S(1)}, bf16[4608,128]{1,0:T(8,128)(2,1)S(1)}, bf16[4,128,384]{2,1,0:T(8,128)(2,1)}, bf16[2,128,384]{2,1,0:T(...) custom-call(s32[3]{0:T(128)S(1)} %copy-done.6, bf16[4,128,384]{2,1,0:T(8,128)(2,1)S(1)} %copy-done.5, ...), custom_call_target="tpu_custom_call" | custom-call | flops 6000000000 | bytes 8000000 | tf_op jit(solution)/shard_map/mlp_both_ways/pallas_call | solution.py:449
  28.8 4.3 %collective-permute-start.2 = (bf16[4608,128]{1,0:T(8,128)(2,1)S(1)}, bf16[4608,128]{1,0:T(8,128)(2,1)S(1)}, u32[]{:S(2)}, u32[]{:S(2)}) collective-permute-start(bf16[4608,128]{1,0:T(8,128)(2,1)S(1)} %get-tuple-element.73), channel_id=1, source_target_pairs={{0,2},{1,3},{2,0},{3,1},{4,6},{5,7},{6,4},{7,5},{8,10},{9,11},{10,... | collective-permute-start | bytes 3538952 | tf_op jit(solution)/shard_map/ppermute | solution.py:864
  33.0 7.4 %attention_backward.1 = (bf16[2304,128]{1,0:T(8,128)(2,1)S(1)}, bf16[2304,128]{1,0:T(8,128)(2,1)S(1)}, f32[4,128,384]{2,1,0:T(8,128)}, bf16[2,2,128,384]{3,2,1,0:T(8,128)(2,1)S(1)}, f32[16,128]{1,0:T(8,128)S(1)}) custom-call(s32[3]{0:T(128)S(1)} %copy-done.6, bf16[4,128,384]{2,1,0:T(8,128)(2,1)S(1)} %copy-done.5, ...), custom_call_target="tpu_custom_call" | custom-call | flops 5000000000 | bytes 6000000 | tf_op jit(solution)/shard_map/attention_backward/pallas_call | solution.py:449
  40.5 2.0 %collective-permute-done.3 = bf16[2304,128]{1,0:T(8,128)(2,1)S(1)} collective-permute-done((bf16[2304,128]{1,0:T(8,128)(2,1)S(1)}, bf16[2304,128]{1,0:T(8,128)(2,1)S(1)}, u32[]{:S(2)}, u32[]{:S(2)}) %collective-permute-start.3) | collective-permute-done | bytes 589856 | tf_op jit(solution)/shard_map/ppermute | solution.py:864
  43.4 31.6 %all_to_all.10.a_ref = bf16[16,480,128]{2,1,0:T(8,128)(2,1)S(1)} all-to-all(bf16[16,480,128]{2,1,0:T(8,128)(2,1)S(1)} %join_messages.1), channel_id=1, replica_groups={{0,4,1,5,64,68,65,69,128,132,129,133,192,196,193,197},{2,6,3,7,66,70,67..., dimensions={0} | all-to-all | bytes 3932160 | tf_op jit(solution)/shard_map/all_to_all | solution.py:838
  76.5 1.7 %collective-permute-start.4 = (bf16[224,128]{1,0:T(8,128)(2,1)S(1)}, bf16[224,128]{1,0:T(8,128)(2,1)S(1)}, u32[]{:S(2)}, u32[]{:S(2)}) collective-permute-start(bf16[224,128]{1,0:T(8,128)(2,1)S(1)} %get-tuple-element.87), channel_id=1, source_target_pairs={{0,8},{2,10},{4,12},{6,14},{1,9},{3,11},{5,13},{7,15},{64,72},{66,... | collective-permute-start | bytes 172040 | tf_op jit(solution)/shard_map/ppermute | solution.py:846
  78.2 1.5 %collective-permute-done.4 = bf16[224,128]{1,0:T(8,128)(2,1)S(1)} collective-permute-done((bf16[224,128]{1,0:T(8,128)(2,1)S(1)}, bf16[224,128]{1,0:T(8,128)(2,1)S(1)}, u32[]{:S(2)}, u32[]{:S(2)}) %collective-permute-start.4) | collective-permute-done | bytes 57376 | tf_op jit(solution)/shard_map/ppermute | solution.py:846
  79.8 3.1 %collective-permute-start.5 = (bf16[224,128]{1,0:T(8,128)(2,1)S(1)}, bf16[224,128]{1,0:T(8,128)(2,1)S(1)}, u32[]{:S(2)}, u32[]{:S(2)}) collective-permute-start(bf16[224,128]{1,0:T(8,128)(2,1)S(1)} %add_convert_fusion.2), channel_id=1, source_target_pairs={{0,16},{2,18},{4,20},{6,22},{1,17},{3,19},{5,21},{7,23},{64,80},{6... | collective-permute-start | bytes 172040 | tf_op jit(solution)/shard_map/ppermute | solution.py:851
  84.5 5.4 %collective-permute-start.6 = (bf16[224,128]{1,0:T(8,128)(2,1)S(1)}, bf16[224,128]{1,0:T(8,128)(2,1)S(1)}, u32[]{:S(2)}, u32[]{:S(2)}) collective-permute-start(bf16[224,128]{1,0:T(8,128)(2,1)S(1)} %add_convert_fusion.1), channel_id=1, source_target_pairs={{0,48},{2,50},{4,52},{6,54},{1,49},{3,51},{5,53},{7,55},{64,112},{... | collective-permute-start | bytes 172040 | tf_op jit(solution)/shard_map/ppermute | solution.py:851
  89.9 1.9 %collective-permute-done.6 = bf16[224,128]{1,0:T(8,128)(2,1)S(1)} collective-permute-done((bf16[224,128]{1,0:T(8,128)(2,1)S(1)}, bf16[224,128]{1,0:T(8,128)(2,1)S(1)}, u32[]{:S(2)}, u32[]{:S(2)}) %collective-permute-start.6) | collective-permute-done | bytes 57376 | tf_op jit(solution)/shard_map/ppermute | solution.py:851
  92.2 1.5 broadcast_in_dim.2
  93.6 5.3 %all-to-all-start.1 = ((bf16[32,224,128]{2,1,0:T(8,128)(2,1)}), bf16[32,224,128]{2,1,0:T(8,128)(2,1)}, u32[]{:S(2)}, u32[]{:S(2)}) async-start(bf16[32,224,128]{2,1,0:T(8,128)(2,1)} %broadcast_in_dim.2), calls=%async_computation.1 | async-start | bytes 3670016 | tf_op jit(solution)/shard_map/all_to_all | solution.py:838
  99.0 1.4 place_swaps.1
  100.4 17.6 %all-gather.2.cloned.1.call-done.rows_ref = bf16[6144,128]{1,0:T(8,128)(2,1)} async-done(((bf16[768,128]{1,0:T(8,128)(2,1)}), bf16[6144,128]{1,0:T(8,128)(2,1)}) %all-gather.2.cloned.1.call-update) | async-done | bytes 1572880 | tf_op jit(solution)/shard_map/all_gather | solution.py:904
  118.0 2.9 %collective-permute-start.8 = (bf16[6144,128]{1,0:T(8,128)(2,1)}, bf16[6144,128]{1,0:T(8,128)(2,1)S(1)}, u32[]{:S(2)}, u32[]{:S(2)}) collective-permute-start(bf16[6144,128]{1,0:T(8,128)(2,1)} %all-gather.2.cloned.1.call-done.rows_ref), channel_id=1, source_target_pairs={{0,2},{1,3},{2,0},{3,1},{4,6},{5,7},{6,4},{7,5},{8,10},{9,11},{10,... | collective-permute-start | bytes 4718600 | tf_op jit(solution)/shard_map/ppermute | solution.py:864
  120.9 1.4 copy-done.1
  124.1 7.5 %condition_gradients.1 = (f32[256,384]{1,0:T(8,128)}, f32[384,384]{1,0:T(8,128)}, f32[1001,384]{1,0:T(8,128)}, f32[384,2304]{1,0:T(8,128)}, f32[1,64]{1,0:T(1,128)}, /*index=5*/f32[1,64]{1,0:T(1,128)}) custom-call(s32[3]{0:T(128)S(1)} %copy-done.6, bf16[256,2304]{1,0:T(8,128)(2,1)S(1)} %get-tuple-element.98.refs_0_, ...), custom_call_target="tpu_custom_call" | custom-call | flops 100000000 | bytes 100000 | tf_op jit(solution)/shard_map/condition_gradients/pallas_call | solution.py:688
  131.6 1.6 %collective-permute-start.9 = (bf16[32,224,128]{2,1,0:T(8,128)(2,1)}, bf16[32,224,128]{2,1,0:T(8,128)(2,1)S(1)}, u32[]{:S(2)}, u32[]{:S(2)}) collective-permute-start(bf16[32,224,128]{2,1,0:T(8,128)(2,1)} %all-to-all-done.1.refs_1_), channel_id=1, source_target_pairs={{0,2},{1,3},{2,0},{3,1},{4,6},{5,7},{6,4},{7,5},{8,10},{9,11},{10,... | collective-permute-start | bytes 5505032 | tf_op jit(solution)/shard_map/ppermute | solution.py:864
  133.2 4.3 %unpack_own.1 = (f32[384,1152]{1,0:T(8,128)}, f32[384,384]{1,0:T(8,128)}, f32[384,2048]{1,0:T(8,128)}, f32[1024,384]{1,0:T(8,128)}) custom-call(s32[3]{0:T(128)S(1)} %copy-done.6, bf16[32,224,128]{2,1,0:T(8,128)(2,1)} %all-to-all-done.1.refs_1_), custom_call_target="tpu_custom_call" | custom-call | flops 2000000 | bytes 6000000 | tf_op jit(solution)/shard_map/unpack_own/pallas_call | solution.py:790
  137.5 2.6 %unpack_other.1 = (f32[384,1152]{1,0:T(8,128)}, f32[384,384]{1,0:T(8,128)}, f32[384,2048]{1,0:T(8,128)}, f32[1024,384]{1,0:T(8,128)}) custom-call(s32[3]{0:T(128)S(1)} %copy-done.6, bf16[32,224,128]{2,1,0:T(8,128)(2,1)S(1)} %collective-permute-done.9.refs_1_, ...), custom_call_target="tpu_custom_call", output_to_operand_aliasing={{0}: (2, {}), {1}: (3, {}), {2}: (4, {}), {3}: (5, {})} | custom-call | flops 2000000 | bytes 6000000 | tf_op jit(solution)/shard_map/unpack_other/pallas_call | solution.py:790
  (57 shorter events, 8.6 us)
Async XLA Ops:
  7.2 110.8 %all-gather.2.cloned.1.call-start = ((), (), s32[]{:S(2)}) async-start(), calls=%async_computation.2 | async-start | bytes 1769472 | tf_op jit(solution)/shard_map/all_gather | solution.py:904
  10.3 8.4 %collective-permute-start = (bf16[2,144,384]{2,1,0:T(8,128)(2,1)}, bf16[2,144,384]{2,1,0:T(8,128)(2,1)S(1)}, u32[]{:S(2)}, u32[]{:S(2)}) collective-permute-start(bf16[2,144,384]{2,1,0:T(8,128)(2,1)} %get-tuple-element.68), channel_id=1, source_target_pairs={{0,1},{1,0},{2,3},{3,2},{4,5},{5,4},{6,7},{7,6},{8,9},{9,8},{10,11... | collective-permute-start | bytes 663560 | tf_op jit(solution)/shard_map/ppermute | solution.py:860
  13.9 4.8 %copy-start.5 = (bf16[4,128,384]{2,1,0:T(8,128)(2,1)S(1)}, bf16[4,128,384]{2,1,0:T(8,128)(2,1)}, u32[]{:S(2)}) copy-start(bf16[4,128,384]{2,1,0:T(8,128)(2,1)} %kept_ref.5) | copy-start | bytes 1179652
  13.9 4.8 %copy-start.6 = (s32[3]{0:T(128)S(1)}, s32[3]{0:T(128)}, u32[]{:S(2)}) copy-start(s32[3]{0:T(128)} %pad_add_fusion.at_ref.refs_0_) | copy-start | bytes 40
  13.9 4.8 %copy-start.9 = (s32[4,128]{1,0:T(4,128)S(1)}, s32[4,128]{1,0:T(4,128)}, u32[]{:S(2)}) copy-start(s32[4,128]{1,0:T(4,128)} %row_ref.5) | copy-start | bytes 6148
  13.9 4.9 %copy-start.10 = (s32[4,128]{1,0:T(4,128)S(1)}, s32[4,128]{1,0:T(4,128)}, u32[]{:S(2)}) copy-start(s32[4,128]{1,0:T(4,128)} %col_ref.5) | copy-start | bytes 6148
  13.9 4.9 %copy-start.12 = (bf16[384,1152]{1,0:T(8,128)(2,1)S(1)}, bf16[384,1152]{1,0:T(8,128)(2,1)}, u32[]{:S(2)}) copy-start(bf16[384,1152]{1,0:T(8,128)(2,1)} %w_ref.3) | copy-start | bytes 2654212
  13.9 4.9 %copy-start.15 = (f32[64]{0:T(128)S(1)}, f32[64]{0:T(128)}, u32[]{:S(2)}) copy-start(f32[64]{0:T(128)} %param.27) | copy-start | bytes 772
  13.9 4.9 %copy-start.16 = (f32[64]{0:T(128)S(1)}, f32[64]{0:T(128)}, u32[]{:S(2)}) copy-start(f32[64]{0:T(128)} %param.28) | copy-start | bytes 772
  13.9 4.9 %copy-start.17 = (bf16[4,32,128]{2,1,0:T(8,128)(2,1)S(1)}, bf16[4,32,128]{2,1,0:T(8,128)(2,1)}, u32[]{:S(2)}) copy-start(bf16[4,32,128]{2,1,0:T(8,128)(2,1)} %constant.40.clone.table_ref) | copy-start | bytes 98308
  14.0 8.7 %collective-permute-start.1 = (bf16[2,128,384]{2,1,0:T(8,128)(2,1)}, bf16[2,128,384]{2,1,0:T(8,128)(2,1)S(1)}, u32[]{:S(2)}, u32[]{:S(2)}) collective-permute-start(bf16[2,128,384]{2,1,0:T(8,128)(2,1)} %get-tuple-element.69), channel_id=1, source_target_pairs={{0,1},{1,0},{2,3},{3,2},{4,5},{5,4},{6,7},{7,6},{8,9},{9,8},{10,11... | collective-permute-start | bytes 589832 | tf_op jit(solution)/shard_map/ppermute | solution.py:860
  28.8 13.7 %collective-permute-start.2 = (bf16[4608,128]{1,0:T(8,128)(2,1)S(1)}, bf16[4608,128]{1,0:T(8,128)(2,1)S(1)}, u32[]{:S(2)}, u32[]{:S(2)}) collective-permute-start(bf16[4608,128]{1,0:T(8,128)(2,1)S(1)} %get-tuple-element.73), channel_id=1, source_target_pairs={{0,2},{1,3},{2,0},{3,1},{4,6},{5,7},{6,4},{7,5},{8,10},{9,11},{10,... | collective-permute-start | bytes 3538952 | tf_op jit(solution)/shard_map/ppermute | solution.py:864
  33.0 9.4 %copy-start.8 = (f32[16,128]{1,0:T(8,128)S(1)}, f32[16,128]{1,0:T(8,128)}, u32[]{:S(2)}) copy-start(f32[16,128]{1,0:T(8,128)} %get-tuple-element.83.extra_ref) | copy-start | bytes 24580
  40.4 2.0 %collective-permute-start.3 = (bf16[2304,128]{1,0:T(8,128)(2,1)S(1)}, bf16[2304,128]{1,0:T(8,128)(2,1)S(1)}, u32[]{:S(2)}, u32[]{:S(2)}) collective-permute-start(bf16[2304,128]{1,0:T(8,128)(2,1)S(1)} %get-tuple-element.80), channel_id=1, source_target_pairs={{0,2},{1,3},{2,0},{3,1},{4,6},{5,7},{6,4},{7,5},{8,10},{9,11},{10,... | collective-permute-start | bytes 1769480 | tf_op jit(solution)/shard_map/ppermute | solution.py:864
  76.5 3.3 %collective-permute-start.4 = (bf16[224,128]{1,0:T(8,128)(2,1)S(1)}, bf16[224,128]{1,0:T(8,128)(2,1)S(1)}, u32[]{:S(2)}, u32[]{:S(2)}) collective-permute-start(bf16[224,128]{1,0:T(8,128)(2,1)S(1)} %get-tuple-element.87), channel_id=1, source_target_pairs={{0,8},{2,10},{4,12},{6,14},{1,9},{3,11},{5,13},{7,15},{64,72},{66,... | collective-permute-start | bytes 172040 | tf_op jit(solution)/shard_map/ppermute | solution.py:846
  79.8 4.6 %collective-permute-start.5 = (bf16[224,128]{1,0:T(8,128)(2,1)S(1)}, bf16[224,128]{1,0:T(8,128)(2,1)S(1)}, u32[]{:S(2)}, u32[]{:S(2)}) collective-permute-start(bf16[224,128]{1,0:T(8,128)(2,1)S(1)} %add_convert_fusion.2), channel_id=1, source_target_pairs={{0,16},{2,18},{4,20},{6,22},{1,17},{3,19},{5,21},{7,23},{64,80},{6... | collective-permute-start | bytes 172040 | tf_op jit(solution)/shard_map/ppermute | solution.py:851
  82.9 9.3 %collective-permute-start.7 = (bf16[2,2,128,384]{3,2,1,0:T(8,128)(2,1)S(1)}, bf16[2,2,128,384]{3,2,1,0:T(8,128)(2,1)S(1)}, u32[]{:S(2)}, u32[]{:S(2)}) collective-permute-start(bf16[2,2,128,384]{3,2,1,0:T(8,128)(2,1)S(1)} %get-tuple-element.88), channel_id=1, source_target_pairs={{0,1},{1,0},{2,3},{3,2},{4,5},{5,4},{6,7},{7,6},{8,9},{9,8},{10,11... | collective-permute-start | bytes 1179656 | tf_op jit(solution)/shard_map/ppermute | solution.py:860
  84.5 7.3 %collective-permute-start.6 = (bf16[224,128]{1,0:T(8,128)(2,1)S(1)}, bf16[224,128]{1,0:T(8,128)(2,1)S(1)}, u32[]{:S(2)}, u32[]{:S(2)}) collective-permute-start(bf16[224,128]{1,0:T(8,128)(2,1)S(1)} %add_convert_fusion.1), channel_id=1, source_target_pairs={{0,48},{2,50},{4,52},{6,54},{1,49},{3,51},{5,53},{7,55},{64,112},{... | collective-permute-start | bytes 172040 | tf_op jit(solution)/shard_map/ppermute | solution.py:851
  93.6 27.2 %copy-start = (bf16[384,2304]{1,0:T(8,128)(2,1)S(1)}, bf16[384,2304]{1,0:T(8,128)(2,1)}, u32[]{:S(2)}) copy-start(bf16[384,2304]{1,0:T(8,128)(2,1)} %refs_8_.1) | copy-start | bytes 5308420
  93.6 38.0 %all-to-all-start.1 = ((bf16[32,224,128]{2,1,0:T(8,128)(2,1)}), bf16[32,224,128]{2,1,0:T(8,128)(2,1)}, u32[]{:S(2)}, u32[]{:S(2)}) async-start(bf16[32,224,128]{2,1,0:T(8,128)(2,1)} %broadcast_in_dim.2), calls=%async_computation.1 | async-start | bytes 3670016 | tf_op jit(solution)/shard_map/all_to_all | solution.py:838
  99.0 25.1 %copy-start.2 = (bf16[384,384]{1,0:T(8,128)(2,1)S(1)}, bf16[384,384]{1,0:T(8,128)(2,1)}, u32[]{:S(2)}) copy-start(bf16[384,384]{1,0:T(8,128)(2,1)} %refs_7_.1) | copy-start | bytes 884740
  99.0 25.1 %copy-start.3 = (bf16[256,384]{1,0:T(8,128)(2,1)S(1)}, bf16[256,384]{1,0:T(8,128)(2,1)}, u32[]{:S(2)}) copy-start(bf16[256,384]{1,0:T(8,128)(2,1)} %refs_6_.1) | copy-start | bytes 589828
  118.0 6.1 %collective-permute-start.8 = (bf16[6144,128]{1,0:T(8,128)(2,1)}, bf16[6144,128]{1,0:T(8,128)(2,1)S(1)}, u32[]{:S(2)}, u32[]{:S(2)}) collective-permute-start(bf16[6144,128]{1,0:T(8,128)(2,1)} %all-gather.2.cloned.1.call-done.rows_ref), channel_id=1, source_target_pairs={{0,2},{1,3},{2,0},{3,1},{4,6},{5,7},{6,4},{7,5},{8,10},{9,11},{10,... | collective-permute-start | bytes 4718600 | tf_op jit(solution)/shard_map/ppermute | solution.py:864
  131.6 5.9 %collective-permute-start.9 = (bf16[32,224,128]{2,1,0:T(8,128)(2,1)}, bf16[32,224,128]{2,1,0:T(8,128)(2,1)S(1)}, u32[]{:S(2)}, u32[]{:S(2)}) collective-permute-start(bf16[32,224,128]{2,1,0:T(8,128)(2,1)} %all-to-all-done.1.refs_1_), channel_id=1, source_target_pairs={{0,2},{1,3},{2,0},{3,1},{4,6},{5,7},{6,4},{7,5},{8,10},{9,11},{10,... | collective-permute-start | bytes 5505032 | tf_op jit(solution)/shard_map/ppermute | solution.py:864
  (6 other events, 17.6 us)
Sparse Core Ops, SparseCore 0:
  78.3 39.5 all-gather.1

commit v6 on v5

--- a/solution.py
+++ b/solution.py
@@ -87,8 +87,8 @@
     return np.stack(out)
 
 
-def pack_kernel(at_ref, lat_ref, dy_ref, row_ref, col_ref, lat_out, dy_out):
-    other = 2 - 2 * at_ref[0]
+def pack_kernel(lat_ref, dy_ref, row_ref, col_ref, lat_out, dy_out):
+    other = 2 - 2 * lax.axis_index("band")
     dy_out[...] = dy_ref[...]
     for i in range(2):
         lat_out[i, :128] = lat_ref[i]
@@ -397,22 +397,19 @@
     return pl.CostEstimate(flops=flops, bytes_accessed=nbytes, transcendentals=0)
 
 
-def pack_call(at, latents, out_grad, pos_row, pos_col):
-    theirs = pl.BlockSpec((2, 128, 384), lambda j, at: (1 - at[0], 0, 0))
+def pack_call(latents, out_grad, pos_row, pos_col):
+    theirs = pl.BlockSpec((2, 128, 384), lambda j: (1 - lax.axis_index("band"), 0, 0))
     shapes = [(2, 144, 384), (2, 128, 384)]
     return pl.pallas_call(
         pack_kernel,
-        grid_spec=pltpu.PrefetchScalarGridSpec(
-            num_scalar_prefetch=1,
-            grid=(1,),
-            in_specs=[theirs, theirs, whole_spec((4, 128)), whole_spec((4, 128))],
-            out_specs=[RESIDENT] * 2,
-        ),
+        grid=(1,),
+        in_specs=[theirs, theirs, whole_spec((4, 128)), whole_spec((4, 128))],
+        out_specs=[RESIDENT] * 2,
         out_shape=[shape_of(s, bf16) for s in shapes],
         compiler_params=params(56),
         cost_estimate=cost(200_000, 800_000),
         name="pack_swaps",
-    )(at, latents, out_grad, pos_row, pos_col)
+    )(latents, out_grad, pos_row, pos_col)
 
 
 def modulation_call(at, timesteps, labels, t_w1, t_w2, label_table, mod_w):
@@ -884,7 +881,7 @@
 ):
     band, img = lax.axis_index("band"), lax.axis_index("img")
     at = jnp.stack([band, img % 2, img // 4 % 2]).astype(jnp.int32)
-    send, dsend = pack_call(at, latents, out_grad, pos_row, pos_col)
+    send, dsend = pack_call(latents, out_grad, pos_row, pos_col)
     got, dgot = swap(send), swap(dsend)
     mod, extra = modulation_call(at, timesteps, labels, t_w1, t_w2, label_table, mod_w)
     mod = relay_call(mod)

time: 147 us -> 146 us (level)
  transfers between devices with their start and end apart: 12 -> 12, of which waited for: 8 -> 7; matrix products, arithmetic and copies ran while one was open for 1% -> 1% of each run, Pallas kernels for 20% -> 20%
where the time goes in v6:
time: 146 us
  Pallas kernels  41.9 us (29%)
  blocking collectives  31.7 us (22%)
  starting transfers between devices  29 us (20%)
  waiting for transfers between devices  24.3 us (17%)
  between operations  14.3 us (10%)
  local copies, waits for them, and re-layouts  3.7 us (3%)
    all_to_all x1, blocking collectives, exchange(): return lax.all_to_all(v, AXES, 0, 0, tiled=True, axis_index_groups=lists)  31.7 us
    all_gather x1, waiting for transfers between devices, body(): lax.all_gather(extra.reshape(768, 128), AXES, axis=0, tiled=True, axis_in...  17.6 us
    pallas_call x3, Pallas kernels, call(): pl.pallas_call(kernel, grid=(1,), in_specs=[SCALARS] + [spec(n in loose,...  16.6 us
    ppermute x4, starting transfers between devices, core_swap(): return lax.ppermute(v, AXES, CORE_SWAP)  8.67 us
    ppermute x2, starting transfers between devices, column_sum(): v = plus(v, lax.ppermute(v, AXES, moves(to)))  8.47 us
    pallas_call x1, Pallas kernels, condition_call(): pl.pallas_call(condition_kernel, grid=(1,), in_specs=[SCALARS] + [RESIDEN...  7.48 us
    pallas_call x2, Pallas kernels, unpack_call(): pl.pallas_call(lambda *refs: unpack_kernel(own, *refs), grid_spec=pltpu.P...  6.88 us
    all_to_all x1, starting transfers between devices, exchange(): return lax.all_to_all(v, AXES, 0, 0, tiled=True, axis_index_groups=lists)  5.34 us
  transfers between devices with their start and end apart: 12, of which 7 were waited for; matrix products, arithmetic and copies ran while one was open for 1% of the time, Pallas kernels for 20%

profile of v6, /device:TPU:1, one launch (start us, length us, event | category | flops | bytes accessed | tf_op | source)
XLA Modules:
  0.0 145.6 jit_solution(9343190108029933168)
XLA Ops:
  7.2 1.8 %pack_swaps.1 = (bf16[2,144,384]{2,1,0:T(8,128)(2,1)}, bf16[2,128,384]{2,1,0:T(8,128)(2,1)}) custom-call(bf16[4,128,384]{2,1,0:T(8,128)(2,1)} %kept_ref.5, bf16[4,128,384]{2,1,0:T(8,128)(2,1)} %dkept_ref.1, s32[4,128]{1,0:T(4,128)} %row_ref.5, s32[4,128]{1,0:T(4,128)} %col_ref.5), custom_call_target="tpu_custom_call" | custom-call | flops 200000 | bytes 800000 | tf_op jit(solution)/shard_map/pack_swaps/pallas_call | solution.py:403
  9.0 3.6 %collective-permute-start = (bf16[2,144,384]{2,1,0:T(8,128)(2,1)}, bf16[2,144,384]{2,1,0:T(8,128)(2,1)S(1)}, u32[]{:S(2)}, u32[]{:S(2)}) collective-permute-start(bf16[2,144,384]{2,1,0:T(8,128)(2,1)} %get-tuple-element.68), channel_id=1, source_target_pairs={{0,1},{1,0},{2,3},{3,2},{4,5},{5,4},{6,7},{7,6},{8,9},{9,8},{10,11... | collective-permute-start | bytes 663560 | tf_op jit(solution)/shard_map/ppermute | solution.py:857
  13.3 3.9 %modulation.1 = (f32[2,6,384]{2,1,0:T(8,128)}, f32[16,128]{1,0:T(8,128)}) custom-call(s32[3]{0:T(128)} %pad_add_fusion.at_ref.refs_0_, s32[4]{0:T(128)} %t_ref.1, s32[4]{0:T(128)} %l_ref.1, bf16[256,384]{1,0:T(8,128)(2,1)} %refs_6_.1, bf16[384,384]{1,0:T(8,128)(2,1)} %refs_7_.1, bf16[1001,384]{1,0:T(8,128)(2,1)} %row1_ref.1, bf16[1001,384]{1,0:T(8,128)(2,1)} %row1_ref.1, ...), custom_call_target="tpu_custom_call" | custom-call | flops 1000000000 | bytes 3000000 | tf_op jit(solution)/shard_map/modulation/pallas_call | solution.py:420
  18.1 3.2 %attention_forward.1 = (bf16[2,256,384]{2,1,0:T(8,128)(2,1)S(1)}, bf16[2,256,384]{2,1,0:T(8,128)(2,1)S(1)}, bf16[2,256,384]{2,1,0:T(8,128)(2,1)S(1)}, bf16[512,384]{1,0:T(8,128)(2,1)S(1)}) custom-call(s32[3]{0:T(128)S(1)} %copy-done.6, bf16[4,128,384]{2,1,0:T(8,128)(2,1)S(1)} %copy-done.5, bf16[2,144,384]{2,1,0:T(8,128)(2,1)S(1)} %collective-permute-done.got_ref, ...), custom_call_target="tpu_custom_call" | custom-call | flops 3000000000 | bytes 4000000 | tf_op jit(solution)/shard_map/attention_forward/pallas_call | solution.py:446
  21.4 6.1 %mlp_both_ways.1 = (bf16[4608,128]{1,0:T(8,128)(2,1)S(1)}, bf16[4608,128]{1,0:T(8,128)(2,1)S(1)}, bf16[4,128,384]{2,1,0:T(8,128)(2,1)}, bf16[2,128,384]{2,1,0:T(...) custom-call(s32[3]{0:T(128)S(1)} %copy-done.6, bf16[4,128,384]{2,1,0:T(8,128)(2,1)S(1)} %copy-done.5, ...), custom_call_target="tpu_custom_call" | custom-call | flops 6000000000 | bytes 8000000 | tf_op jit(solution)/shard_map/mlp_both_ways/pallas_call | solution.py:446
  27.4 4.2 %collective-permute-start.2 = (bf16[4608,128]{1,0:T(8,128)(2,1)S(1)}, bf16[4608,128]{1,0:T(8,128)(2,1)S(1)}, u32[]{:S(2)}, u32[]{:S(2)}) collective-permute-start(bf16[4608,128]{1,0:T(8,128)(2,1)S(1)} %get-tuple-element.73), channel_id=1, source_target_pairs={{0,2},{1,3},{2,0},{3,1},{4,6},{5,7},{6,4},{7,5},{8,10},{9,11},{10,... | collective-permute-start | bytes 3538952 | tf_op jit(solution)/shard_map/ppermute | solution.py:861
  31.6 7.3 %attention_backward.1 = (bf16[2304,128]{1,0:T(8,128)(2,1)S(1)}, bf16[2304,128]{1,0:T(8,128)(2,1)S(1)}, f32[4,128,384]{2,1,0:T(8,128)}, bf16[2,2,128,384]{3,2,1,0:T(8,128)(2,1)S(1)}, f32[16,128]{1,0:T(8,128)S(1)}) custom-call(s32[3]{0:T(128)S(1)} %copy-done.6, bf16[4,128,384]{2,1,0:T(8,128)(2,1)S(1)} %copy-done.5, ...), custom_call_target="tpu_custom_call" | custom-call | flops 5000000000 | bytes 6000000 | tf_op jit(solution)/shard_map/attention_backward/pallas_call | solution.py:446
  38.9 2.0 %collective-permute-done.3 = bf16[2304,128]{1,0:T(8,128)(2,1)S(1)} collective-permute-done((bf16[2304,128]{1,0:T(8,128)(2,1)S(1)}, bf16[2304,128]{1,0:T(8,128)(2,1)S(1)}, u32[]{:S(2)}, u32[]{:S(2)}) %collective-permute-start.3) | collective-permute-done | bytes 589856 | tf_op jit(solution)/shard_map/ppermute | solution.py:861
  41.8 31.7 %all_to_all.10.a_ref = bf16[16,480,128]{2,1,0:T(8,128)(2,1)S(1)} all-to-all(bf16[16,480,128]{2,1,0:T(8,128)(2,1)S(1)} %join_messages.1), channel_id=1, replica_groups={{0,4,1,5,64,68,65,69,128,132,129,133,192,196,193,197},{2,6,3,7,66,70,67..., dimensions={0} | all-to-all | bytes 3932160 | tf_op jit(solution)/shard_map/all_to_all | solution.py:835
  75.1 1.7 %collective-permute-start.4 = (bf16[224,128]{1,0:T(8,128)(2,1)S(1)}, bf16[224,128]{1,0:T(8,128)(2,1)S(1)}, u32[]{:S(2)}, u32[]{:S(2)}) collective-permute-start(bf16[224,128]{1,0:T(8,128)(2,1)S(1)} %get-tuple-element.87), channel_id=1, source_target_pairs={{0,8},{2,10},{4,12},{6,14},{1,9},{3,11},{5,13},{7,15},{64,72},{66,... | collective-permute-start | bytes 172040 | tf_op jit(solution)/shard_map/ppermute | solution.py:843
  76.8 1.5 %collective-permute-done.4 = bf16[224,128]{1,0:T(8,128)(2,1)S(1)} collective-permute-done((bf16[224,128]{1,0:T(8,128)(2,1)S(1)}, bf16[224,128]{1,0:T(8,128)(2,1)S(1)}, u32[]{:S(2)}, u32[]{:S(2)}) %collective-permute-start.4) | collective-permute-done | bytes 57376 | tf_op jit(solution)/shard_map/ppermute | solution.py:843
  78.4 3.1 %collective-permute-start.5 = (bf16[224,128]{1,0:T(8,128)(2,1)S(1)}, bf16[224,128]{1,0:T(8,128)(2,1)S(1)}, u32[]{:S(2)}, u32[]{:S(2)}) collective-permute-start(bf16[224,128]{1,0:T(8,128)(2,1)S(1)} %add_convert_fusion.2), channel_id=1, source_target_pairs={{0,16},{2,18},{4,20},{6,22},{1,17},{3,19},{5,21},{7,23},{64,80},{6... | collective-permute-start | bytes 172040 | tf_op jit(solution)/shard_map/ppermute | solution.py:848
  83.1 5.4 %collective-permute-start.6 = (bf16[224,128]{1,0:T(8,128)(2,1)S(1)}, bf16[224,128]{1,0:T(8,128)(2,1)S(1)}, u32[]{:S(2)}, u32[]{:S(2)}) collective-permute-start(bf16[224,128]{1,0:T(8,128)(2,1)S(1)} %add_convert_fusion.1), channel_id=1, source_target_pairs={{0,48},{2,50},{4,52},{6,54},{1,49},{3,51},{5,53},{7,55},{64,112},{... | collective-permute-start | bytes 172040 | tf_op jit(solution)/shard_map/ppermute | solution.py:848
  88.5 1.9 %collective-permute-done.6 = bf16[224,128]{1,0:T(8,128)(2,1)S(1)} collective-permute-done((bf16[224,128]{1,0:T(8,128)(2,1)S(1)}, bf16[224,128]{1,0:T(8,128)(2,1)S(1)}, u32[]{:S(2)}, u32[]{:S(2)}) %collective-permute-start.6) | collective-permute-done | bytes 57376 | tf_op jit(solution)/shard_map/ppermute | solution.py:848
  90.8 1.5 %broadcast_in_dim.2 = bf16[32,224,128]{2,1,0:T(8,128)(2,1)} broadcast(bf16[224,128]{1,0:T(8,128)(2,1)S(1)} %add_convert_fusion), dimensions={1,2} | broadcast | bytes 1892352 | tf_op jit(solution)/shard_map/broadcast_in_dim | solution.py:906
  92.2 5.3 %all-to-all-start.1 = ((bf16[32,224,128]{2,1,0:T(8,128)(2,1)}), bf16[32,224,128]{2,1,0:T(8,128)(2,1)}, u32[]{:S(2)}, u32[]{:S(2)}) async-start(bf16[32,224,128]{2,1,0:T(8,128)(2,1)} %broadcast_in_dim.2), calls=%async_computation.1 | async-start | bytes 3670016 | tf_op jit(solution)/shard_map/all_to_all | solution.py:835
  97.6 1.4 place_swaps.1
  99.0 17.6 %all-gather.2.cloned.1.call-done.rows_ref = bf16[6144,128]{1,0:T(8,128)(2,1)} async-done(((bf16[768,128]{1,0:T(8,128)(2,1)}), bf16[6144,128]{1,0:T(8,128)(2,1)}) %all-gather.2.cloned.1.call-update) | async-done | bytes 1572880 | tf_op jit(solution)/shard_map/all_gather | solution.py:901
  116.6 2.9 %collective-permute-start.8 = (bf16[6144,128]{1,0:T(8,128)(2,1)}, bf16[6144,128]{1,0:T(8,128)(2,1)S(1)}, u32[]{:S(2)}, u32[]{:S(2)}) collective-permute-start(bf16[6144,128]{1,0:T(8,128)(2,1)} %all-gather.2.cloned.1.call-done.rows_ref), channel_id=1, source_target_pairs={{0,2},{1,3},{2,0},{3,1},{4,6},{5,7},{6,4},{7,5},{8,10},{9,11},{10,... | collective-permute-start | bytes 4718600 | tf_op jit(solution)/shard_map/ppermute | solution.py:861
  119.5 1.4 copy-done.1
  122.7 7.5 %condition_gradients.1 = (f32[256,384]{1,0:T(8,128)}, f32[384,384]{1,0:T(8,128)}, f32[1001,384]{1,0:T(8,128)}, f32[384,2304]{1,0:T(8,128)}, f32[1,64]{1,0:T(1,128)}, /*index=5*/f32[1,64]{1,0:T(1,128)}) custom-call(s32[3]{0:T(128)S(1)} %copy-done.6, bf16[256,2304]{1,0:T(8,128)(2,1)S(1)} %get-tuple-element.98.refs_0_, ...), custom_call_target="tpu_custom_call" | custom-call | flops 100000000 | bytes 100000 | tf_op jit(solution)/shard_map/condition_gradients/pallas_call | solution.py:685
  130.2 1.6 %collective-permute-start.9 = (bf16[32,224,128]{2,1,0:T(8,128)(2,1)}, bf16[32,224,128]{2,1,0:T(8,128)(2,1)S(1)}, u32[]{:S(2)}, u32[]{:S(2)}) collective-permute-start(bf16[32,224,128]{2,1,0:T(8,128)(2,1)} %all-to-all-done.1.refs_1_), channel_id=1, source_target_pairs={{0,2},{1,3},{2,0},{3,1},{4,6},{5,7},{6,4},{7,5},{8,10},{9,11},{10,... | collective-permute-start | bytes 5505032 | tf_op jit(solution)/shard_map/ppermute | solution.py:861
  131.8 4.3 %unpack_own.1 = (f32[384,1152]{1,0:T(8,128)}, f32[384,384]{1,0:T(8,128)}, f32[384,2048]{1,0:T(8,128)}, f32[1024,384]{1,0:T(8,128)}) custom-call(s32[3]{0:T(128)S(1)} %copy-done.6, bf16[32,224,128]{2,1,0:T(8,128)(2,1)} %all-to-all-done.1.refs_1_), custom_call_target="tpu_custom_call" | custom-call | flops 2000000 | bytes 6000000 | tf_op jit(solution)/shard_map/unpack_own/pallas_call | solution.py:787
  136.1 2.6 %unpack_other.1 = (f32[384,1152]{1,0:T(8,128)}, f32[384,384]{1,0:T(8,128)}, f32[384,2048]{1,0:T(8,128)}, f32[1024,384]{1,0:T(8,128)}) custom-call(s32[3]{0:T(128)S(1)} %copy-done.6, bf16[32,224,128]{2,1,0:T(8,128)(2,1)S(1)} %collective-permute-done.9.refs_1_, ...), custom_call_target="tpu_custom_call", output_to_operand_aliasing={{0}: (2, {}), {1}: (3, {}), {2}: (4, {}), {3}: (5, {})} | custom-call | flops 2000000 | bytes 6000000 | tf_op jit(solution)/shard_map/unpack_other/pallas_call | solution.py:787
  (57 shorter events, 7.9 us)
Async XLA Ops:
  7.2 109.4 %all-gather.2.cloned.1.call-start = ((), (), s32[]{:S(2)}) async-start(), calls=%async_computation.2 | async-start | bytes 1769472 | tf_op jit(solution)/shard_map/all_gather | solution.py:901
  9.0 8.9 %collective-permute-start = (bf16[2,144,384]{2,1,0:T(8,128)(2,1)}, bf16[2,144,384]{2,1,0:T(8,128)(2,1)S(1)}, u32[]{:S(2)}, u32[]{:S(2)}) collective-permute-start(bf16[2,144,384]{2,1,0:T(8,128)(2,1)} %get-tuple-element.68), channel_id=1, source_target_pairs={{0,1},{1,0},{2,3},{3,2},{4,5},{5,4},{6,7},{7,6},{8,9},{9,8},{10,11... | collective-permute-start | bytes 663560 | tf_op jit(solution)/shard_map/ppermute | solution.py:857
  12.6 8.7 %collective-permute-start.1 = (bf16[2,128,384]{2,1,0:T(8,128)(2,1)}, bf16[2,128,384]{2,1,0:T(8,128)(2,1)S(1)}, u32[]{:S(2)}, u32[]{:S(2)}) collective-permute-start(bf16[2,128,384]{2,1,0:T(8,128)(2,1)} %get-tuple-element.69), channel_id=1, source_target_pairs={{0,1},{1,0},{2,3},{3,2},{4,5},{5,4},{6,7},{7,6},{8,9},{9,8},{10,11... | collective-permute-start | bytes 589832 | tf_op jit(solution)/shard_map/ppermute | solution.py:857
  13.2 4.7 %copy-start.5 = (bf16[4,128,384]{2,1,0:T(8,128)(2,1)S(1)}, bf16[4,128,384]{2,1,0:T(8,128)(2,1)}, u32[]{:S(2)}) copy-start(bf16[4,128,384]{2,1,0:T(8,128)(2,1)} %kept_ref.5) | copy-start | bytes 1179652
  13.2 4.7 %copy-start.6 = (s32[3]{0:T(128)S(1)}, s32[3]{0:T(128)}, u32[]{:S(2)}) copy-start(s32[3]{0:T(128)} %pad_add_fusion.at_ref.refs_0_) | copy-start | bytes 40
  13.2 4.7 %copy-start.9 = (s32[4,128]{1,0:T(4,128)S(1)}, s32[4,128]{1,0:T(4,128)}, u32[]{:S(2)}) copy-start(s32[4,128]{1,0:T(4,128)} %row_ref.5) | copy-start | bytes 6148
  13.2 4.7 %copy-start.10 = (s32[4,128]{1,0:T(4,128)S(1)}, s32[4,128]{1,0:T(4,128)}, u32[]{:S(2)}) copy-start(s32[4,128]{1,0:T(4,128)} %col_ref.5) | copy-start | bytes 6148
  13.2 4.7 %copy-start.12 = (bf16[384,1152]{1,0:T(8,128)(2,1)S(1)}, bf16[384,1152]{1,0:T(8,128)(2,1)}, u32[]{:S(2)}) copy-start(bf16[384,1152]{1,0:T(8,128)(2,1)} %w_ref.3) | copy-start | bytes 2654212
  13.3 4.7 %copy-start.15 = (f32[64]{0:T(128)S(1)}, f32[64]{0:T(128)}, u32[]{:S(2)}) copy-start(f32[64]{0:T(128)} %param.27) | copy-start | bytes 772
  13.3 4.7 %copy-start.16 = (f32[64]{0:T(128)S(1)}, f32[64]{0:T(128)}, u32[]{:S(2)}) copy-start(f32[64]{0:T(128)} %param.28) | copy-start | bytes 772
  13.3 4.7 %copy-start.17 = (bf16[4,32,128]{2,1,0:T(8,128)(2,1)S(1)}, bf16[4,32,128]{2,1,0:T(8,128)(2,1)}, u32[]{:S(2)}) copy-start(bf16[4,32,128]{2,1,0:T(8,128)(2,1)} %constant.40.clone.table_ref) | copy-start | bytes 98308
  27.4 13.5 %collective-permute-start.2 = (bf16[4608,128]{1,0:T(8,128)(2,1)S(1)}, bf16[4608,128]{1,0:T(8,128)(2,1)S(1)}, u32[]{:S(2)}, u32[]{:S(2)}) collective-permute-start(bf16[4608,128]{1,0:T(8,128)(2,1)S(1)} %get-tuple-element.73), channel_id=1, source_target_pairs={{0,2},{1,3},{2,0},{3,1},{4,6},{5,7},{6,4},{7,5},{8,10},{9,11},{10,... | collective-permute-start | bytes 3538952 | tf_op jit(solution)/shard_map/ppermute | solution.py:861
  31.6 9.3 %copy-start.8 = (f32[16,128]{1,0:T(8,128)S(1)}, f32[16,128]{1,0:T(8,128)}, u32[]{:S(2)}) copy-start(f32[16,128]{1,0:T(8,128)} %get-tuple-element.83.extra_ref) | copy-start | bytes 24580
  38.9 2.0 %collective-permute-start.3 = (bf16[2304,128]{1,0:T(8,128)(2,1)S(1)}, bf16[2304,128]{1,0:T(8,128)(2,1)S(1)}, u32[]{:S(2)}, u32[]{:S(2)}) collective-permute-start(bf16[2304,128]{1,0:T(8,128)(2,1)S(1)} %get-tuple-element.80), channel_id=1, source_target_pairs={{0,2},{1,3},{2,0},{3,1},{4,6},{5,7},{6,4},{7,5},{8,10},{9,11},{10,... | collective-permute-start | bytes 1769480 | tf_op jit(solution)/shard_map/ppermute | solution.py:861
  75.1 3.3 %collective-permute-start.4 = (bf16[224,128]{1,0:T(8,128)(2,1)S(1)}, bf16[224,128]{1,0:T(8,128)(2,1)S(1)}, u32[]{:S(2)}, u32[]{:S(2)}) collective-permute-start(bf16[224,128]{1,0:T(8,128)(2,1)S(1)} %get-tuple-element.87), channel_id=1, source_target_pairs={{0,8},{2,10},{4,12},{6,14},{1,9},{3,11},{5,13},{7,15},{64,72},{66,... | collective-permute-start | bytes 172040 | tf_op jit(solution)/shard_map/ppermute | solution.py:843
  78.4 4.6 %collective-permute-start.5 = (bf16[224,128]{1,0:T(8,128)(2,1)S(1)}, bf16[224,128]{1,0:T(8,128)(2,1)S(1)}, u32[]{:S(2)}, u32[]{:S(2)}) collective-permute-start(bf16[224,128]{1,0:T(8,128)(2,1)S(1)} %add_convert_fusion.2), channel_id=1, source_target_pairs={{0,16},{2,18},{4,20},{6,22},{1,17},{3,19},{5,21},{7,23},{64,80},{6... | collective-permute-start | bytes 172040 | tf_op jit(solution)/shard_map/ppermute | solution.py:848
  81.5 9.3 %collective-permute-start.7 = (bf16[2,2,128,384]{3,2,1,0:T(8,128)(2,1)S(1)}, bf16[2,2,128,384]{3,2,1,0:T(8,128)(2,1)S(1)}, u32[]{:S(2)}, u32[]{:S(2)}) collective-permute-start(bf16[2,2,128,384]{3,2,1,0:T(8,128)(2,1)S(1)} %get-tuple-element.88), channel_id=1, source_target_pairs={{0,1},{1,0},{2,3},{3,2},{4,5},{5,4},{6,7},{7,6},{8,9},{9,8},{10,11... | collective-permute-start | bytes 1179656 | tf_op jit(solution)/shard_map/ppermute | solution.py:857
  83.1 7.3 %collective-permute-start.6 = (bf16[224,128]{1,0:T(8,128)(2,1)S(1)}, bf16[224,128]{1,0:T(8,128)(2,1)S(1)}, u32[]{:S(2)}, u32[]{:S(2)}) collective-permute-start(bf16[224,128]{1,0:T(8,128)(2,1)S(1)} %add_convert_fusion.1), channel_id=1, source_target_pairs={{0,48},{2,50},{4,52},{6,54},{1,49},{3,51},{5,53},{7,55},{64,112},{... | collective-permute-start | bytes 172040 | tf_op jit(solution)/shard_map/ppermute | solution.py:848
  92.2 27.3 %copy-start = (bf16[384,2304]{1,0:T(8,128)(2,1)S(1)}, bf16[384,2304]{1,0:T(8,128)(2,1)}, u32[]{:S(2)}) copy-start(bf16[384,2304]{1,0:T(8,128)(2,1)} %refs_8_.1) | copy-start | bytes 5308420
  92.2 38.0 %all-to-all-start.1 = ((bf16[32,224,128]{2,1,0:T(8,128)(2,1)}), bf16[32,224,128]{2,1,0:T(8,128)(2,1)}, u32[]{:S(2)}, u32[]{:S(2)}) async-start(bf16[32,224,128]{2,1,0:T(8,128)(2,1)} %broadcast_in_dim.2), calls=%async_computation.1 | async-start | bytes 3670016 | tf_op jit(solution)/shard_map/all_to_all | solution.py:835
  97.6 25.2 %copy-start.2 = (bf16[384,384]{1,0:T(8,128)(2,1)S(1)}, bf16[384,384]{1,0:T(8,128)(2,1)}, u32[]{:S(2)}) copy-start(bf16[384,384]{1,0:T(8,128)(2,1)} %refs_7_.1) | copy-start | bytes 884740
  97.6 25.1 %copy-start.3 = (bf16[256,384]{1,0:T(8,128)(2,1)S(1)}, bf16[256,384]{1,0:T(8,128)(2,1)}, u32[]{:S(2)}) copy-start(bf16[256,384]{1,0:T(8,128)(2,1)} %refs_6_.1) | copy-start | bytes 589828
  116.6 6.1 %collective-permute-start.8 = (bf16[6144,128]{1,0:T(8,128)(2,1)}, bf16[6144,128]{1,0:T(8,128)(2,1)S(1)}, u32[]{:S(2)}, u32[]{:S(2)}) collective-permute-start(bf16[6144,128]{1,0:T(8,128)(2,1)} %all-gather.2.cloned.1.call-done.rows_ref), channel_id=1, source_target_pairs={{0,2},{1,3},{2,0},{3,1},{4,6},{5,7},{6,4},{7,5},{8,10},{9,11},{10,... | collective-permute-start | bytes 4718600 | tf_op jit(solution)/shard_map/ppermute | solution.py:861
  130.2 5.9 %collective-permute-start.9 = (bf16[32,224,128]{2,1,0:T(8,128)(2,1)}, bf16[32,224,128]{2,1,0:T(8,128)(2,1)S(1)}, u32[]{:S(2)}, u32[]{:S(2)}) collective-permute-start(bf16[32,224,128]{2,1,0:T(8,128)(2,1)} %all-to-all-done.1.refs_1_), channel_id=1, source_target_pairs={{0,2},{1,3},{2,0},{3,1},{4,6},{5,7},{6,4},{7,5},{8,10},{9,11},{10,... | collective-permute-start | bytes 5505032 | tf_op jit(solution)/shard_map/ppermute | solution.py:861
  (6 other events, 15.3 us)
Sparse Core Ops, SparseCore 0:
  77.0 39.6 all-gather.1
